TPU v7x, 32 devices: a whole 2x2x4 slice. The times are simulated.
32 devices in a mesh: replica: 2 (over y), gx: 8 (over z, x), gy: 2 (over core).
Axes of the slice: x: 2, y: 2, z: 4, core: 2. Of those that a mesh axis runs over, the one named last changes fastest.
Arguments:
- tokens: bfloat16 [2, 128, 8192], P(None, ('replica', 'gy'), 'gx'), parts along dimension 1, may hold values from -6 to 6
- gate_weight: bfloat16 [8192, 26624], P('gx', 'gy'), may hold values from -0.09375 to 0.09375
- up_weight: bfloat16 [8192, 26624], P('gx', 'gy'), may hold values from -0.09375 to 0.09375
- down_weight: bfloat16 [26624, 8192], P('gy', 'gx'), may hold values from -0.0390625 to 0.0390625
Outputs:
- mixed: bfloat16 [2, 128, 8192], P(None, ('replica', 'gy'), 'gx'), parts along dimension 1
There are 2 independent parts, one for each index of `replica`. A program takes and returns all parts, laid end to end along the dimension named above; an argument that names none is the same for every part. Nothing has to cross between parts.
All inputs are finite; a program needn't handle non-finite values.
Results may differ from a plain program's by a relative error of at most 0.015.
Values may be sent and summed in bfloat16 or wider, within the bound.
No kernel may reach another device: no remote copies, remote signals or barrier semaphores. Data moves between devices by JAX's collectives and lax.ppermute only.
A program may use at most 384 MiB of HBM per device.

v0:
```python
import jax
import jax.numpy as jnp
from jax import lax
from jax.sharding import PartitionSpec as P


def body(tokens, gate_weight, up_weight, down_weight):

    def layer_apply(local_input):
        row_block = lax.all_gather(local_input, "gy", axis=0, tiled=True)
        batch_rows = row_block.shape[0]
        gate_term = jnp.dot(row_block, gate_weight, preferred_element_type=jnp.float32)
        up_term = jnp.dot(row_block, up_weight, preferred_element_type=jnp.float32)
        stacked = jnp.concatenate([gate_term, up_term], axis=0)
        summed = lax.psum_scatter(stacked, "gx", scatter_dimension=1, tiled=True)
        gate_part = summed[:batch_rows]
        up_part = summed[batch_rows:]
        hidden_part = (jax.nn.silu(gate_part) * up_part).astype(jnp.bfloat16)
        partial_out = jnp.dot(
            lax.all_gather(hidden_part, "gx", axis=1, tiled=True),
            down_weight,
            preferred_element_type=jnp.float32,
        )
        return lax.psum_scatter(partial_out, "gy", scatter_dimension=0, tiled=True).astype(
            jnp.bfloat16
        )

    first_out = layer_apply(tokens[0])
    second_input = (tokens[1].astype(jnp.float32) + first_out.astype(jnp.float32)).astype(
        jnp.bfloat16
    )
    second_out = layer_apply(second_input)
    return jnp.stack([first_out, second_out])


def solution(mesh):
    return jax.shard_map(
        body,
        mesh=mesh,
        in_specs=(P(None, ("replica", "gy"), "gx"), P("gx", "gy"), P("gx", "gy"), P("gy", "gx")),
        out_specs=P(None, ("replica", "gy"), "gx"),
        check_vma=False,
    )
```

profile of v0, /device:TPU:0, one launch (start us, length us, event | category | flops | bytes accessed | tf_op | source)
XLA Modules:
  0.0 464.4 jit_solution(1341621453483729544)
XLA Ops:
  6.5 0.0 reduce-scatter.5.cloned.1.call-start
  6.5 0.8 slice.18
  7.4 2.0 all-gather
  9.4 11.2 %fusion.3 = f32[64,13312]{1,0:T(8,128)S(1)} fusion(bf16[1024,13312]{1,0:T(8,128)(2,1)} %param.6, bf16[1,64,1024]{2,1,0:T(8,128)(2,1)S(1)} %all-gather), kind=kOutput, calls=%fused_computation.9 | convolution fusion | flops 1744830464 | bytes 30801920 | tf_op jit(solution)/shard_map/dot_general | solution.py:13
  20.6 11.2 %fusion.5 = f32[64,13312]{1,0:T(8,128)S(1)} fusion(bf16[1024,13312]{1,0:T(8,128)(2,1)} %param.5, bf16[1,64,1024]{2,1,0:T(8,128)(2,1)S(1)} %all-gather), kind=kOutput, calls=%fused_computation.11 | convolution fusion | flops 1744830464 | bytes 30801920 | tf_op jit(solution)/shard_map/dot_general | solution.py:12
  31.9 3.3 pad_maximum_fusion
  35.1 0.0 reduce-scatter.5.cloned.1.call-update
  35.2 0.0 all-gather.4.cloned.1.call-start
  35.2 128.5 %reduce-scatter.5.cloned.1.call-done = f32[128,1664]{1,0:T(8,128)} async-done(((f32[128,13312]{1,0:T(8,128)}), f32[128,1664]{1,0:T(8,128)}) %reduce-scatter.5.cloned.1.call-update) | async-done | bytes 851984 | tf_op jit(solution)/shard_map/reduce_scatter | solution.py:15
  163.7 1.9 fusion.1
  165.6 0.0 all-gather.4.cloned.1.call-update
  165.6 0.0 copy-start
  165.6 0.0 reduce-scatter.7.cloned.1.call-start
  165.7 44.8 %all-gather.4.cloned.1.call-done = bf16[64,13312]{1,0:T(8,128)(2,1)} async-done(((bf16[64,1664]{1,0:T(8,128)(2,1)}), bf16[64,13312]{1,0:T(8,128)(2,1)}) %all-gather.4.cloned.1.call-update) | async-done | bytes 1703952 | tf_op jit(solution)/shard_map/all_gather | solution.py:20
  210.4 14.8 %fusion.7 = f32[64,1024]{1,0:T(8,128)} fusion(bf16[64,13312]{1,0:T(8,128)(2,1)} %all-gather.4.cloned.1.call-done, bf16[13312,1024]{1,0:T(8,128)(2,1)} %param.7), kind=kOutput, calls=%fused_computation.15 | convolution fusion | flops 1744830464 | bytes 29229056 | tf_op jit(solution)/shard_map/dot_general | solution.py:19
  225.3 0.0 reduce-scatter.7.cloned.1.call-update
  225.3 0.0 reduce-scatter.9.cloned.1.call-start
  225.3 6.6 %reduce-scatter.7.cloned.1.call-done = f32[32,1024]{1,0:T(8,128)} async-done(((f32[64,1024]{1,0:T(8,128)}), f32[32,1024]{1,0:T(8,128)}) %reduce-scatter.7.cloned.1.call-update) | async-done | bytes 131088 | tf_op jit(solution)/shard_map/reduce_scatter | solution.py:24
  231.9 0.0 copy-done
  231.9 0.9 convert_bitcast_fusion.1
  232.9 1.9 all_gather.14
  234.8 11.2 %fusion.9 = f32[64,13312]{1,0:T(8,128)S(1)} fusion(bf16[64,1024]{1,0:T(8,128)(2,1)S(1)} %all_gather.14, bf16[1024,13312]{1,0:T(8,128)(2,1)} %param.6), kind=kOutput, calls=%fused_computation.17 | convolution fusion | flops 1744830464 | bytes 30801920 | tf_op jit(solution)/shard_map/dot_general | solution.py:13
  246.0 11.2 %fusion.8 = f32[64,13312]{1,0:T(8,128)S(1)} fusion(bf16[64,1024]{1,0:T(8,128)(2,1)S(1)} %all_gather.14, bf16[1024,13312]{1,0:T(8,128)(2,1)} %param.5), kind=kOutput, calls=%fused_computation.16 | convolution fusion | flops 1744830464 | bytes 30801920 | tf_op jit(solution)/shard_map/dot_general | solution.py:12
  257.2 3.3 pad_maximum_fusion.1
  260.5 0.0 reduce-scatter.9.cloned.1.call-update
  260.5 0.2 all-gather.6.cloned.1.call-start
  260.8 126.8 %reduce-scatter.9.cloned.1.call-done = f32[128,1664]{1,0:T(8,128)} async-done(((f32[128,13312]{1,0:T(8,128)}), f32[128,1664]{1,0:T(8,128)}) %reduce-scatter.9.cloned.1.call-update) | async-done | bytes 851984 | tf_op jit(solution)/shard_map/reduce_scatter | solution.py:15
  387.6 1.9 fusion
  389.5 0.0 all-gather.6.cloned.1.call-update
  389.6 0.0 reduce-scatter.11.cloned.1.call-start
  389.6 44.9 %all-gather.6.cloned.1.call-done = bf16[64,13312]{1,0:T(8,128)(2,1)} async-done(((bf16[64,1664]{1,0:T(8,128)(2,1)}), bf16[64,13312]{1,0:T(8,128)(2,1)}) %all-gather.6.cloned.1.call-update) | async-done | bytes 1703952 | tf_op jit(solution)/shard_map/all_gather | solution.py:20
  434.5 14.8 %fusion.10 = f32[64,1024]{1,0:T(8,128)} fusion(bf16[64,13312]{1,0:T(8,128)(2,1)} %all-gather.6.cloned.1.call-done, bf16[13312,1024]{1,0:T(8,128)(2,1)} %param.7), kind=kOutput, calls=%fused_computation.18 | convolution fusion | flops 1744830464 | bytes 29229056 | tf_op jit(solution)/shard_map/dot_general | solution.py:19
  449.3 0.0 reduce-scatter.11.cloned.1.call-update
  449.3 6.6 %reduce-scatter.11.cloned.1.call-done = f32[32,1024]{1,0:T(8,128)} async-done(((f32[64,1024]{1,0:T(8,128)}), f32[32,1024]{1,0:T(8,128)}) %reduce-scatter.11.cloned.1.call-update) | async-done | bytes 131088 | tf_op jit(solution)/shard_map/reduce_scatter | solution.py:24
  455.9 0.9 convert_bitcast_fusion
  456.9 0.7 pad_maximum_fusion.2
Async XLA Ops:
  6.5 157.1 %reduce-scatter.5.cloned.1.call-start = ((), (), s32[]{:S(2)}) async-start(), calls=%async_computation.4 | async-start | bytes 7667712 | tf_op jit(solution)/shard_map/reduce_scatter | solution.py:15
  35.2 175.3 %all-gather.4.cloned.1.call-start = ((), (), s32[]{:S(2)}) async-start(), calls=%async_computation.5 | async-start | bytes 1916928 | tf_op jit(solution)/shard_map/all_gather | solution.py:20
  165.6 66.3 %copy-start = (bf16[2,32,1024]{2,1,0:T(8,128)(2,1)S(1)}, bf16[2,32,1024]{2,1,0:T(8,128)(2,1)}, u32[]{:S(2)}) copy-start(bf16[2,32,1024]{2,1,0:T(8,128)(2,1)} %param.4) | copy-start | bytes 393220
  165.6 66.3 %reduce-scatter.7.cloned.1.call-start = ((), (), s32[]{:S(2)}) async-start(), calls=%async_computation.6 | async-start | bytes 393216 | tf_op jit(solution)/shard_map/reduce_scatter | solution.py:24
  225.3 162.3 %reduce-scatter.9.cloned.1.call-start = ((), (), s32[]{:S(2)}) async-start(), calls=%async_computation.7 | async-start | bytes 7667712 | tf_op jit(solution)/shard_map/reduce_scatter | solution.py:15
  260.5 173.9 %all-gather.6.cloned.1.call-start = ((), (), s32[]{:S(2)}) async-start(), calls=%async_computation.8 | async-start | bytes 1916928 | tf_op jit(solution)/shard_map/all_gather | solution.py:20
  389.6 66.4 %reduce-scatter.11.cloned.1.call-start = ((), (), s32[]{:S(2)}) async-start(), calls=%async_computation.9 | async-start | bytes 393216 | tf_op jit(solution)/shard_map/reduce_scatter | solution.py:24
Sparse Core Ops, SparseCore 0:
  35.3 128.3 reduce-scatter.4
  165.9 44.5 all-gather.3
  225.4 6.4 reduce-scatter.6
  260.7 126.8 reduce-scatter.8
  389.9 44.5 all-gather.5
  449.4 6.4 reduce-scatter.10
where the time goes:
time: 465 us; the launch traced here: 464 us
  waiting for transfers between devices  358 us (77%)
  matrix products  74.6 us (16%)
  between operations  13.5 us (3%)
  other arithmetic  12.9 us (3%)
    reduce_scatter x2, waiting for transfers between devices, layer_apply(): summed = lax.psum_scatter(stacked, 'gx', scatter_dimension=1, tiled=True)  255 us
    all_gather x2, waiting for transfers between devices, layer_apply(): lax.all_gather(hidden_part, 'gx', axis=1, tiled=True)  89.6 us
    dot_general x2, matrix products, layer_apply(): jnp.dot(lax.all_gather(hidden_part, 'gx', axis=1, tiled=True), down_weigh...  29.6 us
    dot_general x2, matrix products, layer_apply(): jnp.dot(row_block, gate_weight, preferred_element_type=jnp.float32)  22.5 us
    dot_general x2, matrix products, layer_apply(): up_term = jnp.dot(row_block, up_weight, preferred_element_type=jnp.float32)  22.5 us
    reduce_scatter x2, waiting for transfers between devices, layer_apply(): lax.psum_scatter(partial_out, 'gy', scatter_dimension=0, tiled=True)  13.2 us
  transfers between devices with their start and end apart: 6, of which 6 were waited for; matrix products, arithmetic and copies ran while one was open for 0% of the time, Pallas kernels for 0%

commit v1 on v0

v1 whole, which is shorter than its diff:
```python
import jax
import jax.numpy as jnp
from jax import lax
from jax.experimental import pallas as pl
from jax.experimental.pallas import tpu as pltpu
from jax.sharding import PartitionSpec as P

BF16 = jnp.bfloat16
F32 = jnp.float32
BLOCK = 512
CHUNKS = ((4, 3), (3, 3))
STREAM_BITS = ((0, 1), (1, 0))
FAR = 2
VMEM = pl.BlockSpec(memory_space=pltpu.VMEM)
SMEM = pl.BlockSpec(memory_space=pltpu.SMEM)
HBM = pl.BlockSpec(memory_space=pltpu.HBM)
PARAMS = pltpu.CompilerParams(vmem_limit_bytes=24 * 2**20)


def swap(array, bit):
    return lax.ppermute(array, "gx", [(i, i ^ (1 << bit)) for i in range(8)])


def cost(flops, nbytes, exps=0):
    return pl.CostEstimate(flops=flops, bytes_accessed=nbytes, transcendentals=exps)


def aligned(index, step):
    return pl.ds(pl.multiple_of(index * step, 128), step)


def gate_up(v, gate_weight, up_weight, starts, counts, out_type):
    rows, depth = v.shape
    blocks = sum(counts)

    def kernel(starts_ref, v_ref, gate_ref, up_ref, *rest):
        out_refs, (held, sems) = rest[: len(counts)], rest[len(counts) :]
        firsts = [sum(counts[:r]) for r in range(len(counts))]

        def copy(r, i, which):
            columns = pl.ds(pl.multiple_of((starts_ref[r] + i) * BLOCK, BLOCK), BLOCK)
            slot = firsts[r] + i
            source = (gate_ref, up_ref)[which].at[:, columns]
            return pltpu.make_async_copy(source, held.at[slot, which], sems.at[slot, which])

        for r, n in enumerate(counts):
            for i in range(n):
                for which in range(2):
                    copy(r, i, which).start()
        for r, n in enumerate(counts):

            @pl.loop(0, n)
            def _(i):
                for which in range(2):
                    copy(r, i, which).wait()
                    out_refs[r][which, :, aligned(i, BLOCK)] = jnp.dot(
                        v_ref[...], held[firsts[r] + i, which], preferred_element_type=F32
                    ).astype(out_type)

    out = pl.pallas_call(
        kernel,
        out_shape=[jax.ShapeDtypeStruct((2, rows, n * BLOCK), out_type) for n in counts],
        in_specs=[SMEM, VMEM, HBM, HBM],
        out_specs=[VMEM] * len(counts),
        scratch_shapes=[
            pltpu.VMEM((blocks, 2, depth, BLOCK), BF16),
            pltpu.SemaphoreType.DMA((blocks, 2)),
        ],
        compiler_params=PARAMS,
        cost_estimate=cost(4 * rows * depth * blocks * BLOCK, 4 * depth * blocks * BLOCK),
        name="gate_up",
    )(jnp.stack(starts), v, gate_weight, up_weight)
    return list(out)


def down(total, hiddens, down_weight, starts):
    rows = hiddens[0].shape[0]
    columns = down_weight.shape[1]
    counts = [h.shape[1] // BLOCK for h in hiddens]
    blocks = sum(counts)

    def kernel(starts_ref, *rest):
        hidden_refs, rest = rest[: len(counts)], rest[len(counts) :]
        total_ref, rest = (rest[0], rest[1:]) if total is not None else (None, rest)
        weight_ref, out_ref, held, sems = rest
        firsts = [sum(counts[:r]) for r in range(len(counts))]

        def copy(r, i):
            at = pl.ds(pl.multiple_of((starts_ref[r] + i) * BLOCK, BLOCK), BLOCK)
            slot = firsts[r] + i
            return pltpu.make_async_copy(weight_ref.at[at, :], held.at[slot], sems.at[slot])

        for r, n in enumerate(counts):
            for i in range(n):
                copy(r, i).start()
        out_ref[...] = jnp.zeros_like(out_ref) if total_ref is None else total_ref[...]
        for r, n in enumerate(counts):

            @pl.loop(0, n)
            def _(i):
                copy(r, i).wait()
                out_ref[...] += jnp.dot(
                    hidden_refs[r][:, aligned(i, BLOCK)],
                    held[firsts[r] + i],
                    preferred_element_type=F32,
                )

    totals = [] if total is None else [total]
    return pl.pallas_call(
        kernel,
        out_shape=jax.ShapeDtypeStruct((rows, columns), F32),
        in_specs=[SMEM] + [VMEM] * (len(counts) + len(totals)) + [HBM],
        out_specs=VMEM,
        scratch_shapes=[
            pltpu.VMEM((blocks, BLOCK, columns), BF16),
            pltpu.SemaphoreType.DMA((blocks,)),
        ],
        compiler_params=PARAMS,
        cost_estimate=cost(2 * rows * columns * blocks * BLOCK, 2 * columns * blocks * BLOCK),
        name="down",
    )(jnp.stack(starts), *hiddens, *totals, down_weight)


def small(name, kernel, out_shape, *operands):
    n = sum(o.size for o in operands[1:])
    return pl.pallas_call(
        kernel,
        out_shape=out_shape,
        in_specs=[SMEM] + [VMEM] * (len(operands) - 1),
        out_specs=jax.tree.map(lambda _: VMEM, out_shape),
        compiler_params=PARAMS,
        cost_estimate=cost(2 * n, 8 * n),
        name=name,
    )(*operands)


def shape(dims, dtype):
    return jax.ShapeDtypeStruct(dims, dtype)


def halve(bits, bit, kept, received):
    _, rows, width = kept.shape
    half = width // 2

    def kernel(bits_ref, kept_ref, received_ref, own_ref, send_ref):
        mine, theirs = aligned(bits_ref[bit], half), aligned(1 - bits_ref[bit], half)
        send_ref[...] = (kept_ref[:, :, theirs] + received_ref[:, :, theirs].astype(F32)).astype(BF16)
        own_ref[...] = kept_ref[:, :, mine] + received_ref[:, :, mine].astype(F32)

    dims = (2, rows, half)
    return small("halve", kernel, [shape(dims, F32), shape(dims, BF16)], bits, kept, received)


def halve_far(bits, kepts, receiveds):
    rows = kepts[0].shape[1]
    halves = [k.shape[2] // 2 for k in kepts]

    def kernel(bits_ref, *refs):
        kept_refs, received_refs = refs[: len(halves)], refs[len(halves) : -2]
        own_ref, send_ref = refs[-2:]
        at = 0
        for kept_ref, received_ref, half in zip(kept_refs, received_refs, halves):
            to = slice(at, at + half)
            mine, theirs = aligned(bits_ref[FAR], half), aligned(1 - bits_ref[FAR], half)
            send_ref[:, :, to] = (
                kept_ref[:, :, theirs] + received_ref[:, :, theirs].astype(F32)
            ).astype(BF16)
            own_ref[:, :, to] = kept_ref[:, :, mine] + received_ref[:, :, mine].astype(F32)
            at += half

    dims = (2, rows, sum(halves))
    shapes = [shape(dims, F32), shape(dims, BF16)]
    return small("halve_far", kernel, shapes, bits, *kepts, *receiveds)


def gated(bits, own, received):
    _, rows, width = own.shape

    def kernel(bits_ref, own_ref, received_ref, out_ref):
        gate = own_ref[0] + received_ref[0].astype(F32)
        up = own_ref[1] + received_ref[1].astype(F32)
        out_ref[...] = (gate / (1.0 + jnp.exp(-gate)) * up).astype(BF16)

    return small("gated", kernel, shape((rows, width), BF16), bits, own, received)


def join_far(bits, own, received, halves):
    rows = own.shape[0]

    def kernel(bits_ref, own_ref, received_ref, *out_refs):
        at = 0
        for out_ref, half in zip(out_refs, halves):
            out_ref[:, aligned(bits_ref[FAR], half)] = own_ref[:, at : at + half]
            out_ref[:, aligned(1 - bits_ref[FAR], half)] = received_ref[:, at : at + half]
            at += half

    shapes = [shape((rows, 2 * half), BF16) for half in halves]
    return small("join_far", kernel, shapes, bits, own, received)


def join(bits, bit, own, received):
    rows, half = own.shape

    def kernel(bits_ref, own_ref, received_ref, out_ref):
        out_ref[:, aligned(bits_ref[bit], half)] = own_ref[...]
        out_ref[:, aligned(1 - bits_ref[bit], half)] = received_ref[...]

    return small("join", kernel, shape((rows, 2 * half), BF16), bits, own, received)


def fast_layer(v, gate_weight, up_weight, down_weight):
    gx = lax.axis_index("gx")
    bits = jnp.stack([gx & 1, (gx >> 1) & 1, gx >> 2])
    mine, theirs, at = [], [], 0
    for counts in CHUNKS:
        mine.append([])
        theirs.append([])
        for n, (first, _) in zip(counts, STREAM_BITS):
            mine[-1].append(at + bits[first] * n)
            theirs[-1].append(at + (1 - bits[first]) * n)
            at += 2 * n
    received, kept = [], []
    for c, counts in enumerate(CHUNKS):
        received.append([])
        for n, start, (first, _) in zip(counts, theirs[c], STREAM_BITS):
            (sent,) = gate_up(v, gate_weight, up_weight, [start], [n], BF16)
            received[c].append(swap(sent, first))
        kept.append(gate_up(v, gate_weight, up_weight, mine[c], counts, F32))
    total = None
    for c, counts in enumerate(CHUNKS):
        owns, others = [], []
        for s, (_, second) in enumerate(STREAM_BITS):
            own, send = halve(bits, second, kept[c][s], received[c][s])
            owns.append(own)
            others.append(swap(send, second))
        own, send = halve_far(bits, owns, others)
        hidden = gated(bits, own, swap(send, FAR))
        quarters = join_far(bits, hidden, swap(hidden, FAR), [128 * n for n in counts])
        halves = [
            join(bits, second, q, swap(q, second)) for q, (_, second) in zip(quarters, STREAM_BITS)
        ]
        others = [swap(h, first) for h, (first, _) in zip(halves, STREAM_BITS)]
        total = down(total, halves, down_weight, mine[c])
        total = down(total, others, down_weight, theirs[c])
    return (total + lax.ppermute(total, "gy", [(0, 1), (1, 0)])).astype(BF16)


def fast_body(tokens, gate_weight, up_weight, down_weight):
    own_rows = tokens.shape[1]
    gy = lax.axis_index("gy")
    gate_weight, up_weight, down_weight = (
        pltpu.with_memory_space_constraint(w, pltpu.HBM)
        for w in (gate_weight, up_weight, down_weight)
    )
    rows = lax.all_gather(tokens, "gy", axis=1, tiled=True)
    first_out = fast_layer(rows[0], gate_weight, up_weight, down_weight)
    second_input = (rows[1].astype(F32) + first_out.astype(F32)).astype(BF16)
    second_out = fast_layer(second_input, gate_weight, up_weight, down_weight)
    outs = jnp.stack([first_out, second_out])
    return lax.dynamic_slice_in_dim(outs, gy * own_rows, own_rows, axis=1)


def plain_body(tokens, gate_weight, up_weight, down_weight):
    def layer_apply(local_input):
        row_block = lax.all_gather(local_input, "gy", axis=0, tiled=True)
        batch_rows = row_block.shape[0]
        gate_term = jnp.dot(row_block, gate_weight, preferred_element_type=F32)
        up_term = jnp.dot(row_block, up_weight, preferred_element_type=F32)
        stacked = jnp.concatenate([gate_term, up_term], axis=0)
        summed = lax.psum_scatter(stacked, "gx", scatter_dimension=1, tiled=True)
        hidden_part = (jax.nn.silu(summed[:batch_rows]) * summed[batch_rows:]).astype(BF16)
        partial_out = jnp.dot(
            lax.all_gather(hidden_part, "gx", axis=1, tiled=True),
            down_weight,
            preferred_element_type=F32,
        )
        return lax.psum_scatter(partial_out, "gy", scatter_dimension=0, tiled=True).astype(BF16)

    first_out = layer_apply(tokens[0])
    second_input = (tokens[1].astype(F32) + first_out.astype(F32)).astype(BF16)
    second_out = layer_apply(second_input)
    return jnp.stack([first_out, second_out])


def solution(mesh):
    fast = mesh.shape["gx"] == 8 and mesh.shape["gy"] == 2
    return jax.shard_map(
        fast_body if fast else plain_body,
        mesh=mesh,
        in_specs=(P(None, ("replica", "gy"), "gx"), P("gx", "gy"), P("gx", "gy"), P("gy", "gx")),
        out_specs=P(None, ("replica", "gy"), "gx"),
        check_vma=False,
    )
```

time: 465 us -> 210 us (0.45)
  waiting for transfers between devices: 358 us -> 50.3 us
  Pallas kernels: 0 us -> 102 us
  matrix products: 74.6 us -> 0 us
  starting transfers between devices: 0.39 us -> 52.7 us
  between operations: 13.5 us -> 0.52 us
  other arithmetic: 12.9 us -> 1.12 us
    reduce_scatter x4 -> x0, waiting for transfers between devices: 268 us -> none  [the longest x2 255 us: layer_apply(): summed = lax.psum_scatter(stacked, 'gx', scatter_dimension=1, tiled=True)]
    pallas_call x0 -> x48, Pallas kernels: none -> 102 us  [the longest x12 52.3 us: gate_up(): pl.pallas_call(kernel, out_shape=[jax.ShapeDtypeStruct((2, rows, n * BLOC...]
    all_gather x2 -> x0, waiting for transfers between devices: 89.6 us -> none  [layer_apply(): lax.all_gather(hidden_part, 'gx', axis=1, tiled=True)]
    dot_general x6 -> x0, matrix products: 74.6 us -> none  [the longest x2 29.6 us: layer_apply(): jnp.dot(lax.all_gather(hidden_part, 'gx', axis=1, tiled=True), down_weigh...]
    ppermute x0 -> x42, starting transfers between devices: none -> 52.7 us  [the longest x40 52.5 us: swap(): return lax.ppermute(array, 'gx', [(i, i ^ 1 << bit) for i in range(8)])]
    ppermute x0 -> x42, waiting for transfers between devices: none -> 50.3 us  [the longest x40 47.3 us: swap(): return lax.ppermute(array, 'gx', [(i, i ^ 1 << bit) for i in range(8)])]
    concatenate x2 -> x0, other arithmetic: 6.52 us -> none  [layer_apply(): stacked = jnp.concatenate([gate_term, up_term], axis=0)]
  transfers between devices with their start and end apart: 6 -> 42, of which waited for: 6 -> 15; matrix products, arithmetic and copies ran while one was open for 0% -> 0% of each run, Pallas kernels for 0% -> 41%
where the time goes in v1:
time: 210 us
  Pallas kernels  102 us (49%)
  starting transfers between devices  52.7 us (25%)
  waiting for transfers between devices  50.3 us (24%)
  blocking collectives  2.36 us (1%)
    ppermute x40, starting transfers between devices, swap(): return lax.ppermute(array, 'gx', [(i, i ^ 1 << bit) for i in range(8)])  52.5 us
    pallas_call x12, Pallas kernels, gate_up(): pl.pallas_call(kernel, out_shape=[jax.ShapeDtypeStruct((2, rows, n * BLOC...  52.3 us
    ppermute x40, waiting for transfers between devices, swap(): return lax.ppermute(array, 'gx', [(i, i ^ 1 << bit) for i in range(8)])  47.3 us
    pallas_call x8, Pallas kernels, down(): pl.pallas_call(kernel, out_shape=jax.ShapeDtypeStruct((rows, columns), F3...  30.9 us
    pallas_call x28, Pallas kernels, small(): pl.pallas_call(kernel, out_shape=out_shape, in_specs=[SMEM] + [VMEM] * (l...  18.9 us
  transfers between devices with their start and end apart: 42, of which 15 were waited for; matrix products, arithmetic and copies ran while one was open for 0% of the time, Pallas kernels for 41%

profile of v1, /device:TPU:0, one launch (start us, length us, event | category | flops | bytes accessed | tf_op | source)
XLA Modules:
  0.0 209.8 jit_solution(394965667490694568)
XLA Ops:
  0.0 2.4 %all_gather.3 = bf16[2,64,1024]{2,1,0:T(8,128)(2,1)S(1)} all-gather(bf16[2,32,1024]{2,1,0:T(8,128)(2,1)} %param.4), channel_id=1, replica_groups=mesh['replica'=2,'gx'=8,'gy'=2] {'gy'}, dimensions={1}, use_global_device_ids=true | all-gather | bytes 393216 | tf_op jit(solution)/shard_map/all_gather | solution.py:255
  2.4 0.7 copy-done
  3.1 3.9 %gate_up.16 = bf16[2,64,2048]{2,1,0:T(8,128)(2,1)S(1)} custom-call(s32[1]{0:T(128)} %bitcast.8.starts_ref, bf16[64,1024]{1,0:T(8,128)(2,1)S(1)} %slice_bitcast_fusion.1.v_ref, bf16[1024,13312]{1,0:T(8,128)(2,1)} %gate_ref.23, bf16[1024,13312]{1,0:T(8,128)(2,1)} %up_ref.23), custom_call_target="tpu_custom_call" | custom-call | flops 536870912 | bytes 8388608 | tf_op jit(solution)/shard_map/gate_up/pallas_call | solution.py:60
  7.0 2.9 %collective-permute-start.10 = (bf16[2,64,2048]{2,1,0:T(8,128)(2,1)S(1)}, bf16[2,64,2048]{2,1,0:T(8,128)(2,1)S(1)}, u32[]{:S(2)}, u32[]{:S(2)}) collective-permute-start(bf16[2,64,2048]{2,1,0:T(8,128)(2,1)S(1)} %gate_up.16), channel_id=1, source_target_pairs={{0,2},{2,0},{4,6},{6,4},{8,10},{10,8},{12,14},{14,12},{1,3},{3,1},... | collective-permute-start | bytes 1572872 | tf_op jit(solution)/shard_map/ppermute | solution.py:21
  9.8 3.9 %gate_up.17 = bf16[2,64,1536]{2,1,0:T(8,128)(2,1)} custom-call(s32[1]{0:T(128)} %bitcast.9.starts_ref, bf16[64,1024]{1,0:T(8,128)(2,1)S(1)} %slice_bitcast_fusion.1.v_ref, bf16[1024,13312]{1,0:T(8,128)(2,1)} %gate_ref.23, bf16[1024,13312]{1,0:T(8,128)(2,1)} %up_ref.23), custom_call_target="tpu_custom_call" | custom-call | flops 402653184 | bytes 6291456 | tf_op jit(solution)/shard_map/gate_up/pallas_call | solution.py:60
  13.8 1.6 collective-permute-start.11
  15.4 3.9 %gate_up.13 = bf16[2,64,1536]{2,1,0:T(8,128)(2,1)} custom-call(s32[1]{0:T(128)} %bitcast.starts_ref, bf16[64,1024]{1,0:T(8,128)(2,1)S(1)} %slice_bitcast_fusion.1.v_ref, bf16[1024,13312]{1,0:T(8,128)(2,1)} %gate_ref.23, bf16[1024,13312]{1,0:T(8,128)(2,1)} %up_ref.23), custom_call_target="tpu_custom_call" | custom-call | flops 402653184 | bytes 6291456 | tf_op jit(solution)/shard_map/gate_up/pallas_call | solution.py:60
  20.0 3.2 %gate_up.14 = bf16[2,64,1536]{2,1,0:T(8,128)(2,1)S(1)} custom-call(s32[1]{0:T(128)} %bitcast.1.starts_ref, bf16[64,1024]{1,0:T(8,128)(2,1)S(1)} %slice_bitcast_fusion.1.v_ref, bf16[1024,13312]{1,0:T(8,128)(2,1)} %gate_ref.23, bf16[1024,13312]{1,0:T(8,128)(2,1)} %up_ref.23), custom_call_target="tpu_custom_call" | custom-call | flops 402653184 | bytes 6291456 | tf_op jit(solution)/shard_map/gate_up/pallas_call | solution.py:60
  23.4 6.3 %gate_up.15 = (f32[2,64,2048]{2,1,0:T(8,128)S(1)}, f32[2,64,1536]{2,1,0:T(8,128)S(1)}) custom-call(s32[2]{0:T(128)S(1)} %pad_add_fusion.4.starts_ref, bf16[64,1024]{1,0:T(8,128)(2,1)S(1)} %slice_bitcast_fusion.1.v_ref, bf16[1024,13312]{1,0:T(8,128)(2,1)} %gate_ref.23, bf16[1024,13312]{1,0:T(8,128)(2,1)} %up_ref.23), custom_call_target="tpu_custom_call" | custom-call | flops 939524096 | bytes 14680064 | tf_op jit(solution)/shard_map/gate_up/pallas_call | solution.py:60
  29.8 1.3 halve.10
  31.1 2.0 collective-permute-start.12
  33.1 1.1 halve.11
  34.2 1.6 collective-permute-start.13
  35.9 5.7 %gate_up.12 = (f32[2,64,1536]{2,1,0:T(8,128)S(1)}, f32[2,64,1536]{2,1,0:T(8,128)S(1)}) custom-call(s32[2]{0:T(128)S(1)} %pad_add_fusion.2.starts_ref, bf16[64,1024]{1,0:T(8,128)(2,1)S(1)} %slice_bitcast_fusion.1.v_ref, bf16[1024,13312]{1,0:T(8,128)(2,1)} %gate_ref.23, bf16[1024,13312]{1,0:T(8,128)(2,1)} %up_ref.23), custom_call_target="tpu_custom_call" | custom-call | flops 805306368 | bytes 12582912 | tf_op jit(solution)/shard_map/gate_up/pallas_call | solution.py:60
  41.5 1.1 halve.8
  43.3 1.1 halve.9
  45.1 3.0 %collective-permute-start.14 = (bf16[2,64,896]{2,1,0:T(8,128)(2,1)S(1)}, bf16[2,64,896]{2,1,0:T(8,128)(2,1)S(1)}, u32[]{:S(2)}, u32[]{:S(2)}) collective-permute-start(bf16[2,64,896]{2,1,0:T(8,128)(2,1)S(1)} %get-tuple-element.62), channel_id=1, source_target_pairs={{0,8},{2,10},{4,12},{6,14},{8,0},{10,2},{12,4},{14,6},{1,9},{3,11}... | collective-permute-start | bytes 688136 | tf_op jit(solution)/shard_map/ppermute | solution.py:21
  48.1 2.4 %collective-permute-done.2.refs_2_ = bf16[2,64,768]{2,1,0:T(8,128)(2,1)S(1)} collective-permute-done((bf16[2,64,768]{2,1,0:T(8,128)(2,1)S(1)}, bf16[2,64,768]{2,1,0:T(8,128)(2,1)S(1)}, u32[]{:S(2)}, u32[]{:S(2)}) %collective-permute-start.2) | collective-permute-done | bytes 196640 | tf_op jit(solution)/shard_map/ppermute | solution.py:21
  51.1 2.6 %collective-permute-start.4 = (bf16[2,64,768]{2,1,0:T(8,128)(2,1)S(1)}, bf16[2,64,768]{2,1,0:T(8,128)(2,1)S(1)}, u32[]{:S(2)}, u32[]{:S(2)}) collective-permute-start(bf16[2,64,768]{2,1,0:T(8,128)(2,1)S(1)} %get-tuple-element.52), channel_id=1, source_target_pairs={{0,8},{2,10},{4,12},{6,14},{8,0},{10,2},{12,4},{14,6},{1,9},{3,11}... | collective-permute-start | bytes 589832 | tf_op jit(solution)/shard_map/ppermute | solution.py:21
  53.8 9.0 %collective-permute-done.14.received_ref = bf16[2,64,896]{2,1,0:T(8,128)(2,1)S(1)} collective-permute-done((bf16[2,64,896]{2,1,0:T(8,128)(2,1)S(1)}, bf16[2,64,896]{2,1,0:T(8,128)(2,1)S(1)}, u32[]{:S(2)}, u32[]{:S(2)}) %collective-permute-start.14) | collective-permute-done | bytes 229408 | tf_op jit(solution)/shard_map/ppermute | solution.py:21
  63.5 6.9 %collective-permute-done.15.received_ref = bf16[64,896]{1,0:T(8,128)(2,1)S(1)} collective-permute-done((bf16[64,896]{1,0:T(8,128)(2,1)S(1)}, bf16[64,896]{1,0:T(8,128)(2,1)S(1)}, u32[]{:S(2)}, u32[]{:S(2)}) %collective-permute-start.15) | collective-permute-done | bytes 114720 | tf_op jit(solution)/shard_map/ppermute | solution.py:21
  72.1 3.4 %collective-permute-start.5 = (bf16[64,768]{1,0:T(8,128)(2,1)S(1)}, bf16[64,768]{1,0:T(8,128)(2,1)S(1)}, u32[]{:S(2)}, u32[]{:S(2)}) collective-permute-start(bf16[64,768]{1,0:T(8,128)(2,1)S(1)} %gated.4.own_ref), channel_id=1, source_target_pairs={{0,8},{2,10},{4,12},{6,14},{8,0},{10,2},{12,4},{14,6},{1,9},{3,11}... | collective-permute-start | bytes 294920 | tf_op jit(solution)/shard_map/ppermute | solution.py:21
  75.6 1.6 collective-permute-start.18
  77.1 2.8 %collective-permute-done.5.received_ref = bf16[64,768]{1,0:T(8,128)(2,1)S(1)} collective-permute-done((bf16[64,768]{1,0:T(8,128)(2,1)S(1)}, bf16[64,768]{1,0:T(8,128)(2,1)S(1)}, u32[]{:S(2)}, u32[]{:S(2)}) %collective-permute-start.5) | collective-permute-done | bytes 98336 | tf_op jit(solution)/shard_map/ppermute | solution.py:21
  80.5 1.5 collective-permute-start.8
  83.0 1.7 collective-permute-start.19
  87.0 0.8 collective-permute-done.6.received_ref
  88.3 0.8 collective-permute-start.7
  89.2 4.0 %down.8.rest_2_ = f32[64,1024]{1,0:T(8,128)S(1)} custom-call(s32[2]{0:T(128)S(1)} %pad_add_fusion.4.starts_ref, bf16[64,2048]{1,0:T(8,128)(2,1)S(1)} %join.10.rest_0_, bf16[64,1536]{1,0:T(8,128)(2,1)S(1)} %join.11.rest_1_, bf16[13312,1024]{1,0:T(8,128)(2,1)} %rest_3_.11), custom_call_target="tpu_custom_call" | custom-call | flops 469762048 | bytes 7340032 | tf_op jit(solution)/shard_map/down/pallas_call | solution.py:109
  93.2 4.0 %down.9.rest_2_ = f32[64,1024]{1,0:T(8,128)S(1)} custom-call(s32[2]{0:T(128)S(1)} %pad_add_fusion.3.starts_ref, bf16[64,2048]{1,0:T(8,128)(2,1)S(1)} %collective-permute-done.17.rest_0_, bf16[64,1536]{1,0:T(8,128)(2,1)S(1)} %collective-permute-done.19.rest_1_, f32[64,1024]{1,0:T(8,128)S(1)} %down.8.rest_2_, bf16[13312,1024]{1,0:T(8,128)(2,1)} %rest_3_.11), custom_call_target="tpu_custom_call" | custom-call | flops 469762048 | bytes 7340032 | tf_op jit(solution)/shard_map/down/pallas_call | solution.py:109
  97.2 3.7 %down.10.rest_2_ = f32[64,1024]{1,0:T(8,128)S(1)} custom-call(s32[2]{0:T(128)S(1)} %pad_add_fusion.2.starts_ref, bf16[64,1536]{1,0:T(8,128)(2,1)S(1)} %join.8.rest_0_, bf16[64,1536]{1,0:T(8,128)(2,1)S(1)} %join.9.rest_1_, f32[64,1024]{1,0:T(8,128)S(1)} %down.9.rest_2_, bf16[13312,1024]{1,0:T(8,128)(2,1)} %rest_3_.11), custom_call_target="tpu_custom_call" | custom-call | flops 402653184 | bytes 6291456 | tf_op jit(solution)/shard_map/down/pallas_call | solution.py:109
  101.0 3.7 %down.11 = f32[64,1024]{1,0:T(8,128)S(1)} custom-call(s32[2]{0:T(128)S(1)} %pad_add_fusion.starts_ref, bf16[64,1536]{1,0:T(8,128)(2,1)S(1)} %collective-permute-done.7.rest_0_, bf16[64,1536]{1,0:T(8,128)(2,1)S(1)} %collective-permute-done.9.rest_1_, f32[64,1024]{1,0:T(8,128)S(1)} %down.10.rest_2_, bf16[13312,1024]{1,0:T(8,128)(2,1)} %rest_3_.11), custom_call_target="tpu_custom_call" | custom-call | flops 402653184 | bytes 6291456 | tf_op jit(solution)/shard_map/down/pallas_call | solution.py:109
  104.8 1.5 collective-permute-done.20
  106.3 3.9 %gate_up.22 = bf16[2,64,2048]{2,1,0:T(8,128)(2,1)S(1)} custom-call(s32[1]{0:T(128)} %bitcast.8.starts_ref, bf16[64,1024]{1,0:T(8,128)(2,1)S(1)} %get-tuple-element.85.v_ref, bf16[1024,13312]{1,0:T(8,128)(2,1)} %gate_ref.23, bf16[1024,13312]{1,0:T(8,128)(2,1)} %up_ref.23), custom_call_target="tpu_custom_call" | custom-call | flops 536870912 | bytes 8388608 | tf_op jit(solution)/shard_map/gate_up/pallas_call | solution.py:60
  110.2 1.4 collective-permute-start.31
  111.6 3.2 %gate_up.23 = bf16[2,64,1536]{2,1,0:T(8,128)(2,1)S(1)} custom-call(s32[1]{0:T(128)} %bitcast.9.starts_ref, bf16[64,1024]{1,0:T(8,128)(2,1)S(1)} %get-tuple-element.85.v_ref, bf16[1024,13312]{1,0:T(8,128)(2,1)} %gate_ref.23, bf16[1024,13312]{1,0:T(8,128)(2,1)} %up_ref.23), custom_call_target="tpu_custom_call" | custom-call | flops 402653184 | bytes 6291456 | tf_op jit(solution)/shard_map/gate_up/pallas_call | solution.py:60
  114.8 1.1 collective-permute-start.32
  115.9 3.2 %gate_up.20 = bf16[2,64,1536]{2,1,0:T(8,128)(2,1)S(1)} custom-call(s32[1]{0:T(128)} %bitcast.1.starts_ref, bf16[64,1024]{1,0:T(8,128)(2,1)S(1)} %get-tuple-element.85.v_ref, bf16[1024,13312]{1,0:T(8,128)(2,1)} %gate_ref.23, bf16[1024,13312]{1,0:T(8,128)(2,1)} %up_ref.23), custom_call_target="tpu_custom_call" | custom-call | flops 402653184 | bytes 6291456 | tf_op jit(solution)/shard_map/gate_up/pallas_call | solution.py:60
  119.1 1.1 collective-permute-start.22
  120.1 3.2 %gate_up.19 = bf16[2,64,1536]{2,1,0:T(8,128)(2,1)S(1)} custom-call(s32[1]{0:T(128)} %bitcast.starts_ref, bf16[64,1024]{1,0:T(8,128)(2,1)S(1)} %get-tuple-element.85.v_ref, bf16[1024,13312]{1,0:T(8,128)(2,1)} %gate_ref.23, bf16[1024,13312]{1,0:T(8,128)(2,1)} %up_ref.23), custom_call_target="tpu_custom_call" | custom-call | flops 402653184 | bytes 6291456 | tf_op jit(solution)/shard_map/gate_up/pallas_call | solution.py:60
  123.3 0.8 collective-permute-start.21
  124.1 6.3 %gate_up.21 = (f32[2,64,2048]{2,1,0:T(8,128)S(1)}, f32[2,64,1536]{2,1,0:T(8,128)S(1)}) custom-call(s32[2]{0:T(128)S(1)} %pad_add_fusion.4.starts_ref, bf16[64,1024]{1,0:T(8,128)(2,1)S(1)} %get-tuple-element.85.v_ref, bf16[1024,13312]{1,0:T(8,128)(2,1)} %gate_ref.23, bf16[1024,13312]{1,0:T(8,128)(2,1)} %up_ref.23), custom_call_target="tpu_custom_call" | custom-call | flops 939524096 | bytes 14680064 | tf_op jit(solution)/shard_map/gate_up/pallas_call | solution.py:60
  131.1 1.9 collective-permute-start.33
  134.3 5.1 %collective-permute-done.34.refs_3_ = bf16[2,64,768]{2,1,0:T(8,128)(2,1)S(1)} collective-permute-done((bf16[2,64,768]{2,1,0:T(8,128)(2,1)S(1)}, bf16[2,64,768]{2,1,0:T(8,128)(2,1)S(1)}, u32[]{:S(2)}, u32[]{:S(2)}) %collective-permute-start.34) | collective-permute-done | bytes 196640 | tf_op jit(solution)/shard_map/ppermute | solution.py:21
  140.4 2.1 %collective-permute-start.35 = (bf16[2,64,896]{2,1,0:T(8,128)(2,1)S(1)}, bf16[2,64,896]{2,1,0:T(8,128)(2,1)S(1)}, u32[]{:S(2)}, u32[]{:S(2)}) collective-permute-start(bf16[2,64,896]{2,1,0:T(8,128)(2,1)S(1)} %get-tuple-element.82), channel_id=1, source_target_pairs={{0,8},{2,10},{4,12},{6,14},{8,0},{10,2},{12,4},{14,6},{1,9},{3,11}... | collective-permute-start | bytes 688136 | tf_op jit(solution)/shard_map/ppermute | solution.py:21
  142.5 5.7 %gate_up.18 = (f32[2,64,1536]{2,1,0:T(8,128)S(1)}, f32[2,64,1536]{2,1,0:T(8,128)S(1)}) custom-call(s32[2]{0:T(128)S(1)} %pad_add_fusion.2.starts_ref, bf16[64,1024]{1,0:T(8,128)(2,1)S(1)} %get-tuple-element.85.v_ref, bf16[1024,13312]{1,0:T(8,128)(2,1)} %gate_ref.23, bf16[1024,13312]{1,0:T(8,128)(2,1)} %up_ref.23), custom_call_target="tpu_custom_call" | custom-call | flops 805306368 | bytes 12582912 | tf_op jit(solution)/shard_map/gate_up/pallas_call | solution.py:60
  148.9 1.7 collective-permute-start.24
  151.5 3.1 %collective-permute-done.24.refs_3_ = bf16[2,64,768]{2,1,0:T(8,128)(2,1)S(1)} collective-permute-done((bf16[2,64,768]{2,1,0:T(8,128)(2,1)S(1)}, bf16[2,64,768]{2,1,0:T(8,128)(2,1)S(1)}, u32[]{:S(2)}, u32[]{:S(2)}) %collective-permute-start.24) | collective-permute-done | bytes 196640 | tf_op jit(solution)/shard_map/ppermute | solution.py:21
  154.6 2.4 %collective-permute-done.23.refs_2_ = bf16[2,64,768]{2,1,0:T(8,128)(2,1)S(1)} collective-permute-done((bf16[2,64,768]{2,1,0:T(8,128)(2,1)S(1)}, bf16[2,64,768]{2,1,0:T(8,128)(2,1)S(1)}, u32[]{:S(2)}, u32[]{:S(2)}) %collective-permute-start.23) | collective-permute-done | bytes 196640 | tf_op jit(solution)/shard_map/ppermute | solution.py:21
  158.9 2.5 %collective-permute-start.36 = (bf16[64,896]{1,0:T(8,128)(2,1)S(1)}, bf16[64,896]{1,0:T(8,128)(2,1)S(1)}, u32[]{:S(2)}, u32[]{:S(2)}) collective-permute-start(bf16[64,896]{1,0:T(8,128)(2,1)S(1)} %gated.7.own_ref), channel_id=1, source_target_pairs={{0,8},{2,10},{4,12},{6,14},{8,0},{10,2},{12,4},{14,6},{1,9},{3,11}... | collective-permute-start | bytes 344072 | tf_op jit(solution)/shard_map/ppermute | solution.py:21
  161.3 10.9 %collective-permute-done.36.received_ref = bf16[64,896]{1,0:T(8,128)(2,1)S(1)} collective-permute-done((bf16[64,896]{1,0:T(8,128)(2,1)S(1)}, bf16[64,896]{1,0:T(8,128)(2,1)S(1)}, u32[]{:S(2)}, u32[]{:S(2)}) %collective-permute-start.36) | collective-permute-done | bytes 114720 | tf_op jit(solution)/shard_map/ppermute | solution.py:21
  173.7 3.4 %collective-permute-start.26 = (bf16[64,768]{1,0:T(8,128)(2,1)S(1)}, bf16[64,768]{1,0:T(8,128)(2,1)S(1)}, u32[]{:S(2)}, u32[]{:S(2)}) collective-permute-start(bf16[64,768]{1,0:T(8,128)(2,1)S(1)} %gated.6.own_ref), channel_id=1, source_target_pairs={{0,8},{2,10},{4,12},{6,14},{8,0},{10,2},{12,4},{14,6},{1,9},{3,11}... | collective-permute-start | bytes 294920 | tf_op jit(solution)/shard_map/ppermute | solution.py:21
  177.1 1.4 collective-permute-start.39
  179.7 2.7 %collective-permute-start.38 = (bf16[64,2048]{1,0:T(8,128)(2,1)S(1)}, bf16[64,2048]{1,0:T(8,128)(2,1)S(1)}, u32[]{:S(2)}, u32[]{:S(2)}) collective-permute-start(bf16[64,2048]{1,0:T(8,128)(2,1)S(1)} %join.14.rest_0_), channel_id=1, source_target_pairs={{0,2},{2,0},{4,6},{6,4},{8,10},{10,8},{12,14},{14,12},{1,3},{3,1},... | collective-permute-start | bytes 786440 | tf_op jit(solution)/shard_map/ppermute | solution.py:21
  183.0 1.1 collective-permute-start.29
  184.9 1.8 collective-permute-start.40
  186.7 2.8 %collective-permute-done.29.received_ref = bf16[64,768]{1,0:T(8,128)(2,1)S(1)} collective-permute-done((bf16[64,768]{1,0:T(8,128)(2,1)S(1)}, bf16[64,768]{1,0:T(8,128)(2,1)S(1)}, u32[]{:S(2)}, u32[]{:S(2)}) %collective-permute-start.29) | collective-permute-done | bytes 98336 | tf_op jit(solution)/shard_map/ppermute | solution.py:21
  190.7 1.3 collective-permute-start.28
  192.0 4.0 %down.12.rest_2_ = f32[64,1024]{1,0:T(8,128)S(1)} custom-call(s32[2]{0:T(128)S(1)} %pad_add_fusion.4.starts_ref, bf16[64,2048]{1,0:T(8,128)(2,1)S(1)} %join.14.rest_0_, bf16[64,1536]{1,0:T(8,128)(2,1)S(1)} %join.15.rest_1_, bf16[13312,1024]{1,0:T(8,128)(2,1)} %rest_3_.11), custom_call_target="tpu_custom_call" | custom-call | flops 469762048 | bytes 7340032 | tf_op jit(solution)/shard_map/down/pallas_call | solution.py:109
  196.0 4.0 %down.13.rest_2_ = f32[64,1024]{1,0:T(8,128)S(1)} custom-call(s32[2]{0:T(128)S(1)} %pad_add_fusion.3.starts_ref, bf16[64,2048]{1,0:T(8,128)(2,1)S(1)} %collective-permute-done.38.rest_0_, bf16[64,1536]{1,0:T(8,128)(2,1)S(1)} %collective-permute-done.40.rest_1_, f32[64,1024]{1,0:T(8,128)S(1)} %down.12.rest_2_, bf16[13312,1024]{1,0:T(8,128)(2,1)} %rest_3_.11), custom_call_target="tpu_custom_call" | custom-call | flops 469762048 | bytes 7340032 | tf_op jit(solution)/shard_map/down/pallas_call | solution.py:109
  200.1 3.7 %down.14.rest_2_ = f32[64,1024]{1,0:T(8,128)S(1)} custom-call(s32[2]{0:T(128)S(1)} %pad_add_fusion.2.starts_ref, bf16[64,1536]{1,0:T(8,128)(2,1)S(1)} %join.12.rest_0_, bf16[64,1536]{1,0:T(8,128)(2,1)S(1)} %join.13.rest_1_, f32[64,1024]{1,0:T(8,128)S(1)} %down.13.rest_2_, bf16[13312,1024]{1,0:T(8,128)(2,1)} %rest_3_.11), custom_call_target="tpu_custom_call" | custom-call | flops 402653184 | bytes 6291456 | tf_op jit(solution)/shard_map/down/pallas_call | solution.py:109
  203.8 3.7 %down.15 = f32[64,1024]{1,0:T(8,128)S(1)} custom-call(s32[2]{0:T(128)S(1)} %pad_add_fusion.starts_ref, bf16[64,1536]{1,0:T(8,128)(2,1)S(1)} %collective-permute-done.28.rest_0_, bf16[64,1536]{1,0:T(8,128)(2,1)S(1)} %collective-permute-done.30.rest_1_, f32[64,1024]{1,0:T(8,128)S(1)} %down.14.rest_2_, bf16[13312,1024]{1,0:T(8,128)(2,1)} %rest_3_.11), custom_call_target="tpu_custom_call" | custom-call | flops 402653184 | bytes 6291456 | tf_op jit(solution)/shard_map/down/pallas_call | solution.py:109
  207.6 1.5 collective-permute-done.41
  209.1 0.7 fusion.2
  (82 shorter events, 21.7 us)
Async XLA Ops:
  2.4 0.7 copy-start
  7.0 22.8 %collective-permute-start.10 = (bf16[2,64,2048]{2,1,0:T(8,128)(2,1)S(1)}, bf16[2,64,2048]{2,1,0:T(8,128)(2,1)S(1)}, u32[]{:S(2)}, u32[]{:S(2)}) collective-permute-start(bf16[2,64,2048]{2,1,0:T(8,128)(2,1)S(1)} %gate_up.16), channel_id=1, source_target_pairs={{0,2},{2,0},{4,6},{6,4},{8,10},{10,8},{12,14},{14,12},{1,3},{3,1},... | collective-permute-start | bytes 1572872 | tf_op jit(solution)/shard_map/ppermute | solution.py:21
  13.8 19.3 %collective-permute-start.11 = (bf16[2,64,1536]{2,1,0:T(8,128)(2,1)}, bf16[2,64,1536]{2,1,0:T(8,128)(2,1)}, u32[]{:S(2)}, u32[]{:S(2)}) collective-permute-start(bf16[2,64,1536]{2,1,0:T(8,128)(2,1)} %gate_up.17), channel_id=1, source_target_pairs={{0,4},{2,6},{4,0},{6,2},{8,12},{10,14},{12,8},{14,10},{1,5},{3,7},... | collective-permute-start | bytes 1179656 | tf_op jit(solution)/shard_map/ppermute | solution.py:21
  19.4 22.2 %collective-permute-start = (bf16[2,64,1536]{2,1,0:T(8,128)(2,1)}, bf16[2,64,1536]{2,1,0:T(8,128)(2,1)}, u32[]{:S(2)}, u32[]{:S(2)}) collective-permute-start(bf16[2,64,1536]{2,1,0:T(8,128)(2,1)} %gate_up.13), channel_id=1, source_target_pairs={{0,2},{2,0},{4,6},{6,4},{8,10},{10,8},{12,14},{14,12},{1,3},{3,1},... | collective-permute-start | bytes 1179656 | tf_op jit(solution)/shard_map/ppermute | solution.py:21
  23.2 20.1 %collective-permute-start.1 = (bf16[2,64,1536]{2,1,0:T(8,128)(2,1)S(1)}, bf16[2,64,1536]{2,1,0:T(8,128)(2,1)}, u32[]{:S(2)}, u32[]{:S(2)}) collective-permute-start(bf16[2,64,1536]{2,1,0:T(8,128)(2,1)S(1)} %gate_up.14), channel_id=1, source_target_pairs={{0,4},{2,6},{4,0},{6,2},{8,12},{10,14},{12,8},{14,10},{1,5},{3,7},... | collective-permute-start | bytes 1179656 | tf_op jit(solution)/shard_map/ppermute | solution.py:21
  31.1 13.4 %collective-permute-start.12 = (bf16[2,64,1024]{2,1,0:T(8,128)(2,1)}, bf16[2,64,1024]{2,1,0:T(8,128)(2,1)S(1)}, u32[]{:S(2)}, u32[]{:S(2)}) collective-permute-start(bf16[2,64,1024]{2,1,0:T(8,128)(2,1)} %get-tuple-element.59), channel_id=1, source_target_pairs={{0,4},{2,6},{4,0},{6,2},{8,12},{10,14},{12,8},{14,10},{1,5},{3,7},... | collective-permute-start | bytes 786440 | tf_op jit(solution)/shard_map/ppermute | solution.py:21
  34.2 10.3 %collective-permute-start.13 = (bf16[2,64,768]{2,1,0:T(8,128)(2,1)S(1)}, bf16[2,64,768]{2,1,0:T(8,128)(2,1)S(1)}, u32[]{:S(2)}, u32[]{:S(2)}) collective-permute-start(bf16[2,64,768]{2,1,0:T(8,128)(2,1)S(1)} %get-tuple-element.60), channel_id=1, source_target_pairs={{0,2},{2,0},{4,6},{6,4},{8,10},{10,8},{12,14},{14,12},{1,3},{3,1},... | collective-permute-start | bytes 589832 | tf_op jit(solution)/shard_map/ppermute | solution.py:21
  42.6 7.8 %collective-permute-start.2 = (bf16[2,64,768]{2,1,0:T(8,128)(2,1)S(1)}, bf16[2,64,768]{2,1,0:T(8,128)(2,1)S(1)}, u32[]{:S(2)}, u32[]{:S(2)}) collective-permute-start(bf16[2,64,768]{2,1,0:T(8,128)(2,1)S(1)} %get-tuple-element.49), channel_id=1, source_target_pairs={{0,4},{2,6},{4,0},{6,2},{8,12},{10,14},{12,8},{14,10},{1,5},{3,7},... | collective-permute-start | bytes 589832 | tf_op jit(solution)/shard_map/ppermute | solution.py:21
  44.4 6.1 %collective-permute-start.3 = (bf16[2,64,768]{2,1,0:T(8,128)(2,1)S(1)}, bf16[2,64,768]{2,1,0:T(8,128)(2,1)S(1)}, u32[]{:S(2)}, u32[]{:S(2)}) collective-permute-start(bf16[2,64,768]{2,1,0:T(8,128)(2,1)S(1)} %get-tuple-element.50), channel_id=1, source_target_pairs={{0,2},{2,0},{4,6},{6,4},{8,10},{10,8},{12,14},{14,12},{1,3},{3,1},... | collective-permute-start | bytes 589832 | tf_op jit(solution)/shard_map/ppermute | solution.py:21
  45.1 17.6 %collective-permute-start.14 = (bf16[2,64,896]{2,1,0:T(8,128)(2,1)S(1)}, bf16[2,64,896]{2,1,0:T(8,128)(2,1)S(1)}, u32[]{:S(2)}, u32[]{:S(2)}) collective-permute-start(bf16[2,64,896]{2,1,0:T(8,128)(2,1)S(1)} %get-tuple-element.62), channel_id=1, source_target_pairs={{0,8},{2,10},{4,12},{6,14},{8,0},{10,2},{12,4},{14,6},{1,9},{3,11}... | collective-permute-start | bytes 688136 | tf_op jit(solution)/shard_map/ppermute | solution.py:21
  51.1 20.4 %collective-permute-start.4 = (bf16[2,64,768]{2,1,0:T(8,128)(2,1)S(1)}, bf16[2,64,768]{2,1,0:T(8,128)(2,1)S(1)}, u32[]{:S(2)}, u32[]{:S(2)}) collective-permute-start(bf16[2,64,768]{2,1,0:T(8,128)(2,1)S(1)} %get-tuple-element.52), channel_id=1, source_target_pairs={{0,8},{2,10},{4,12},{6,14},{8,0},{10,2},{12,4},{14,6},{1,9},{3,11}... | collective-permute-start | bytes 589832 | tf_op jit(solution)/shard_map/ppermute | solution.py:21
  63.4 7.0 %collective-permute-start.15 = (bf16[64,896]{1,0:T(8,128)(2,1)S(1)}, bf16[64,896]{1,0:T(8,128)(2,1)S(1)}, u32[]{:S(2)}, u32[]{:S(2)}) collective-permute-start(bf16[64,896]{1,0:T(8,128)(2,1)S(1)} %gated.5.own_ref), channel_id=1, source_target_pairs={{0,8},{2,10},{4,12},{6,14},{8,0},{10,2},{12,4},{14,6},{1,9},{3,11}... | collective-permute-start | bytes 344072 | tf_op jit(solution)/shard_map/ppermute | solution.py:21
  70.9 13.7 %collective-permute-start.16 = (bf16[64,1024]{1,0:T(8,128)(2,1)S(1)}, bf16[64,1024]{1,0:T(8,128)(2,1)S(1)}, u32[]{:S(2)}, u32[]{:S(2)}) collective-permute-start(bf16[64,1024]{1,0:T(8,128)(2,1)S(1)} %get-tuple-element.63.own_ref), channel_id=1, source_target_pairs={{0,4},{2,6},{4,0},{6,2},{8,12},{10,14},{12,8},{14,10},{1,5},{3,7},... | collective-permute-start | bytes 393224 | tf_op jit(solution)/shard_map/ppermute | solution.py:21
  72.1 7.8 %collective-permute-start.5 = (bf16[64,768]{1,0:T(8,128)(2,1)S(1)}, bf16[64,768]{1,0:T(8,128)(2,1)S(1)}, u32[]{:S(2)}, u32[]{:S(2)}) collective-permute-start(bf16[64,768]{1,0:T(8,128)(2,1)S(1)} %gated.4.own_ref), channel_id=1, source_target_pairs={{0,8},{2,10},{4,12},{6,14},{8,0},{10,2},{12,4},{14,6},{1,9},{3,11}... | collective-permute-start | bytes 294920 | tf_op jit(solution)/shard_map/ppermute | solution.py:21
  75.6 6.8 %collective-permute-start.18 = (bf16[64,768]{1,0:T(8,128)(2,1)S(1)}, bf16[64,768]{1,0:T(8,128)(2,1)S(1)}, u32[]{:S(2)}, u32[]{:S(2)}) collective-permute-start(bf16[64,768]{1,0:T(8,128)(2,1)S(1)} %get-tuple-element.64.own_ref), channel_id=1, source_target_pairs={{0,2},{2,0},{4,6},{6,4},{8,10},{10,8},{12,14},{14,12},{1,3},{3,1},... | collective-permute-start | bytes 294920 | tf_op jit(solution)/shard_map/ppermute | solution.py:21
  80.5 5.6 %collective-permute-start.8 = (bf16[64,768]{1,0:T(8,128)(2,1)S(1)}, bf16[64,768]{1,0:T(8,128)(2,1)S(1)}, u32[]{:S(2)}, u32[]{:S(2)}) collective-permute-start(bf16[64,768]{1,0:T(8,128)(2,1)S(1)} %get-tuple-element.54.own_ref), channel_id=1, source_target_pairs={{0,2},{2,0},{4,6},{6,4},{8,10},{10,8},{12,14},{14,12},{1,3},{3,1},... | collective-permute-start | bytes 294920 | tf_op jit(solution)/shard_map/ppermute | solution.py:21
  82.0 5.7 %collective-permute-start.6 = (bf16[64,768]{1,0:T(8,128)(2,1)S(1)}, bf16[64,768]{1,0:T(8,128)(2,1)S(1)}, u32[]{:S(2)}, u32[]{:S(2)}) collective-permute-start(bf16[64,768]{1,0:T(8,128)(2,1)S(1)} %get-tuple-element.53.own_ref), channel_id=1, source_target_pairs={{0,4},{2,6},{4,0},{6,2},{8,12},{10,14},{12,8},{14,10},{1,5},{3,7},... | collective-permute-start | bytes 294920 | tf_op jit(solution)/shard_map/ppermute | solution.py:21
  83.0 10.2 %collective-permute-start.19 = (bf16[64,1536]{1,0:T(8,128)(2,1)S(1)}, bf16[64,1536]{1,0:T(8,128)(2,1)S(1)}, u32[]{:S(2)}, u32[]{:S(2)}) collective-permute-start(bf16[64,1536]{1,0:T(8,128)(2,1)S(1)} %join.11.rest_1_), channel_id=1, source_target_pairs={{0,4},{2,6},{4,0},{6,2},{8,12},{10,14},{12,8},{14,10},{1,5},{3,7},... | collective-permute-start | bytes 589832 | tf_op jit(solution)/shard_map/ppermute | solution.py:21
  85.3 7.9 %collective-permute-start.17 = (bf16[64,2048]{1,0:T(8,128)(2,1)S(1)}, bf16[64,2048]{1,0:T(8,128)(2,1)S(1)}, u32[]{:S(2)}, u32[]{:S(2)}) collective-permute-start(bf16[64,2048]{1,0:T(8,128)(2,1)S(1)} %join.10.rest_0_), channel_id=1, source_target_pairs={{0,2},{2,0},{4,6},{6,4},{8,10},{10,8},{12,14},{14,12},{1,3},{3,1},... | collective-permute-start | bytes 786440 | tf_op jit(solution)/shard_map/ppermute | solution.py:21
  86.7 14.2 %collective-permute-start.9 = (bf16[64,1536]{1,0:T(8,128)(2,1)S(1)}, bf16[64,1536]{1,0:T(8,128)(2,1)S(1)}, u32[]{:S(2)}, u32[]{:S(2)}) collective-permute-start(bf16[64,1536]{1,0:T(8,128)(2,1)S(1)} %join.9.rest_1_), channel_id=1, source_target_pairs={{0,4},{2,6},{4,0},{6,2},{8,12},{10,14},{12,8},{14,10},{1,5},{3,7},... | collective-permute-start | bytes 589832 | tf_op jit(solution)/shard_map/ppermute | solution.py:21
  88.3 12.6 %collective-permute-start.7 = (bf16[64,1536]{1,0:T(8,128)(2,1)S(1)}, bf16[64,1536]{1,0:T(8,128)(2,1)S(1)}, u32[]{:S(2)}, u32[]{:S(2)}) collective-permute-start(bf16[64,1536]{1,0:T(8,128)(2,1)S(1)} %join.8.rest_0_), channel_id=1, source_target_pairs={{0,2},{2,0},{4,6},{6,4},{8,10},{10,8},{12,14},{14,12},{1,3},{3,1},... | collective-permute-start | bytes 589832 | tf_op jit(solution)/shard_map/ppermute | solution.py:21
  97.2 9.1 %copy-start.1 = (bf16[2,64,1024]{2,1,0:T(8,128)(2,1)S(1)}, bf16[2,64,1024]{2,1,0:T(8,128)(2,1)}, u32[]{:S(2)}) copy-start(bf16[2,64,1024]{2,1,0:T(8,128)(2,1)} %copy-done) | copy-start | bytes 786436
  104.7 1.6 collective-permute-start.20
  110.2 20.2 %collective-permute-start.31 = (bf16[2,64,2048]{2,1,0:T(8,128)(2,1)S(1)}, bf16[2,64,2048]{2,1,0:T(8,128)(2,1)S(1)}, u32[]{:S(2)}, u32[]{:S(2)}) collective-permute-start(bf16[2,64,2048]{2,1,0:T(8,128)(2,1)S(1)} %gate_up.22), channel_id=1, source_target_pairs={{0,2},{2,0},{4,6},{6,4},{8,10},{10,8},{12,14},{14,12},{1,3},{3,1},... | collective-permute-start | bytes 1572872 | tf_op jit(solution)/shard_map/ppermute | solution.py:21
  114.8 18.2 %collective-permute-start.32 = (bf16[2,64,1536]{2,1,0:T(8,128)(2,1)S(1)}, bf16[2,64,1536]{2,1,0:T(8,128)(2,1)S(1)}, u32[]{:S(2)}, u32[]{:S(2)}) collective-permute-start(bf16[2,64,1536]{2,1,0:T(8,128)(2,1)S(1)} %gate_up.23), channel_id=1, source_target_pairs={{0,4},{2,6},{4,0},{6,2},{8,12},{10,14},{12,8},{14,10},{1,5},{3,7},... | collective-permute-start | bytes 1179656 | tf_op jit(solution)/shard_map/ppermute | solution.py:21
  119.1 29.1 %collective-permute-start.22 = (bf16[2,64,1536]{2,1,0:T(8,128)(2,1)S(1)}, bf16[2,64,1536]{2,1,0:T(8,128)(2,1)S(1)}, u32[]{:S(2)}, u32[]{:S(2)}) collective-permute-start(bf16[2,64,1536]{2,1,0:T(8,128)(2,1)S(1)} %gate_up.20), channel_id=1, source_target_pairs={{0,4},{2,6},{4,0},{6,2},{8,12},{10,14},{12,8},{14,10},{1,5},{3,7},... | collective-permute-start | bytes 1179656 | tf_op jit(solution)/shard_map/ppermute | solution.py:21
  123.3 27.2 %collective-permute-start.21 = (bf16[2,64,1536]{2,1,0:T(8,128)(2,1)S(1)}, bf16[2,64,1536]{2,1,0:T(8,128)(2,1)S(1)}, u32[]{:S(2)}, u32[]{:S(2)}) collective-permute-start(bf16[2,64,1536]{2,1,0:T(8,128)(2,1)S(1)} %gate_up.19), channel_id=1, source_target_pairs={{0,2},{2,0},{4,6},{6,4},{8,10},{10,8},{12,14},{14,12},{1,3},{3,1},... | collective-permute-start | bytes 1179656 | tf_op jit(solution)/shard_map/ppermute | solution.py:21
  131.1 8.7 %collective-permute-start.33 = (bf16[2,64,1024]{2,1,0:T(8,128)(2,1)S(1)}, bf16[2,64,1024]{2,1,0:T(8,128)(2,1)S(1)}, u32[]{:S(2)}, u32[]{:S(2)}) collective-permute-start(bf16[2,64,1024]{2,1,0:T(8,128)(2,1)S(1)} %get-tuple-element.79), channel_id=1, source_target_pairs={{0,4},{2,6},{4,0},{6,2},{8,12},{10,14},{12,8},{14,10},{1,5},{3,7},... | collective-permute-start | bytes 786440 | tf_op jit(solution)/shard_map/ppermute | solution.py:21
  133.6 5.7 %collective-permute-start.34 = (bf16[2,64,768]{2,1,0:T(8,128)(2,1)S(1)}, bf16[2,64,768]{2,1,0:T(8,128)(2,1)S(1)}, u32[]{:S(2)}, u32[]{:S(2)}) collective-permute-start(bf16[2,64,768]{2,1,0:T(8,128)(2,1)S(1)} %get-tuple-element.80), channel_id=1, source_target_pairs={{0,2},{2,0},{4,6},{6,4},{8,10},{10,8},{12,14},{14,12},{1,3},{3,1},... | collective-permute-start | bytes 589832 | tf_op jit(solution)/shard_map/ppermute | solution.py:21
  140.4 17.8 %collective-permute-start.35 = (bf16[2,64,896]{2,1,0:T(8,128)(2,1)S(1)}, bf16[2,64,896]{2,1,0:T(8,128)(2,1)S(1)}, u32[]{:S(2)}, u32[]{:S(2)}) collective-permute-start(bf16[2,64,896]{2,1,0:T(8,128)(2,1)S(1)} %get-tuple-element.82), channel_id=1, source_target_pairs={{0,8},{2,10},{4,12},{6,14},{8,0},{10,2},{12,4},{14,6},{1,9},{3,11}... | collective-permute-start | bytes 688136 | tf_op jit(solution)/shard_map/ppermute | solution.py:21
  148.9 5.7 %collective-permute-start.24 = (bf16[2,64,768]{2,1,0:T(8,128)(2,1)S(1)}, bf16[2,64,768]{2,1,0:T(8,128)(2,1)S(1)}, u32[]{:S(2)}, u32[]{:S(2)}) collective-permute-start(bf16[2,64,768]{2,1,0:T(8,128)(2,1)S(1)} %get-tuple-element.70), channel_id=1, source_target_pairs={{0,2},{2,0},{4,6},{6,4},{8,10},{10,8},{12,14},{14,12},{1,3},{3,1},... | collective-permute-start | bytes 589832 | tf_op jit(solution)/shard_map/ppermute | solution.py:21
  151.2 5.8 %collective-permute-start.23 = (bf16[2,64,768]{2,1,0:T(8,128)(2,1)S(1)}, bf16[2,64,768]{2,1,0:T(8,128)(2,1)S(1)}, u32[]{:S(2)}, u32[]{:S(2)}) collective-permute-start(bf16[2,64,768]{2,1,0:T(8,128)(2,1)S(1)} %get-tuple-element.69), channel_id=1, source_target_pairs={{0,4},{2,6},{4,0},{6,2},{8,12},{10,14},{12,8},{14,10},{1,5},{3,7},... | collective-permute-start | bytes 589832 | tf_op jit(solution)/shard_map/ppermute | solution.py:21
  157.6 15.4 %collective-permute-start.25 = (bf16[2,64,768]{2,1,0:T(8,128)(2,1)S(1)}, bf16[2,64,768]{2,1,0:T(8,128)(2,1)S(1)}, u32[]{:S(2)}, u32[]{:S(2)}) collective-permute-start(bf16[2,64,768]{2,1,0:T(8,128)(2,1)S(1)} %get-tuple-element.72), channel_id=1, source_target_pairs={{0,8},{2,10},{4,12},{6,14},{8,0},{10,2},{12,4},{14,6},{1,9},{3,11}... | collective-permute-start | bytes 589832 | tf_op jit(solution)/shard_map/ppermute | solution.py:21
  158.9 13.4 %collective-permute-start.36 = (bf16[64,896]{1,0:T(8,128)(2,1)S(1)}, bf16[64,896]{1,0:T(8,128)(2,1)S(1)}, u32[]{:S(2)}, u32[]{:S(2)}) collective-permute-start(bf16[64,896]{1,0:T(8,128)(2,1)S(1)} %gated.7.own_ref), channel_id=1, source_target_pairs={{0,8},{2,10},{4,12},{6,14},{8,0},{10,2},{12,4},{14,6},{1,9},{3,11}... | collective-permute-start | bytes 344072 | tf_op jit(solution)/shard_map/ppermute | solution.py:21
  172.8 6.3 %collective-permute-start.37 = (bf16[64,1024]{1,0:T(8,128)(2,1)S(1)}, bf16[64,1024]{1,0:T(8,128)(2,1)S(1)}, u32[]{:S(2)}, u32[]{:S(2)}) collective-permute-start(bf16[64,1024]{1,0:T(8,128)(2,1)S(1)} %get-tuple-element.83.own_ref), channel_id=1, source_target_pairs={{0,4},{2,6},{4,0},{6,2},{8,12},{10,14},{12,8},{14,10},{1,5},{3,7},... | collective-permute-start | bytes 393224 | tf_op jit(solution)/shard_map/ppermute | solution.py:21
  173.7 8.7 %collective-permute-start.26 = (bf16[64,768]{1,0:T(8,128)(2,1)S(1)}, bf16[64,768]{1,0:T(8,128)(2,1)S(1)}, u32[]{:S(2)}, u32[]{:S(2)}) collective-permute-start(bf16[64,768]{1,0:T(8,128)(2,1)S(1)} %gated.6.own_ref), channel_id=1, source_target_pairs={{0,8},{2,10},{4,12},{6,14},{8,0},{10,2},{12,4},{14,6},{1,9},{3,11}... | collective-permute-start | bytes 294920 | tf_op jit(solution)/shard_map/ppermute | solution.py:21
  177.1 7.2 %collective-permute-start.39 = (bf16[64,768]{1,0:T(8,128)(2,1)S(1)}, bf16[64,768]{1,0:T(8,128)(2,1)S(1)}, u32[]{:S(2)}, u32[]{:S(2)}) collective-permute-start(bf16[64,768]{1,0:T(8,128)(2,1)S(1)} %get-tuple-element.84.own_ref), channel_id=1, source_target_pairs={{0,2},{2,0},{4,6},{6,4},{8,10},{10,8},{12,14},{14,12},{1,3},{3,1},... | collective-permute-start | bytes 294920 | tf_op jit(solution)/shard_map/ppermute | solution.py:21
  179.7 16.3 %collective-permute-start.38 = (bf16[64,2048]{1,0:T(8,128)(2,1)S(1)}, bf16[64,2048]{1,0:T(8,128)(2,1)S(1)}, u32[]{:S(2)}, u32[]{:S(2)}) collective-permute-start(bf16[64,2048]{1,0:T(8,128)(2,1)S(1)} %join.14.rest_0_), channel_id=1, source_target_pairs={{0,2},{2,0},{4,6},{6,4},{8,10},{10,8},{12,14},{14,12},{1,3},{3,1},... | collective-permute-start | bytes 786440 | tf_op jit(solution)/shard_map/ppermute | solution.py:21
  183.0 6.5 %collective-permute-start.29 = (bf16[64,768]{1,0:T(8,128)(2,1)S(1)}, bf16[64,768]{1,0:T(8,128)(2,1)S(1)}, u32[]{:S(2)}, u32[]{:S(2)}) collective-permute-start(bf16[64,768]{1,0:T(8,128)(2,1)S(1)} %get-tuple-element.74.own_ref), channel_id=1, source_target_pairs={{0,2},{2,0},{4,6},{6,4},{8,10},{10,8},{12,14},{14,12},{1,3},{3,1},... | collective-permute-start | bytes 294920 | tf_op jit(solution)/shard_map/ppermute | solution.py:21
  184.0 6.1 %collective-permute-start.27 = (bf16[64,768]{1,0:T(8,128)(2,1)S(1)}, bf16[64,768]{1,0:T(8,128)(2,1)S(1)}, u32[]{:S(2)}, u32[]{:S(2)}) collective-permute-start(bf16[64,768]{1,0:T(8,128)(2,1)S(1)} %get-tuple-element.73.own_ref), channel_id=1, source_target_pairs={{0,4},{2,6},{4,0},{6,2},{8,12},{10,14},{12,8},{14,10},{1,5},{3,7},... | collective-permute-start | bytes 294920 | tf_op jit(solution)/shard_map/ppermute | solution.py:21
  184.9 11.1 %collective-permute-start.40 = (bf16[64,1536]{1,0:T(8,128)(2,1)S(1)}, bf16[64,1536]{1,0:T(8,128)(2,1)S(1)}, u32[]{:S(2)}, u32[]{:S(2)}) collective-permute-start(bf16[64,1536]{1,0:T(8,128)(2,1)S(1)} %join.15.rest_1_), channel_id=1, source_target_pairs={{0,4},{2,6},{4,0},{6,2},{8,12},{10,14},{12,8},{14,10},{1,5},{3,7},... | collective-permute-start | bytes 589832 | tf_op jit(solution)/shard_map/ppermute | solution.py:21
  190.0 13.7 %collective-permute-start.30 = (bf16[64,1536]{1,0:T(8,128)(2,1)S(1)}, bf16[64,1536]{1,0:T(8,128)(2,1)S(1)}, u32[]{:S(2)}, u32[]{:S(2)}) collective-permute-start(bf16[64,1536]{1,0:T(8,128)(2,1)S(1)} %join.13.rest_1_), channel_id=1, source_target_pairs={{0,4},{2,6},{4,0},{6,2},{8,12},{10,14},{12,8},{14,10},{1,5},{3,7},... | collective-permute-start | bytes 589832 | tf_op jit(solution)/shard_map/ppermute | solution.py:21
  190.7 13.1 %collective-permute-start.28 = (bf16[64,1536]{1,0:T(8,128)(2,1)S(1)}, bf16[64,1536]{1,0:T(8,128)(2,1)S(1)}, u32[]{:S(2)}, u32[]{:S(2)}) collective-permute-start(bf16[64,1536]{1,0:T(8,128)(2,1)S(1)} %join.12.rest_0_), channel_id=1, source_target_pairs={{0,2},{2,0},{4,6},{6,4},{8,10},{10,8},{12,14},{14,12},{1,3},{3,1},... | collective-permute-start | bytes 589832 | tf_op jit(solution)/shard_map/ppermute | solution.py:21
  207.5 1.6 collective-permute-start.41

commit v2 on v0

v2 whole, which is shorter than its diff:
```python
import jax
import jax.numpy as jnp
from jax import lax
from jax.experimental import pallas as pl
from jax.experimental.pallas import tpu as pltpu
from jax.sharding import PartitionSpec as P

BF16 = jnp.bfloat16
F32 = jnp.float32
BLOCK = 512
CHUNKS = ((4, 4), (3, 2))
STREAM_BITS = ((0, 1), (1, 0))
FAR = 2
VMEM = pl.BlockSpec(memory_space=pltpu.VMEM)
ANY = pl.BlockSpec(memory_space=pl.ANY)
HBM = pl.BlockSpec(memory_space=pltpu.HBM)
PARAMS = pltpu.CompilerParams(vmem_limit_bytes=24 * 2**20)


def swap(array, bit):
    return lax.ppermute(array, "gx", [(i, i ^ (1 << bit)) for i in range(8)])


def aligned(index, step):
    return pl.ds(pl.multiple_of(index * step, 128), step)


def device_bit(bit):
    return (lax.axis_index("gx") >> bit) & 1


class Order:
    def __init__(self, first):
        self.last = first

    def call(self, name, kernel, out_shape, in_specs, operands, scratch):
        def ordered(*refs):
            kernel(*refs[: len(operands)], *refs[len(operands) + 1 :])

        out = pl.pallas_call(
            ordered,
            out_shape=out_shape,
            in_specs=in_specs + [ANY],
            out_specs=[VMEM] * len(out_shape),
            scratch_shapes=scratch,
            compiler_params=PARAMS,
            cost_estimate=pl.CostEstimate(flops=0, bytes_accessed=0, transcendentals=0),
            name=name,
        )(*operands, self.last)
        self.last = out[0]
        return list(out)


def shape(dims, dtype):
    return jax.ShapeDtypeStruct(dims, dtype)


def begin_of(rng, i):
    at, n, bit, side = rng
    return at + (device_bit(bit) ^ side) * n + i


def gate_up_copies(gate_ref, up_ref, rng, held_ref, sems):
    def copy(i, which):
        source = (gate_ref, up_ref)[which].at[:, aligned(begin_of(rng, i), BLOCK)]
        return pltpu.make_async_copy(source, held_ref.at[i, which], sems.at[i, which])

    return copy


def down_copies(weight_ref, rng, held_ref, sems):
    def copy(i):
        source = weight_ref.at[aligned(begin_of(rng, i), BLOCK), :]
        return pltpu.make_async_copy(source, held_ref.at[i], sems.at[i])

    return copy


def fetch(order, gate_weight, up_weight, gate_up_ranges, down_weight, down_ranges):
    depth, columns = gate_weight.shape[0], down_weight.shape[1]
    n_gate_up = len(gate_up_ranges)

    def kernel(gate_ref, up_ref, weight_ref, *rest):
        n_out = n_gate_up + len(down_ranges)
        held, sems = rest[:n_out], rest[n_out:]
        copies = []
        for r, rng in enumerate(gate_up_ranges):
            copy = gate_up_copies(gate_ref, up_ref, rng, held[r], sems[r])
            copies += [copy(i, which) for i in range(rng[1]) for which in range(2)]
        for r, rng in enumerate(down_ranges, n_gate_up):
            copy = down_copies(weight_ref, rng, held[r], sems[r])
            copies += [copy(i) for i in range(rng[1])]
        for copy in copies:
            copy.start()
        for copy in copies:
            copy.wait()

    out = order.call(
        "fetch",
        kernel,
        [shape((rng[1], 2, depth, BLOCK), BF16) for rng in gate_up_ranges]
        + [shape((rng[1], BLOCK, columns), BF16) for rng in down_ranges],
        [HBM, HBM, HBM],
        (gate_weight, up_weight, down_weight),
        [pltpu.SemaphoreType.DMA((rng[1], 2)) for rng in gate_up_ranges]
        + [pltpu.SemaphoreType.DMA((rng[1],)) for rng in down_ranges],
    )
    return out[:n_gate_up], out[n_gate_up:]


def gate_up(order, v, gate_weight, up_weight, ranges, out_type, fetched=None):
    rows, depth = v.shape
    counts = [n for _, n, _, _ in ranges]
    blocks = sum(counts)

    def kernel(v_ref, *rest):
        rest = list(rest)
        if fetched is None:
            gate_ref, up_ref = rest[:2]
            out_refs = rest[2 : 2 + len(ranges)]
            scratch_ref, sems = rest[2 + len(ranges) :]
            parts = [pl.ds(sum(counts[:r]), n) for r, n in enumerate(counts)]
            held = [scratch_ref.at[part] for part in parts]
            copies = [
                gate_up_copies(gate_ref, up_ref, rng, h, sems.at[part])
                for rng, h, part in zip(ranges, held, parts)
            ]
            for copy, n in zip(copies, counts):
                for i in range(n):
                    for which in range(2):
                        copy(i, which).start()
        else:
            held, out_refs = rest[: len(ranges)], rest[len(ranges) :]
        for r, n in enumerate(counts):

            @pl.loop(0, n)
            def _(i):
                for which in range(2):
                    if fetched is None:
                        copies[r](i, which).wait()
                    out_refs[r][which, :, aligned(i, BLOCK)] = jnp.dot(
                        v_ref[...], held[r][i, which], preferred_element_type=F32
                    ).astype(out_type)

    if fetched is None:
        operands, specs = (v, gate_weight, up_weight), [VMEM, HBM, HBM]
        scratch = [
            pltpu.VMEM((blocks, 2, depth, BLOCK), BF16),
            pltpu.SemaphoreType.DMA((blocks, 2)),
        ]
    else:
        operands, specs, scratch = (v, *fetched), [VMEM] * (1 + len(fetched)), []
    shapes = [shape((2, rows, n * BLOCK), out_type) for n in counts]
    return order.call("gate_up", kernel, shapes, specs, operands, scratch)


def down(order, total, hiddens, down_weight, ranges, fetched=()):
    rows = hiddens[0].shape[0]
    columns = down_weight.shape[1]
    counts = [n for _, n, _, _ in ranges]
    n_copied = len(ranges) - len(fetched)
    n_held = sum(counts[:n_copied])

    def kernel(*refs):
        refs = list(refs)
        hidden_refs = [refs.pop(0) for _ in ranges]
        total_ref = refs.pop(0) if total is not None else None
        weight_ref = refs.pop(0)
        fetched_refs = [refs.pop(0) for _ in fetched]
        out_ref = refs.pop(0)
        held, copies = [], []
        for r in range(n_copied):
            part = pl.ds(sum(counts[:r]), counts[r])
            held.append(refs[0].at[part])
            copies.append(down_copies(weight_ref, ranges[r], held[r], refs[1].at[part]))
        for copy, n in zip(copies, counts):
            for i in range(n):
                copy(i).start()
        out_ref[...] = jnp.zeros_like(out_ref) if total_ref is None else total_ref[...]
        for r in [*range(n_copied, len(ranges)), *range(n_copied)]:

            @pl.loop(0, counts[r])
            def _(i):
                if r < n_copied:
                    copies[r](i).wait()
                out_ref[...] += jnp.dot(
                    hidden_refs[r][:, aligned(i, BLOCK)],
                    (held + fetched_refs)[r][i],
                    preferred_element_type=F32,
                )

    totals = [] if total is None else [total]
    return order.call(
        "down",
        kernel,
        [shape((rows, columns), F32)],
        [VMEM] * (len(ranges) + len(totals)) + [HBM] + [VMEM] * len(fetched),
        (*hiddens, *totals, down_weight, *fetched),
        [pltpu.VMEM((n_held, BLOCK, columns), BF16), pltpu.SemaphoreType.DMA((n_held,))]
        if n_held
        else [],
    )[0]


def small(order, name, kernel, out_shape, *operands):
    specs = [VMEM] * len(operands)
    return order.call(name, kernel, out_shape, specs, operands, [])


def halve(order, bit, kept, received):
    _, rows, width = kept.shape
    half = width // 2

    def kernel(kept_ref, received_ref, own_ref, send_ref):
        mine, theirs = aligned(device_bit(bit), half), aligned(1 - device_bit(bit), half)
        send_ref[...] = (kept_ref[:, :, theirs] + received_ref[:, :, theirs].astype(F32)).astype(BF16)
        own_ref[...] = kept_ref[:, :, mine] + received_ref[:, :, mine].astype(F32)

    dims = (2, rows, half)
    return small(order, "halve", kernel, [shape(dims, F32), shape(dims, BF16)], kept, received)


def halve_far(order, kepts, receiveds):
    rows = kepts[0].shape[1]
    halves = [k.shape[2] // 2 for k in kepts]

    def kernel(*refs):
        kept_refs, received_refs = refs[: len(halves)], refs[len(halves) : -2]
        own_ref, send_ref = refs[-2:]
        at = 0
        for kept_ref, received_ref, half in zip(kept_refs, received_refs, halves):
            to = slice(at, at + half)
            mine, theirs = aligned(device_bit(FAR), half), aligned(1 - device_bit(FAR), half)
            send_ref[:, :, to] = (
                kept_ref[:, :, theirs] + received_ref[:, :, theirs].astype(F32)
            ).astype(BF16)
            own_ref[:, :, to] = kept_ref[:, :, mine] + received_ref[:, :, mine].astype(F32)
            at += half

    dims = (2, rows, sum(halves))
    shapes = [shape(dims, F32), shape(dims, BF16)]
    return small(order, "halve_far", kernel, shapes, *kepts, *receiveds)


def gated(order, own, received):
    _, rows, width = own.shape

    def kernel(own_ref, received_ref, out_ref):
        gate = own_ref[0] + received_ref[0].astype(F32)
        up = own_ref[1] + received_ref[1].astype(F32)
        out_ref[...] = (gate / (1.0 + jnp.exp(-gate)) * up).astype(BF16)

    return small(order, "gated", kernel, [shape((rows, width), BF16)], own, received)[0]


def join_far(order, own, received, halves):
    rows = own.shape[0]

    def kernel(own_ref, received_ref, *out_refs):
        at = 0
        for out_ref, half in zip(out_refs, halves):
            out_ref[:, aligned(device_bit(FAR), half)] = own_ref[:, at : at + half]
            out_ref[:, aligned(1 - device_bit(FAR), half)] = received_ref[:, at : at + half]
            at += half

    shapes = [shape((rows, 2 * half), BF16) for half in halves]
    return small(order, "join_far", kernel, shapes, own, received)


def join(order, bit, own, received):
    rows, half = own.shape

    def kernel(own_ref, received_ref, out_ref):
        out_ref[:, aligned(device_bit(bit), half)] = own_ref[...]
        out_ref[:, aligned(1 - device_bit(bit), half)] = received_ref[...]

    return small(order, "join", kernel, [shape((rows, 2 * half), BF16)], own, received)[0]


class Chunk:
    def __init__(self, order, at, counts, v, weights):
        self.order, self.counts, self.v, self.weights = order, counts, v, weights
        self.begins = [at + 2 * sum(counts[:s]) for s in range(len(counts))]
        self.received, self.owns, self.others = {}, {}, {}
        self.joined, self.arrived = {}, {}

    def ranges(self, side):
        return [
            (at, n, first, side) for at, n, (first, _) in zip(self.begins, self.counts, STREAM_BITS)
        ]

    def send(self, s, fetched=None):
        held = None if fetched is None else [fetched[s]]
        (sent,) = gate_up(self.order, self.v, *self.weights[:2], [self.ranges(1)[s]], BF16, held)
        self.received[s] = swap(sent, STREAM_BITS[s][0])

    def keep(self):
        self.kept = gate_up(self.order, self.v, *self.weights[:2], self.ranges(0), F32)

    def halve(self, s):
        second = STREAM_BITS[s][1]
        self.owns[s], send = halve(self.order, second, self.kept[s], self.received[s])
        self.others[s] = swap(send, second)

    def halve_far(self):
        self.own, send = halve_far(self.order, [*self.owns.values()], [*self.others.values()])
        self.far = swap(send, FAR)

    def gated(self):
        self.hidden = gated(self.order, self.own, self.far)
        self.far = swap(self.hidden, FAR)

    def join_far(self):
        halves = [128 * n for n in self.counts]
        self.quarters = join_far(self.order, self.hidden, self.far, halves)
        self.others = [swap(q, second) for q, (_, second) in zip(self.quarters, STREAM_BITS)]

    def join(self, s):
        first, second = STREAM_BITS[s]
        self.joined[s] = join(self.order, second, self.quarters[s], self.others[s])
        self.arrived[s] = swap(self.joined[s], first)

    def hiddens(self, side):
        held = self.arrived if side else self.joined
        return [held[s] for s in range(len(self.counts))]


def fast_layer(v, weights, fetched=None, ahead=False):
    order = Order(v)
    a, b = (
        Chunk(order, 2 * sum(map(sum, CHUNKS[:c])), counts, v, weights)
        for c, counts in enumerate(CHUNKS)
    )
    a.send(0, fetched)
    a.send(1, fetched)
    b.send(0)
    b.send(1)
    a.keep()
    a.halve(0)
    a.halve(1)
    b.keep()
    a.halve_far()
    b.halve(0)
    b.halve(1)
    _, b_rows = fetch(order, *weights[:2], [], weights[2], b.ranges(0) + b.ranges(1))
    a.gated()
    b.halve_far()
    next_sends = fetch(order, *weights[:2], a.ranges(1), weights[2], [])[0] if ahead else None
    a.join_far()
    b.gated()
    b.join_far()
    a.join(0)
    a.join(1)
    total = down(order, None, a.hiddens(0), weights[2], a.ranges(0))
    b.join(0)
    b.join(1)
    total = down(order, total, a.hiddens(1), weights[2], a.ranges(1))
    total = down(order, total, b.hiddens(0), weights[2], b.ranges(0), b_rows[:2])
    total = down(order, total, b.hiddens(1), weights[2], b.ranges(1), b_rows[2:])
    return total + lax.ppermute(total, "gy", [(0, 1), (1, 0)]), next_sends


def fast_body(tokens, *weights):
    own_rows = tokens.shape[1]
    gy = lax.axis_index("gy")
    weights = [pltpu.with_memory_space_constraint(w, pltpu.HBM) for w in weights]
    rows = lax.all_gather(tokens, "gy", axis=1, tiled=True)
    first_sum, fetched = fast_layer(rows[0], weights, ahead=True)
    first_out = first_sum.astype(BF16)
    second_input = (rows[1].astype(F32) + first_out.astype(F32)).astype(BF16)
    second_sum, _ = fast_layer(second_input, weights, fetched)
    outs = jnp.stack([first_out, second_sum.astype(BF16)])
    return lax.dynamic_slice_in_dim(outs, gy * own_rows, own_rows, axis=1)


def plain_body(tokens, gate_weight, up_weight, down_weight):
    def layer_apply(local_input):
        row_block = lax.all_gather(local_input, "gy", axis=0, tiled=True)
        batch_rows = row_block.shape[0]
        gate_term = jnp.dot(row_block, gate_weight, preferred_element_type=F32)
        up_term = jnp.dot(row_block, up_weight, preferred_element_type=F32)
        stacked = jnp.concatenate([gate_term, up_term], axis=0)
        summed = lax.psum_scatter(stacked, "gx", scatter_dimension=1, tiled=True)
        hidden_part = (jax.nn.silu(summed[:batch_rows]) * summed[batch_rows:]).astype(BF16)
        partial_out = jnp.dot(
            lax.all_gather(hidden_part, "gx", axis=1, tiled=True),
            down_weight,
            preferred_element_type=F32,
        )
        return lax.psum_scatter(partial_out, "gy", scatter_dimension=0, tiled=True).astype(BF16)

    first_out = layer_apply(tokens[0])
    second_input = (tokens[1].astype(F32) + first_out.astype(F32)).astype(BF16)
    second_out = layer_apply(second_input)
    return jnp.stack([first_out, second_out])


def solution(mesh):
    fast = mesh.shape["gx"] == 8 and mesh.shape["gy"] == 2
    return jax.shard_map(
        fast_body if fast else plain_body,
        mesh=mesh,
        in_specs=(P(None, ("replica", "gy"), "gx"), P("gx", "gy"), P("gx", "gy"), P("gy", "gx")),
        out_specs=P(None, ("replica", "gy"), "gx"),
        check_vma=False,
    )
```

time: 465 us -> 184 us (0.40)
  waiting for transfers between devices: 358 us -> 50.1 us
  Pallas kernels: 0 us -> 82.1 us
  matrix products: 74.6 us -> 0 us
  starting transfers between devices: 0.39 us -> 47.5 us
  between operations: 13.5 us -> 0.58 us
  other arithmetic: 12.9 us -> 0.75 us
    reduce_scatter x4 -> x0, waiting for transfers between devices: 268 us -> none  [the longest x2 255 us: layer_apply(): summed = lax.psum_scatter(stacked, 'gx', scatter_dimension=1, tiled=True)]
    all_gather x2 -> x0, waiting for transfers between devices: 89.6 us -> none  [layer_apply(): lax.all_gather(hidden_part, 'gx', axis=1, tiled=True)]
    pallas_call x0 -> x51, Pallas kernels: none -> 82.1 us  [call(): pl.pallas_call(ordered, out_shape=out_shape, in_specs=in_specs + [ANY], o...]
    dot_general x6 -> x0, matrix products: 74.6 us -> none  [the longest x2 29.6 us: layer_apply(): jnp.dot(lax.all_gather(hidden_part, 'gx', axis=1, tiled=True), down_weigh...]
    ppermute x0 -> x42, waiting for transfers between devices: none -> 50.1 us  [the longest x40 47.1 us: swap(): return lax.ppermute(array, 'gx', [(i, i ^ 1 << bit) for i in range(8)])]
    ppermute x0 -> x42, starting transfers between devices: none -> 47.5 us  [the longest x40 47.3 us: swap(): return lax.ppermute(array, 'gx', [(i, i ^ 1 << bit) for i in range(8)])]
    concatenate x2 -> x0, other arithmetic: 6.52 us -> none  [layer_apply(): stacked = jnp.concatenate([gate_term, up_term], axis=0)]
  transfers between devices with their start and end apart: 6 -> 42, of which waited for: 6 -> 13; matrix products, arithmetic and copies ran while one was open for 0% -> 0% of each run, Pallas kernels for 0% -> 40%
where the time goes in v2:
time: 184 us
  Pallas kernels  82.1 us (45%)
  waiting for transfers between devices  50.1 us (27%)
  starting transfers between devices  47.5 us (26%)
  blocking collectives  2.36 us (1%)
    pallas_call x51, Pallas kernels, call(): pl.pallas_call(ordered, out_shape=out_shape, in_specs=in_specs + [ANY], o...  82.1 us
    ppermute x40, starting transfers between devices, swap(): return lax.ppermute(array, 'gx', [(i, i ^ 1 << bit) for i in range(8)])  47.3 us
    ppermute x40, waiting for transfers between devices, swap(): return lax.ppermute(array, 'gx', [(i, i ^ 1 << bit) for i in range(8)])  47.1 us
  transfers between devices with their start and end apart: 42, of which 13 were waited for; matrix products, arithmetic and copies ran while one was open for 0% of the time, Pallas kernels for 40%

profile of v2, /device:TPU:0, one launch (start us, length us, event | category | flops | bytes accessed | tf_op | source)
XLA Modules:
  0.0 184.1 jit_solution(7945374894067766724)
XLA Ops:
  0.0 2.4 %all_gather.3 = bf16[2,64,1024]{2,1,0:T(8,128)(2,1)S(1)} all-gather(bf16[2,32,1024]{2,1,0:T(8,128)(2,1)} %param.4), channel_id=1, replica_groups=mesh['replica'=2,'gx'=8,'gy'=2] {'gy'}, dimensions={1}, use_global_device_ids=true | all-gather | bytes 393216 | tf_op jit(solution)/shard_map/all_gather | solution.py:367
  2.4 0.7 copy-done
  3.1 3.9 %gate_up.12.refs_3_ = bf16[2,64,2048]{2,1,0:T(8,128)(2,1)S(1)} custom-call(bf16[64,1024]{1,0:T(8,128)(2,1)S(1)} %slice_bitcast_fusion.1.refs_0_.refs_3_, bf16[1024,13312]{1,0:T(8,128)(2,1)} %refs_0_.5, bf16[1024,13312]{1,0:T(8,128)(2,1)} %refs_1_.25, bf16[64,1024]{1,0:T(8,128)(2,1)S(1)} %slice_bitcast_fusion.1.refs_0_.refs_3_), custom_call_target="tpu_custom_call" | custom-call | tf_op jit(solution)/shard_map/gate_up/pallas_call | solution.py:40
  7.0 2.9 %collective-permute-start.1 = (bf16[2,64,2048]{2,1,0:T(8,128)(2,1)S(1)}, bf16[2,64,2048]{2,1,0:T(8,128)(2,1)S(1)}, u32[]{:S(2)}, u32[]{:S(2)}) collective-permute-start(bf16[2,64,2048]{2,1,0:T(8,128)(2,1)S(1)} %gate_up.12.refs_3_), channel_id=1, source_target_pairs={{0,2},{2,0},{4,6},{6,4},{8,10},{10,8},{12,14},{14,12},{1,3},{3,1},... | collective-permute-start | bytes 1572872 | tf_op jit(solution)/shard_map/ppermute | solution.py:21
  9.8 4.0 %gate_up.13.refs_3_ = bf16[2,64,2048]{2,1,0:T(8,128)(2,1)S(1)} custom-call(bf16[64,1024]{1,0:T(8,128)(2,1)S(1)} %slice_bitcast_fusion.1.refs_0_.refs_3_, bf16[1024,13312]{1,0:T(8,128)(2,1)} %refs_0_.5, bf16[1024,13312]{1,0:T(8,128)(2,1)} %refs_1_.25, bf16[2,64,2048]{2,1,0:T(8,128)(2,1)S(1)} %gate_up.12.refs_3_), custom_call_target="tpu_custom_call" | custom-call | tf_op jit(solution)/shard_map/gate_up/pallas_call | solution.py:40
  13.8 1.5 collective-permute-start
  15.3 3.2 %gate_up.14.refs_3_ = bf16[2,64,1536]{2,1,0:T(8,128)(2,1)S(1)} custom-call(bf16[64,1024]{1,0:T(8,128)(2,1)S(1)} %slice_bitcast_fusion.1.refs_0_.refs_3_, bf16[1024,13312]{1,0:T(8,128)(2,1)} %refs_0_.5, bf16[1024,13312]{1,0:T(8,128)(2,1)} %refs_1_.25, bf16[2,64,2048]{2,1,0:T(8,128)(2,1)S(1)} %gate_up.13.refs_3_), custom_call_target="tpu_custom_call" | custom-call | tf_op jit(solution)/shard_map/gate_up/pallas_call | solution.py:40
  18.5 0.7 collective-permute-start.2
  19.2 2.5 %gate_up.15.refs_3_ = bf16[2,64,1024]{2,1,0:T(8,128)(2,1)S(1)} custom-call(bf16[64,1024]{1,0:T(8,128)(2,1)S(1)} %slice_bitcast_fusion.1.refs_0_.refs_3_, bf16[1024,13312]{1,0:T(8,128)(2,1)} %refs_0_.5, bf16[1024,13312]{1,0:T(8,128)(2,1)} %refs_1_.25, bf16[2,64,1536]{2,1,0:T(8,128)(2,1)S(1)} %gate_up.14.refs_3_), custom_call_target="tpu_custom_call" | custom-call | tf_op jit(solution)/shard_map/gate_up/pallas_call | solution.py:40
  21.7 6.4 %gate_up.16 = (f32[2,64,2048]{2,1,0:T(8,128)S(1)}, f32[2,64,2048]{2,1,0:T(8,128)S(1)}) custom-call(bf16[64,1024]{1,0:T(8,128)(2,1)S(1)} %slice_bitcast_fusion.1.refs_0_.refs_3_, bf16[1024,13312]{1,0:T(8,128)(2,1)} %refs_0_.5, bf16[1024,13312]{1,0:T(8,128)(2,1)} %refs_1_.25, bf16[2,64,1024]{2,1,0:T(8,128)(2,1)S(1)} %gate_up.15.refs_3_), custom_call_target="tpu_custom_call" | custom-call | tf_op jit(solution)/shard_map/gate_up/pallas_call | solution.py:40
  28.3 1.6 collective-permute-start.4
  30.4 1.6 collective-permute-start.5
  32.0 4.5 %gate_up.17 = (f32[2,64,1536]{2,1,0:T(8,128)S(1)}, f32[2,64,1024]{2,1,0:T(8,128)S(1)}) custom-call(bf16[64,1024]{1,0:T(8,128)(2,1)S(1)} %slice_bitcast_fusion.1.refs_0_.refs_3_, bf16[1024,13312]{1,0:T(8,128)(2,1)} %refs_0_.5, bf16[1024,13312]{1,0:T(8,128)(2,1)} %refs_1_.25, f32[2,64,1024]{2,1,0:T(8,128)S(1)} %get-tuple-element.58.refs_3_.refs_1_), custom_call_target="tpu_custom_call" | custom-call | tf_op jit(solution)/shard_map/gate_up/pallas_call | solution.py:40
  36.5 5.5 %collective-permute-done.3.refs_2_ = bf16[2,64,1024]{2,1,0:T(8,128)(2,1)S(1)} collective-permute-done((bf16[2,64,1024]{2,1,0:T(8,128)(2,1)S(1)}, bf16[2,64,1024]{2,1,0:T(8,128)(2,1)S(1)}, u32[]{:S(2)}, u32[]{:S(2)}) %collective-permute-start.3) | collective-permute-done | bytes 262176 | tf_op jit(solution)/shard_map/ppermute | solution.py:21
  42.6 5.3 %collective-permute-done.5.refs_1_ = bf16[2,64,1024]{2,1,0:T(8,128)(2,1)S(1)} collective-permute-done((bf16[2,64,1024]{2,1,0:T(8,128)(2,1)S(1)}, bf16[2,64,1024]{2,1,0:T(8,128)(2,1)S(1)}, u32[]{:S(2)}, u32[]{:S(2)}) %collective-permute-start.5) | collective-permute-done | bytes 262176 | tf_op jit(solution)/shard_map/ppermute | solution.py:21
  47.9 2.5 %collective-permute-start.7 = (bf16[2,64,512]{2,1,0:T(8,128)(2,1)S(1)}, bf16[2,64,512]{2,1,0:T(8,128)(2,1)S(1)}, u32[]{:S(2)}, u32[]{:S(2)}) collective-permute-start(bf16[2,64,512]{2,1,0:T(8,128)(2,1)S(1)} %get-tuple-element.67), channel_id=1, source_target_pairs={{0,2},{2,0},{4,6},{6,4},{8,10},{10,8},{12,14},{14,12},{1,3},{3,1},... | collective-permute-start | bytes 393224 | tf_op jit(solution)/shard_map/ppermute | solution.py:21
  50.4 4.1 %fetch.3 = (bf16[3,512,1024]{2,1,0:T(8,128)(2,1)S(1)}, bf16[2,512,1024]{2,1,0:T(8,128)(2,1)S(1)}, bf16[3,512,1024]{2,1,0:T(8,128)(2,1)S(1)}, bf16[2,512,1024]{2,1,0:T(8,128)(2,1)S(1)}) custom-call(bf16[1024,13312]{1,0:T(8,128)(2,1)} %refs_0_.5, bf16[1024,13312]{1,0:T(8,128)(2,1)} %refs_1_.25, bf16[13312,1024]{1,0:T(8,128)(2,1)} %refs_3_.11, ...), custom_call_target="tpu_custom_call" | custom-call | tf_op jit(solution)/shard_map/fetch/pallas_call | solution.py:40
  54.7 1.5 collective-permute-start.9
  56.3 1.5 collective-permute-start.10
  57.7 6.1 %fetch.4 = (bf16[4,2,1024,512]{3,2,1,0:T(8,128)(2,1)S(1)}, bf16[4,2,1024,512]{3,2,1,0:T(8,128)(2,1)S(1)}) custom-call(bf16[1024,13312]{1,0:T(8,128)(2,1)} %refs_0_.5, bf16[1024,13312]{1,0:T(8,128)(2,1)} %refs_1_.25, bf16[13312,1024]{1,0:T(8,128)(2,1)} %refs_3_.11, f32[2,64,640]{2,1,0:T(8,128)S(1)} %get-tuple-element.70.refs_3_.refs_0_), custom_call_target="tpu_custom_call" | custom-call | tf_op jit(solution)/shard_map/fetch/pallas_call | solution.py:40
  63.8 3.0 %collective-permute-done.10.refs_1_ = bf16[64,1024]{1,0:T(8,128)(2,1)S(1)} collective-permute-done((bf16[64,1024]{1,0:T(8,128)(2,1)S(1)}, bf16[64,1024]{1,0:T(8,128)(2,1)S(1)}, u32[]{:S(2)}, u32[]{:S(2)}) %collective-permute-start.10) | collective-permute-done | bytes 131104 | tf_op jit(solution)/shard_map/ppermute | solution.py:21
  66.9 0.9 collective-permute-start.14
  67.9 3.4 %collective-permute-start.11 = (bf16[64,640]{1,0:T(8,128)(2,1)S(1)}, bf16[64,640]{1,0:T(8,128)(2,1)S(1)}, u32[]{:S(2)}, u32[]{:S(2)}) collective-permute-start(bf16[64,640]{1,0:T(8,128)(2,1)S(1)} %gated.5.refs_0_.refs_2_), channel_id=1, source_target_pairs={{0,8},{2,10},{4,12},{6,14},{8,0},{10,2},{12,4},{14,6},{1,9},{3,11}... | collective-permute-start | bytes 245768 | tf_op jit(solution)/shard_map/ppermute | solution.py:21
  71.3 2.4 %collective-permute-done.11.refs_1_ = bf16[64,640]{1,0:T(8,128)(2,1)S(1)} collective-permute-done((bf16[64,640]{1,0:T(8,128)(2,1)S(1)}, bf16[64,640]{1,0:T(8,128)(2,1)S(1)}, u32[]{:S(2)}, u32[]{:S(2)}) %collective-permute-start.11) | collective-permute-done | bytes 81952 | tf_op jit(solution)/shard_map/ppermute | solution.py:21
  73.8 1.5 collective-permute-start.12
  76.0 1.2 collective-permute-start.18
  77.2 0.8 collective-permute-start.16
  78.1 3.8 %down.8.refs_2_ = f32[64,1024]{1,0:T(8,128)S(1)} custom-call(bf16[64,2048]{1,0:T(8,128)(2,1)S(1)} %join.8.refs_2_.refs_0_, bf16[64,2048]{1,0:T(8,128)(2,1)S(1)} %join.9.refs_1_.refs_3_, bf16[13312,1024]{1,0:T(8,128)(2,1)} %refs_3_.11, bf16[64,2048]{1,0:T(8,128)(2,1)S(1)} %join.9.refs_1_.refs_3_), custom_call_target="tpu_custom_call" | custom-call | tf_op jit(solution)/shard_map/down/pallas_call | solution.py:40
  81.9 1.2 collective-permute-start.15
  83.2 2.4 %collective-permute-done.16.refs_1_ = bf16[64,512]{1,0:T(8,128)(2,1)S(1)} collective-permute-done((bf16[64,512]{1,0:T(8,128)(2,1)S(1)}, bf16[64,512]{1,0:T(8,128)(2,1)S(1)}, u32[]{:S(2)}, u32[]{:S(2)}) %collective-permute-start.16) | collective-permute-done | bytes 65568 | tf_op jit(solution)/shard_map/ppermute | solution.py:21
  86.2 3.8 %down.9.refs_2_.refs_6_ = f32[64,1024]{1,0:T(8,128)S(1)} custom-call(bf16[64,2048]{1,0:T(8,128)(2,1)S(1)} %collective-permute-done.18.refs_0_, bf16[64,2048]{1,0:T(8,128)(2,1)S(1)} %collective-permute-done.19.refs_1_, f32[64,1024]{1,0:T(8,128)S(1)} %down.8.refs_2_, bf16[13312,1024]{1,0:T(8,128)(2,1)} %refs_3_.11, bf16[64,1024]{1,0:T(8,128)(2,1)S(1)} %join.11.refs_4_.refs_1_), custom_call_target="tpu_custom_call" | custom-call | tf_op jit(solution)/shard_map/down/pallas_call | solution.py:40
  90.0 1.5 down.10.refs_2_.refs_6_
  91.6 1.5 down.11
  93.2 1.5 collective-permute-done.20
  94.8 1.9 %gate_up.18.refs_2_ = bf16[2,64,2048]{2,1,0:T(8,128)(2,1)S(1)} custom-call(bf16[64,1024]{1,0:T(8,128)(2,1)S(1)} %get-tuple-element.105.refs_0_.refs_2_, bf16[4,2,1024,512]{3,2,1,0:T(8,128)(2,1)S(1)} %get-tuple-element.72.refs_2_.refs_1_, bf16[64,1024]{1,0:T(8,128)(2,1)S(1)} %get-tuple-element.105.refs_0_.refs_2_), custom_call_target="tpu_custom_call" | custom-call | tf_op jit(solution)/shard_map/gate_up/pallas_call | solution.py:40
  96.7 1.7 collective-permute-start.22
  98.4 1.9 %gate_up.19.refs_3_ = bf16[2,64,2048]{2,1,0:T(8,128)(2,1)S(1)} custom-call(bf16[64,1024]{1,0:T(8,128)(2,1)S(1)} %get-tuple-element.105.refs_0_.refs_2_, bf16[4,2,1024,512]{3,2,1,0:T(8,128)(2,1)S(1)} %get-tuple-element.80.refs_1_, bf16[2,64,2048]{2,1,0:T(8,128)(2,1)S(1)} %gate_up.18.refs_2_), custom_call_target="tpu_custom_call" | custom-call | tf_op jit(solution)/shard_map/gate_up/pallas_call | solution.py:40
  100.8 3.2 %gate_up.20.refs_3_ = bf16[2,64,1536]{2,1,0:T(8,128)(2,1)S(1)} custom-call(bf16[64,1024]{1,0:T(8,128)(2,1)S(1)} %get-tuple-element.105.refs_0_.refs_2_, bf16[1024,13312]{1,0:T(8,128)(2,1)} %refs_0_.5, bf16[1024,13312]{1,0:T(8,128)(2,1)} %refs_1_.25, bf16[2,64,2048]{2,1,0:T(8,128)(2,1)S(1)} %gate_up.19.refs_3_), custom_call_target="tpu_custom_call" | custom-call | tf_op jit(solution)/shard_map/gate_up/pallas_call | solution.py:40
  104.0 1.5 collective-permute-start.23
  105.5 2.5 %gate_up.21.refs_3_ = bf16[2,64,1024]{2,1,0:T(8,128)(2,1)S(1)} custom-call(bf16[64,1024]{1,0:T(8,128)(2,1)S(1)} %get-tuple-element.105.refs_0_.refs_2_, bf16[1024,13312]{1,0:T(8,128)(2,1)} %refs_0_.5, bf16[1024,13312]{1,0:T(8,128)(2,1)} %refs_1_.25, bf16[2,64,1536]{2,1,0:T(8,128)(2,1)S(1)} %gate_up.20.refs_3_), custom_call_target="tpu_custom_call" | custom-call | tf_op jit(solution)/shard_map/gate_up/pallas_call | solution.py:40
  108.0 6.4 %gate_up.22 = (f32[2,64,2048]{2,1,0:T(8,128)S(1)}, f32[2,64,2048]{2,1,0:T(8,128)S(1)}) custom-call(bf16[64,1024]{1,0:T(8,128)(2,1)S(1)} %get-tuple-element.105.refs_0_.refs_2_, bf16[1024,13312]{1,0:T(8,128)(2,1)} %refs_0_.5, bf16[1024,13312]{1,0:T(8,128)(2,1)} %refs_1_.25, bf16[2,64,1024]{2,1,0:T(8,128)(2,1)S(1)} %gate_up.21.refs_3_), custom_call_target="tpu_custom_call" | custom-call | tf_op jit(solution)/shard_map/gate_up/pallas_call | solution.py:40
  114.6 0.8 collective-permute-start.25
  115.4 1.5 collective-permute-start.24
  117.5 4.5 %gate_up.23 = (f32[2,64,1536]{2,1,0:T(8,128)S(1)}, f32[2,64,1024]{2,1,0:T(8,128)S(1)}) custom-call(bf16[64,1024]{1,0:T(8,128)(2,1)S(1)} %get-tuple-element.105.refs_0_.refs_2_, bf16[1024,13312]{1,0:T(8,128)(2,1)} %refs_0_.5, bf16[1024,13312]{1,0:T(8,128)(2,1)} %refs_1_.25, f32[2,64,1024]{2,1,0:T(8,128)S(1)} %get-tuple-element.84.refs_3_.refs_1_), custom_call_target="tpu_custom_call" | custom-call | tf_op jit(solution)/shard_map/gate_up/pallas_call | solution.py:40
  122.0 2.7 %collective-permute-done.25.refs_3_ = bf16[2,64,1024]{2,1,0:T(8,128)(2,1)S(1)} collective-permute-done((bf16[2,64,1024]{2,1,0:T(8,128)(2,1)S(1)}, bf16[2,64,1024]{2,1,0:T(8,128)(2,1)S(1)}, u32[]{:S(2)}, u32[]{:S(2)}) %collective-permute-start.25) | collective-permute-done | bytes 262176 | tf_op jit(solution)/shard_map/ppermute | solution.py:21
  124.9 2.1 %collective-permute-start.29 = (bf16[2,64,1024]{2,1,0:T(8,128)(2,1)S(1)}, bf16[2,64,1024]{2,1,0:T(8,128)(2,1)S(1)}, u32[]{:S(2)}, u32[]{:S(2)}) collective-permute-start(bf16[2,64,1024]{2,1,0:T(8,128)(2,1)S(1)} %get-tuple-element.94), channel_id=1, source_target_pairs={{0,8},{2,10},{4,12},{6,14},{8,0},{10,2},{12,4},{14,6},{1,9},{3,11}... | collective-permute-start | bytes 786440 | tf_op jit(solution)/shard_map/ppermute | solution.py:21
  127.1 2.1 %collective-permute-start.27 = (bf16[2,64,768]{2,1,0:T(8,128)(2,1)S(1)}, bf16[2,64,768]{2,1,0:T(8,128)(2,1)S(1)}, u32[]{:S(2)}, u32[]{:S(2)}) collective-permute-start(bf16[2,64,768]{2,1,0:T(8,128)(2,1)S(1)} %get-tuple-element.92), channel_id=1, source_target_pairs={{0,4},{2,6},{4,0},{6,2},{8,12},{10,14},{12,8},{14,10},{1,5},{3,7},... | collective-permute-start | bytes 589832 | tf_op jit(solution)/shard_map/ppermute | solution.py:21
  129.1 1.3 collective-permute-done.26.refs_1_
  130.5 4.1 %fetch.5 = (bf16[3,512,1024]{2,1,0:T(8,128)(2,1)S(1)}, bf16[2,512,1024]{2,1,0:T(8,128)(2,1)S(1)}, bf16[3,512,1024]{2,1,0:T(8,128)(2,1)S(1)}, bf16[2,512,1024]{2,1,0:T(8,128)(2,1)S(1)}) custom-call(bf16[1024,13312]{1,0:T(8,128)(2,1)} %refs_0_.5, bf16[1024,13312]{1,0:T(8,128)(2,1)} %refs_1_.25, bf16[13312,1024]{1,0:T(8,128)(2,1)} %refs_3_.11, ...), custom_call_target="tpu_custom_call" | custom-call | tf_op jit(solution)/shard_map/fetch/pallas_call | solution.py:40
  134.7 4.3 %collective-permute-done.29.refs_1_ = bf16[2,64,1024]{2,1,0:T(8,128)(2,1)S(1)} collective-permute-done((bf16[2,64,1024]{2,1,0:T(8,128)(2,1)S(1)}, bf16[2,64,1024]{2,1,0:T(8,128)(2,1)S(1)}, u32[]{:S(2)}, u32[]{:S(2)}) %collective-permute-start.29) | collective-permute-done | bytes 262176 | tf_op jit(solution)/shard_map/ppermute | solution.py:21
  139.2 1.4 collective-permute-start.30
  140.6 1.6 collective-permute-start.31
  142.2 12.0 %collective-permute-done.31.refs_1_ = bf16[64,1024]{1,0:T(8,128)(2,1)S(1)} collective-permute-done((bf16[64,1024]{1,0:T(8,128)(2,1)S(1)}, bf16[64,1024]{1,0:T(8,128)(2,1)S(1)}, u32[]{:S(2)}, u32[]{:S(2)}) %collective-permute-start.31) | collective-permute-done | bytes 131104 | tf_op jit(solution)/shard_map/ppermute | solution.py:21
  154.3 1.9 %collective-permute-start.35 = (bf16[64,1024]{1,0:T(8,128)(2,1)S(1)}, bf16[64,1024]{1,0:T(8,128)(2,1)S(1)}, u32[]{:S(2)}, u32[]{:S(2)}) collective-permute-start(bf16[64,1024]{1,0:T(8,128)(2,1)S(1)} %get-tuple-element.100.refs_0_), channel_id=1, source_target_pairs={{0,2},{2,0},{4,6},{6,4},{8,10},{10,8},{12,14},{14,12},{1,3},{3,1},... | collective-permute-start | bytes 393224 | tf_op jit(solution)/shard_map/ppermute | solution.py:21
  156.2 2.0 %collective-permute-start.32 = (bf16[64,640]{1,0:T(8,128)(2,1)S(1)}, bf16[64,640]{1,0:T(8,128)(2,1)S(1)}, u32[]{:S(2)}, u32[]{:S(2)}) collective-permute-start(bf16[64,640]{1,0:T(8,128)(2,1)S(1)} %gated.7.refs_0_.refs_2_), channel_id=1, source_target_pairs={{0,8},{2,10},{4,12},{6,14},{8,0},{10,2},{12,4},{14,6},{1,9},{3,11}... | collective-permute-start | bytes 245768 | tf_op jit(solution)/shard_map/ppermute | solution.py:21
  158.2 5.2 %collective-permute-done.32.refs_1_ = bf16[64,640]{1,0:T(8,128)(2,1)S(1)} collective-permute-done((bf16[64,640]{1,0:T(8,128)(2,1)S(1)}, bf16[64,640]{1,0:T(8,128)(2,1)S(1)}, u32[]{:S(2)}, u32[]{:S(2)}) %collective-permute-start.32) | collective-permute-done | bytes 81952 | tf_op jit(solution)/shard_map/ppermute | solution.py:21
  163.9 1.8 collective-permute-start.40
  165.9 1.7 collective-permute-start.37
  167.7 3.8 %down.12.refs_2_ = f32[64,1024]{1,0:T(8,128)S(1)} custom-call(bf16[64,2048]{1,0:T(8,128)(2,1)S(1)} %join.12.refs_2_.refs_0_, bf16[64,2048]{1,0:T(8,128)(2,1)S(1)} %join.13.refs_1_.refs_3_, bf16[13312,1024]{1,0:T(8,128)(2,1)} %refs_3_.11, bf16[64,2048]{1,0:T(8,128)(2,1)S(1)} %join.13.refs_1_.refs_3_), custom_call_target="tpu_custom_call" | custom-call | tf_op jit(solution)/shard_map/down/pallas_call | solution.py:40
  171.8 3.0 %collective-permute-done.37.refs_1_ = bf16[64,512]{1,0:T(8,128)(2,1)S(1)} collective-permute-done((bf16[64,512]{1,0:T(8,128)(2,1)S(1)}, bf16[64,512]{1,0:T(8,128)(2,1)S(1)}, u32[]{:S(2)}, u32[]{:S(2)}) %collective-permute-start.37) | collective-permute-done | bytes 65568 | tf_op jit(solution)/shard_map/ppermute | solution.py:21
  175.0 3.8 %down.13.refs_2_.refs_6_ = f32[64,1024]{1,0:T(8,128)S(1)} custom-call(bf16[64,2048]{1,0:T(8,128)(2,1)S(1)} %collective-permute-done.39.refs_0_, bf16[64,2048]{1,0:T(8,128)(2,1)S(1)} %collective-permute-done.40.refs_1_, f32[64,1024]{1,0:T(8,128)S(1)} %down.12.refs_2_, bf16[13312,1024]{1,0:T(8,128)(2,1)} %refs_3_.11, bf16[64,1024]{1,0:T(8,128)(2,1)S(1)} %join.15.refs_4_.refs_1_), custom_call_target="tpu_custom_call" | custom-call | tf_op jit(solution)/shard_map/down/pallas_call | solution.py:40
  178.8 1.5 down.14.refs_2_.refs_6_
  180.3 1.5 down.15
  181.9 1.5 collective-permute-done.41
  (80 shorter events, 7.1 us)
Async XLA Ops:
  2.4 0.7 copy-start
  7.0 21.1 %collective-permute-start.1 = (bf16[2,64,2048]{2,1,0:T(8,128)(2,1)S(1)}, bf16[2,64,2048]{2,1,0:T(8,128)(2,1)S(1)}, u32[]{:S(2)}, u32[]{:S(2)}) collective-permute-start(bf16[2,64,2048]{2,1,0:T(8,128)(2,1)S(1)} %gate_up.12.refs_3_), channel_id=1, source_target_pairs={{0,2},{2,0},{4,6},{6,4},{8,10},{10,8},{12,14},{14,12},{1,3},{3,1},... | collective-permute-start | bytes 1572872 | tf_op jit(solution)/shard_map/ppermute | solution.py:21
  13.8 14.4 %collective-permute-start = (bf16[2,64,2048]{2,1,0:T(8,128)(2,1)S(1)}, bf16[2,64,2048]{2,1,0:T(8,128)(2,1)S(1)}, u32[]{:S(2)}, u32[]{:S(2)}) collective-permute-start(bf16[2,64,2048]{2,1,0:T(8,128)(2,1)S(1)} %gate_up.13.refs_3_), channel_id=1, source_target_pairs={{0,4},{2,6},{4,0},{6,2},{8,12},{10,14},{12,8},{14,10},{1,5},{3,7},... | collective-permute-start | bytes 1572872 | tf_op jit(solution)/shard_map/ppermute | solution.py:21
  18.5 23.7 %collective-permute-start.2 = (bf16[2,64,1536]{2,1,0:T(8,128)(2,1)S(1)}, bf16[2,64,1536]{2,1,0:T(8,128)(2,1)S(1)}, u32[]{:S(2)}, u32[]{:S(2)}) collective-permute-start(bf16[2,64,1536]{2,1,0:T(8,128)(2,1)S(1)} %gate_up.14.refs_3_), channel_id=1, source_target_pairs={{0,2},{2,0},{4,6},{6,4},{8,10},{10,8},{12,14},{14,12},{1,3},{3,1},... | collective-permute-start | bytes 1179656 | tf_op jit(solution)/shard_map/ppermute | solution.py:21
  28.3 8.2 %collective-permute-start.4 = (bf16[2,64,1024]{2,1,0:T(8,128)(2,1)S(1)}, bf16[2,64,1024]{2,1,0:T(8,128)(2,1)S(1)}, u32[]{:S(2)}, u32[]{:S(2)}) collective-permute-start(bf16[2,64,1024]{2,1,0:T(8,128)(2,1)S(1)} %get-tuple-element.61), channel_id=1, source_target_pairs={{0,2},{2,0},{4,6},{6,4},{8,10},{10,8},{12,14},{14,12},{1,3},{3,1},... | collective-permute-start | bytes 786440 | tf_op jit(solution)/shard_map/ppermute | solution.py:21
  30.0 12.1 %collective-permute-start.3 = (bf16[2,64,1024]{2,1,0:T(8,128)(2,1)S(1)}, bf16[2,64,1024]{2,1,0:T(8,128)(2,1)S(1)}, u32[]{:S(2)}, u32[]{:S(2)}) collective-permute-start(bf16[2,64,1024]{2,1,0:T(8,128)(2,1)S(1)} %get-tuple-element.60), channel_id=1, source_target_pairs={{0,4},{2,6},{4,0},{6,2},{8,12},{10,14},{12,8},{14,10},{1,5},{3,7},... | collective-permute-start | bytes 786440 | tf_op jit(solution)/shard_map/ppermute | solution.py:21
  30.4 17.4 %collective-permute-start.5 = (bf16[2,64,1024]{2,1,0:T(8,128)(2,1)S(1)}, bf16[2,64,1024]{2,1,0:T(8,128)(2,1)S(1)}, u32[]{:S(2)}, u32[]{:S(2)}) collective-permute-start(bf16[2,64,1024]{2,1,0:T(8,128)(2,1)S(1)} %gate_up.15.refs_3_), channel_id=1, source_target_pairs={{0,4},{2,6},{4,0},{6,2},{8,12},{10,14},{12,8},{14,10},{1,5},{3,7},... | collective-permute-start | bytes 786440 | tf_op jit(solution)/shard_map/ppermute | solution.py:21
  42.1 12.4 %collective-permute-start.8 = (bf16[2,64,1024]{2,1,0:T(8,128)(2,1)S(1)}, bf16[2,64,1024]{2,1,0:T(8,128)(2,1)S(1)}, u32[]{:S(2)}, u32[]{:S(2)}) collective-permute-start(bf16[2,64,1024]{2,1,0:T(8,128)(2,1)S(1)} %get-tuple-element.68), channel_id=1, source_target_pairs={{0,8},{2,10},{4,12},{6,14},{8,0},{10,2},{12,4},{14,6},{1,9},{3,11}... | collective-permute-start | bytes 786440 | tf_op jit(solution)/shard_map/ppermute | solution.py:21
  42.3 12.3 %collective-permute-start.6 = (bf16[2,64,768]{2,1,0:T(8,128)(2,1)S(1)}, bf16[2,64,768]{2,1,0:T(8,128)(2,1)S(1)}, u32[]{:S(2)}, u32[]{:S(2)}) collective-permute-start(bf16[2,64,768]{2,1,0:T(8,128)(2,1)S(1)} %get-tuple-element.66), channel_id=1, source_target_pairs={{0,4},{2,6},{4,0},{6,2},{8,12},{10,14},{12,8},{14,10},{1,5},{3,7},... | collective-permute-start | bytes 589832 | tf_op jit(solution)/shard_map/ppermute | solution.py:21
  47.9 6.7 %collective-permute-start.7 = (bf16[2,64,512]{2,1,0:T(8,128)(2,1)S(1)}, bf16[2,64,512]{2,1,0:T(8,128)(2,1)S(1)}, u32[]{:S(2)}, u32[]{:S(2)}) collective-permute-start(bf16[2,64,512]{2,1,0:T(8,128)(2,1)S(1)} %get-tuple-element.67), channel_id=1, source_target_pairs={{0,2},{2,0},{4,6},{6,4},{8,10},{10,8},{12,14},{14,12},{1,3},{3,1},... | collective-permute-start | bytes 393224 | tf_op jit(solution)/shard_map/ppermute | solution.py:21
  54.7 13.1 %collective-permute-start.9 = (bf16[2,64,640]{2,1,0:T(8,128)(2,1)S(1)}, bf16[2,64,640]{2,1,0:T(8,128)(2,1)S(1)}, u32[]{:S(2)}, u32[]{:S(2)}) collective-permute-start(bf16[2,64,640]{2,1,0:T(8,128)(2,1)S(1)} %get-tuple-element.71), channel_id=1, source_target_pairs={{0,8},{2,10},{4,12},{6,14},{8,0},{10,2},{12,4},{14,6},{1,9},{3,11}... | collective-permute-start | bytes 491528 | tf_op jit(solution)/shard_map/ppermute | solution.py:21
  56.3 10.5 %collective-permute-start.10 = (bf16[64,1024]{1,0:T(8,128)(2,1)S(1)}, bf16[64,1024]{1,0:T(8,128)(2,1)S(1)}, u32[]{:S(2)}, u32[]{:S(2)}) collective-permute-start(bf16[64,1024]{1,0:T(8,128)(2,1)S(1)} %gated.4.refs_4_.refs_0_), channel_id=1, source_target_pairs={{0,8},{2,10},{4,12},{6,14},{8,0},{10,2},{12,4},{14,6},{1,9},{3,11}... | collective-permute-start | bytes 393224 | tf_op jit(solution)/shard_map/ppermute | solution.py:21
  66.8 8.5 %collective-permute-start.13 = (bf16[64,1024]{1,0:T(8,128)(2,1)S(1)}, bf16[64,1024]{1,0:T(8,128)(2,1)S(1)}, u32[]{:S(2)}, u32[]{:S(2)}) collective-permute-start(bf16[64,1024]{1,0:T(8,128)(2,1)S(1)} %get-tuple-element.73.refs_2_.refs_0_), channel_id=1, source_target_pairs={{0,4},{2,6},{4,0},{6,2},{8,12},{10,14},{12,8},{14,10},{1,5},{3,7},... | collective-permute-start | bytes 393224 | tf_op jit(solution)/shard_map/ppermute | solution.py:21
  66.9 8.4 %collective-permute-start.14 = (bf16[64,1024]{1,0:T(8,128)(2,1)S(1)}, bf16[64,1024]{1,0:T(8,128)(2,1)S(1)}, u32[]{:S(2)}, u32[]{:S(2)}) collective-permute-start(bf16[64,1024]{1,0:T(8,128)(2,1)S(1)} %get-tuple-element.75.refs_0_), channel_id=1, source_target_pairs={{0,2},{2,0},{4,6},{6,4},{8,10},{10,8},{12,14},{14,12},{1,3},{3,1},... | collective-permute-start | bytes 393224 | tf_op jit(solution)/shard_map/ppermute | solution.py:21
  67.9 5.9 %collective-permute-start.11 = (bf16[64,640]{1,0:T(8,128)(2,1)S(1)}, bf16[64,640]{1,0:T(8,128)(2,1)S(1)}, u32[]{:S(2)}, u32[]{:S(2)}) collective-permute-start(bf16[64,640]{1,0:T(8,128)(2,1)S(1)} %gated.5.refs_0_.refs_2_), channel_id=1, source_target_pairs={{0,8},{2,10},{4,12},{6,14},{8,0},{10,2},{12,4},{14,6},{1,9},{3,11}... | collective-permute-start | bytes 245768 | tf_op jit(solution)/shard_map/ppermute | solution.py:21
  73.8 8.1 %collective-permute-start.12 = (bf16[64,768]{1,0:T(8,128)(2,1)S(1)}, bf16[64,768]{1,0:T(8,128)(2,1)S(1)}, u32[]{:S(2)}, u32[]{:S(2)}) collective-permute-start(bf16[64,768]{1,0:T(8,128)(2,1)S(1)} %get-tuple-element.74.refs_2_.refs_0_), channel_id=1, source_target_pairs={{0,4},{2,6},{4,0},{6,2},{8,12},{10,14},{12,8},{14,10},{1,5},{3,7},... | collective-permute-start | bytes 294920 | tf_op jit(solution)/shard_map/ppermute | solution.py:21
  75.4 10.8 %collective-permute-start.19 = (bf16[64,2048]{1,0:T(8,128)(2,1)S(1)}, bf16[64,2048]{1,0:T(8,128)(2,1)S(1)}, u32[]{:S(2)}, u32[]{:S(2)}) collective-permute-start(bf16[64,2048]{1,0:T(8,128)(2,1)S(1)} %join.9.refs_1_.refs_3_), channel_id=1, source_target_pairs={{0,4},{2,6},{4,0},{6,2},{8,12},{10,14},{12,8},{14,10},{1,5},{3,7},... | collective-permute-start | bytes 786440 | tf_op jit(solution)/shard_map/ppermute | solution.py:21
  76.0 10.2 %collective-permute-start.18 = (bf16[64,2048]{1,0:T(8,128)(2,1)S(1)}, bf16[64,2048]{1,0:T(8,128)(2,1)S(1)}, u32[]{:S(2)}, u32[]{:S(2)}) collective-permute-start(bf16[64,2048]{1,0:T(8,128)(2,1)S(1)} %join.8.refs_2_.refs_0_), channel_id=1, source_target_pairs={{0,2},{2,0},{4,6},{6,4},{8,10},{10,8},{12,14},{14,12},{1,3},{3,1},... | collective-permute-start | bytes 786440 | tf_op jit(solution)/shard_map/ppermute | solution.py:21
  77.2 8.3 %collective-permute-start.16 = (bf16[64,512]{1,0:T(8,128)(2,1)S(1)}, bf16[64,512]{1,0:T(8,128)(2,1)S(1)}, u32[]{:S(2)}, u32[]{:S(2)}) collective-permute-start(bf16[64,512]{1,0:T(8,128)(2,1)S(1)} %get-tuple-element.76.refs_0_), channel_id=1, source_target_pairs={{0,2},{2,0},{4,6},{6,4},{8,10},{10,8},{12,14},{14,12},{1,3},{3,1},... | collective-permute-start | bytes 196616 | tf_op jit(solution)/shard_map/ppermute | solution.py:21
  81.9 9.7 %collective-permute-start.15 = (bf16[64,1536]{1,0:T(8,128)(2,1)S(1)}, bf16[64,1536]{1,0:T(8,128)(2,1)S(1)}, u32[]{:S(2)}, u32[]{:S(2)}) collective-permute-start(bf16[64,1536]{1,0:T(8,128)(2,1)S(1)} %join.10.refs_2_.refs_0_), channel_id=1, source_target_pairs={{0,2},{2,0},{4,6},{6,4},{8,10},{10,8},{12,14},{14,12},{1,3},{3,1},... | collective-permute-start | bytes 589832 | tf_op jit(solution)/shard_map/ppermute | solution.py:21
  85.6 6.0 %collective-permute-start.17 = (bf16[64,1024]{1,0:T(8,128)(2,1)S(1)}, bf16[64,1024]{1,0:T(8,128)(2,1)S(1)}, u32[]{:S(2)}, u32[]{:S(2)}) collective-permute-start(bf16[64,1024]{1,0:T(8,128)(2,1)S(1)} %join.11.refs_4_.refs_1_), channel_id=1, source_target_pairs={{0,4},{2,6},{4,0},{6,2},{8,12},{10,14},{12,8},{14,10},{1,5},{3,7},... | collective-permute-start | bytes 393224 | tf_op jit(solution)/shard_map/ppermute | solution.py:21
  91.6 3.1 %copy-start.1 = (bf16[2,64,1024]{2,1,0:T(8,128)(2,1)S(1)}, bf16[2,64,1024]{2,1,0:T(8,128)(2,1)}, u32[]{:S(2)}) copy-start(bf16[2,64,1024]{2,1,0:T(8,128)(2,1)} %copy-done) | copy-start | bytes 786436
  93.1 1.6 collective-permute-start.20
  96.7 17.7 %collective-permute-start.22 = (bf16[2,64,2048]{2,1,0:T(8,128)(2,1)S(1)}, bf16[2,64,2048]{2,1,0:T(8,128)(2,1)S(1)}, u32[]{:S(2)}, u32[]{:S(2)}) collective-permute-start(bf16[2,64,2048]{2,1,0:T(8,128)(2,1)S(1)} %gate_up.18.refs_2_), channel_id=1, source_target_pairs={{0,2},{2,0},{4,6},{6,4},{8,10},{10,8},{12,14},{14,12},{1,3},{3,1},... | collective-permute-start | bytes 1572872 | tf_op jit(solution)/shard_map/ppermute | solution.py:21
  100.4 14.2 %collective-permute-start.21 = (bf16[2,64,2048]{2,1,0:T(8,128)(2,1)S(1)}, bf16[2,64,2048]{2,1,0:T(8,128)(2,1)S(1)}, u32[]{:S(2)}, u32[]{:S(2)}) collective-permute-start(bf16[2,64,2048]{2,1,0:T(8,128)(2,1)S(1)} %gate_up.19.refs_3_), channel_id=1, source_target_pairs={{0,4},{2,6},{4,0},{6,2},{8,12},{10,14},{12,8},{14,10},{1,5},{3,7},... | collective-permute-start | bytes 1572872 | tf_op jit(solution)/shard_map/ppermute | solution.py:21
  104.0 23.0 %collective-permute-start.23 = (bf16[2,64,1536]{2,1,0:T(8,128)(2,1)S(1)}, bf16[2,64,1536]{2,1,0:T(8,128)(2,1)S(1)}, u32[]{:S(2)}, u32[]{:S(2)}) collective-permute-start(bf16[2,64,1536]{2,1,0:T(8,128)(2,1)S(1)} %gate_up.20.refs_3_), channel_id=1, source_target_pairs={{0,2},{2,0},{4,6},{6,4},{8,10},{10,8},{12,14},{14,12},{1,3},{3,1},... | collective-permute-start | bytes 1179656 | tf_op jit(solution)/shard_map/ppermute | solution.py:21
  114.6 10.1 %collective-permute-start.25 = (bf16[2,64,1024]{2,1,0:T(8,128)(2,1)S(1)}, bf16[2,64,1024]{2,1,0:T(8,128)(2,1)S(1)}, u32[]{:S(2)}, u32[]{:S(2)}) collective-permute-start(bf16[2,64,1024]{2,1,0:T(8,128)(2,1)S(1)} %get-tuple-element.87), channel_id=1, source_target_pairs={{0,2},{2,0},{4,6},{6,4},{8,10},{10,8},{12,14},{14,12},{1,3},{3,1},... | collective-permute-start | bytes 786440 | tf_op jit(solution)/shard_map/ppermute | solution.py:21
  115.4 9.3 %collective-permute-start.24 = (bf16[2,64,1024]{2,1,0:T(8,128)(2,1)S(1)}, bf16[2,64,1024]{2,1,0:T(8,128)(2,1)S(1)}, u32[]{:S(2)}, u32[]{:S(2)}) collective-permute-start(bf16[2,64,1024]{2,1,0:T(8,128)(2,1)S(1)} %get-tuple-element.86), channel_id=1, source_target_pairs={{0,4},{2,6},{4,0},{6,2},{8,12},{10,14},{12,8},{14,10},{1,5},{3,7},... | collective-permute-start | bytes 786440 | tf_op jit(solution)/shard_map/ppermute | solution.py:21
  117.0 13.4 %collective-permute-start.26 = (bf16[2,64,1024]{2,1,0:T(8,128)(2,1)S(1)}, bf16[2,64,1024]{2,1,0:T(8,128)(2,1)S(1)}, u32[]{:S(2)}, u32[]{:S(2)}) collective-permute-start(bf16[2,64,1024]{2,1,0:T(8,128)(2,1)S(1)} %gate_up.21.refs_3_), channel_id=1, source_target_pairs={{0,4},{2,6},{4,0},{6,2},{8,12},{10,14},{12,8},{14,10},{1,5},{3,7},... | collective-permute-start | bytes 786440 | tf_op jit(solution)/shard_map/ppermute | solution.py:21
  124.9 14.1 %collective-permute-start.29 = (bf16[2,64,1024]{2,1,0:T(8,128)(2,1)S(1)}, bf16[2,64,1024]{2,1,0:T(8,128)(2,1)S(1)}, u32[]{:S(2)}, u32[]{:S(2)}) collective-permute-start(bf16[2,64,1024]{2,1,0:T(8,128)(2,1)S(1)} %get-tuple-element.94), channel_id=1, source_target_pairs={{0,8},{2,10},{4,12},{6,14},{8,0},{10,2},{12,4},{14,6},{1,9},{3,11}... | collective-permute-start | bytes 786440 | tf_op jit(solution)/shard_map/ppermute | solution.py:21
  127.1 12.0 %collective-permute-start.27 = (bf16[2,64,768]{2,1,0:T(8,128)(2,1)S(1)}, bf16[2,64,768]{2,1,0:T(8,128)(2,1)S(1)}, u32[]{:S(2)}, u32[]{:S(2)}) collective-permute-start(bf16[2,64,768]{2,1,0:T(8,128)(2,1)S(1)} %get-tuple-element.92), channel_id=1, source_target_pairs={{0,4},{2,6},{4,0},{6,2},{8,12},{10,14},{12,8},{14,10},{1,5},{3,7},... | collective-permute-start | bytes 589832 | tf_op jit(solution)/shard_map/ppermute | solution.py:21
  130.5 8.6 %collective-permute-start.28 = (bf16[2,64,512]{2,1,0:T(8,128)(2,1)S(1)}, bf16[2,64,512]{2,1,0:T(8,128)(2,1)S(1)}, u32[]{:S(2)}, u32[]{:S(2)}) collective-permute-start(bf16[2,64,512]{2,1,0:T(8,128)(2,1)S(1)} %get-tuple-element.93), channel_id=1, source_target_pairs={{0,2},{2,0},{4,6},{6,4},{8,10},{10,8},{12,14},{14,12},{1,3},{3,1},... | collective-permute-start | bytes 393224 | tf_op jit(solution)/shard_map/ppermute | solution.py:21
  139.2 16.9 %collective-permute-start.30 = (bf16[2,64,640]{2,1,0:T(8,128)(2,1)S(1)}, bf16[2,64,640]{2,1,0:T(8,128)(2,1)S(1)}, u32[]{:S(2)}, u32[]{:S(2)}) collective-permute-start(bf16[2,64,640]{2,1,0:T(8,128)(2,1)S(1)} %get-tuple-element.97), channel_id=1, source_target_pairs={{0,8},{2,10},{4,12},{6,14},{8,0},{10,2},{12,4},{14,6},{1,9},{3,11}... | collective-permute-start | bytes 491528 | tf_op jit(solution)/shard_map/ppermute | solution.py:21
  140.6 13.6 %collective-permute-start.31 = (bf16[64,1024]{1,0:T(8,128)(2,1)S(1)}, bf16[64,1024]{1,0:T(8,128)(2,1)S(1)}, u32[]{:S(2)}, u32[]{:S(2)}) collective-permute-start(bf16[64,1024]{1,0:T(8,128)(2,1)S(1)} %gated.6.refs_4_.refs_0_), channel_id=1, source_target_pairs={{0,8},{2,10},{4,12},{6,14},{8,0},{10,2},{12,4},{14,6},{1,9},{3,11}... | collective-permute-start | bytes 393224 | tf_op jit(solution)/shard_map/ppermute | solution.py:21
  154.2 9.6 %collective-permute-start.34 = (bf16[64,1024]{1,0:T(8,128)(2,1)S(1)}, bf16[64,1024]{1,0:T(8,128)(2,1)S(1)}, u32[]{:S(2)}, u32[]{:S(2)}) collective-permute-start(bf16[64,1024]{1,0:T(8,128)(2,1)S(1)} %get-tuple-element.98.refs_2_.refs_0_), channel_id=1, source_target_pairs={{0,4},{2,6},{4,0},{6,2},{8,12},{10,14},{12,8},{14,10},{1,5},{3,7},... | collective-permute-start | bytes 393224 | tf_op jit(solution)/shard_map/ppermute | solution.py:21
  154.3 9.5 %collective-permute-start.35 = (bf16[64,1024]{1,0:T(8,128)(2,1)S(1)}, bf16[64,1024]{1,0:T(8,128)(2,1)S(1)}, u32[]{:S(2)}, u32[]{:S(2)}) collective-permute-start(bf16[64,1024]{1,0:T(8,128)(2,1)S(1)} %get-tuple-element.100.refs_0_), channel_id=1, source_target_pairs={{0,2},{2,0},{4,6},{6,4},{8,10},{10,8},{12,14},{14,12},{1,3},{3,1},... | collective-permute-start | bytes 393224 | tf_op jit(solution)/shard_map/ppermute | solution.py:21
  156.2 7.1 %collective-permute-start.32 = (bf16[64,640]{1,0:T(8,128)(2,1)S(1)}, bf16[64,640]{1,0:T(8,128)(2,1)S(1)}, u32[]{:S(2)}, u32[]{:S(2)}) collective-permute-start(bf16[64,640]{1,0:T(8,128)(2,1)S(1)} %gated.7.refs_0_.refs_2_), channel_id=1, source_target_pairs={{0,8},{2,10},{4,12},{6,14},{8,0},{10,2},{12,4},{14,6},{1,9},{3,11}... | collective-permute-start | bytes 245768 | tf_op jit(solution)/shard_map/ppermute | solution.py:21
  163.4 8.1 %collective-permute-start.33 = (bf16[64,768]{1,0:T(8,128)(2,1)S(1)}, bf16[64,768]{1,0:T(8,128)(2,1)S(1)}, u32[]{:S(2)}, u32[]{:S(2)}) collective-permute-start(bf16[64,768]{1,0:T(8,128)(2,1)S(1)} %get-tuple-element.99.refs_2_.refs_0_), channel_id=1, source_target_pairs={{0,4},{2,6},{4,0},{6,2},{8,12},{10,14},{12,8},{14,10},{1,5},{3,7},... | collective-permute-start | bytes 294920 | tf_op jit(solution)/shard_map/ppermute | solution.py:21
  163.9 11.1 %collective-permute-start.40 = (bf16[64,2048]{1,0:T(8,128)(2,1)S(1)}, bf16[64,2048]{1,0:T(8,128)(2,1)S(1)}, u32[]{:S(2)}, u32[]{:S(2)}) collective-permute-start(bf16[64,2048]{1,0:T(8,128)(2,1)S(1)} %join.13.refs_1_.refs_3_), channel_id=1, source_target_pairs={{0,4},{2,6},{4,0},{6,2},{8,12},{10,14},{12,8},{14,10},{1,5},{3,7},... | collective-permute-start | bytes 786440 | tf_op jit(solution)/shard_map/ppermute | solution.py:21
  165.6 9.3 %collective-permute-start.39 = (bf16[64,2048]{1,0:T(8,128)(2,1)S(1)}, bf16[64,2048]{1,0:T(8,128)(2,1)S(1)}, u32[]{:S(2)}, u32[]{:S(2)}) collective-permute-start(bf16[64,2048]{1,0:T(8,128)(2,1)S(1)} %join.12.refs_2_.refs_0_), channel_id=1, source_target_pairs={{0,2},{2,0},{4,6},{6,4},{8,10},{10,8},{12,14},{14,12},{1,3},{3,1},... | collective-permute-start | bytes 786440 | tf_op jit(solution)/shard_map/ppermute | solution.py:21
  165.9 8.9 %collective-permute-start.37 = (bf16[64,512]{1,0:T(8,128)(2,1)S(1)}, bf16[64,512]{1,0:T(8,128)(2,1)S(1)}, u32[]{:S(2)}, u32[]{:S(2)}) collective-permute-start(bf16[64,512]{1,0:T(8,128)(2,1)S(1)} %get-tuple-element.101.refs_0_), channel_id=1, source_target_pairs={{0,2},{2,0},{4,6},{6,4},{8,10},{10,8},{12,14},{14,12},{1,3},{3,1},... | collective-permute-start | bytes 196616 | tf_op jit(solution)/shard_map/ppermute | solution.py:21
  171.5 8.8 %collective-permute-start.36 = (bf16[64,1536]{1,0:T(8,128)(2,1)S(1)}, bf16[64,1536]{1,0:T(8,128)(2,1)S(1)}, u32[]{:S(2)}, u32[]{:S(2)}) collective-permute-start(bf16[64,1536]{1,0:T(8,128)(2,1)S(1)} %join.14.refs_2_.refs_0_), channel_id=1, source_target_pairs={{0,2},{2,0},{4,6},{6,4},{8,10},{10,8},{12,14},{14,12},{1,3},{3,1},... | collective-permute-start | bytes 589832 | tf_op jit(solution)/shard_map/ppermute | solution.py:21
  174.8 5.5 %collective-permute-start.38 = (bf16[64,1024]{1,0:T(8,128)(2,1)S(1)}, bf16[64,1024]{1,0:T(8,128)(2,1)S(1)}, u32[]{:S(2)}, u32[]{:S(2)}) collective-permute-start(bf16[64,1024]{1,0:T(8,128)(2,1)S(1)} %join.15.refs_4_.refs_1_), channel_id=1, source_target_pairs={{0,4},{2,6},{4,0},{6,2},{8,12},{10,14},{12,8},{14,10},{1,5},{3,7},... | collective-permute-start | bytes 393224 | tf_op jit(solution)/shard_map/ppermute | solution.py:21
  181.8 1.6 collective-permute-start.41

commit v3 on v2

--- a/solution.py
+++ b/solution.py
@@ -8,13 +8,13 @@
 BF16 = jnp.bfloat16
 F32 = jnp.float32
 BLOCK = 512
-CHUNKS = ((4, 4), (3, 2))
+CHUNKS = ((4, 3), (3, 3))
 STREAM_BITS = ((0, 1), (1, 0))
 FAR = 2
 VMEM = pl.BlockSpec(memory_space=pltpu.VMEM)
 ANY = pl.BlockSpec(memory_space=pl.ANY)
 HBM = pl.BlockSpec(memory_space=pltpu.HBM)
-PARAMS = pltpu.CompilerParams(vmem_limit_bytes=24 * 2**20)
+PARAMS = pltpu.CompilerParams(vmem_limit_bytes=18 * 2**20)
 
 
 def swap(array, bit):
@@ -333,38 +333,43 @@
     )
     a.send(0, fetched)
     a.send(1, fetched)
-    b.send(0)
-    b.send(1)
+    b.send(0, fetched and fetched[2:])
+    b.send(1, fetched and fetched[2:])
     a.keep()
     a.halve(0)
     a.halve(1)
     b.keep()
-    a.halve_far()
     b.halve(0)
     b.halve(1)
-    _, b_rows = fetch(order, *weights[:2], [], weights[2], b.ranges(0) + b.ranges(1))
+    a.halve_far()
+    _, ab_rows = fetch(order, *weights[:2], [], weights[2], a.ranges(1) + b.ranges(1))
+    b.halve_far()
+    next_sends = fetch(order, *weights[:2], b.ranges(1), weights[2], [])[0] if ahead else None
     a.gated()
-    b.halve_far()
-    next_sends = fetch(order, *weights[:2], a.ranges(1), weights[2], [])[0] if ahead else None
+    next_sends = fetch(order, *weights[:2], a.ranges(1), weights[2], [])[0] + next_sends if ahead else None
+    b.gated()
     a.join_far()
-    b.gated()
     b.join_far()
     a.join(0)
     a.join(1)
-    total = down(order, None, a.hiddens(0), weights[2], a.ranges(0))
     b.join(0)
     b.join(1)
-    total = down(order, total, a.hiddens(1), weights[2], a.ranges(1))
-    total = down(order, total, b.hiddens(0), weights[2], b.ranges(0), b_rows[:2])
-    total = down(order, total, b.hiddens(1), weights[2], b.ranges(1), b_rows[2:])
+    total = down(order, None, a.hiddens(0) + b.hiddens(0), weights[2], a.ranges(0) + b.ranges(0))
+    total = down(order, total, a.hiddens(1), weights[2], a.ranges(1), ab_rows[:2])
+    total = down(order, total, b.hiddens(1), weights[2], b.ranges(1), ab_rows[2:])
     return total + lax.ppermute(total, "gy", [(0, 1), (1, 0)]), next_sends
+
+
+def pair_rows(own, gy):
+    other = lax.ppermute(own, "gy", [(0, 1), (1, 0)])
+    return jnp.where(gy == 0, jnp.concatenate([own, other]), jnp.concatenate([other, own]))
 
 
 def fast_body(tokens, *weights):
     own_rows = tokens.shape[1]
     gy = lax.axis_index("gy")
     weights = [pltpu.with_memory_space_constraint(w, pltpu.HBM) for w in weights]
-    rows = lax.all_gather(tokens, "gy", axis=1, tiled=True)
+    rows = [pair_rows(t, gy) for t in tokens]
     first_sum, fetched = fast_layer(rows[0], weights, ahead=True)
     first_out = first_sum.astype(BF16)
     second_input = (rows[1].astype(F32) + first_out.astype(F32)).astype(BF16)

time: 184 us -> 172 us (0.935)
  waiting for transfers between devices: 50.1 us -> 34.6 us
  starting transfers between devices: 47.5 us -> 50 us
  local copies, waits for them, and re-layouts: 0.71 us -> 3.16 us
  blocking collectives: 2.36 us -> 0 us
    ppermute x40, waiting for transfers between devices: 47.1 us -> 31.1 us  [swap(): return lax.ppermute(array, 'gx', [(i, i ^ 1 << bit) for i in range(8)])]
    all_gather x1 -> x0, blocking collectives: 2.36 us -> none  [fast_body(): rows = lax.all_gather(tokens, 'gy', axis=1, tiled=True)]
    ppermute x0 -> x2, waiting for transfers between devices: none -> 2.02 us  [pair_rows(): other = lax.ppermute(own, 'gy', [(0, 1), (1, 0)])]
    pallas_call x51 -> x50, Pallas kernels: 82.1 us -> 82.8 us  [call(): pl.pallas_call(ordered, out_shape=out_shape, in_specs=in_specs + [ANY], o...]
  transfers between devices with their start and end apart: 42 -> 44, of which waited for: 13 -> 16; matrix products, arithmetic and copies ran while one was open for 0% -> 0% of each run, Pallas kernels for 40% -> 43%
where the time goes in v3:
time: 172 us
  Pallas kernels  82.8 us (48%)
  starting transfers between devices  50 us (29%)
  waiting for transfers between devices  34.6 us (20%)
  local copies, waits for them, and re-layouts  3.16 us (2%)
    pallas_call x50, Pallas kernels, call(): pl.pallas_call(ordered, out_shape=out_shape, in_specs=in_specs + [ANY], o...  82.8 us
    ppermute x40, starting transfers between devices, swap(): return lax.ppermute(array, 'gx', [(i, i ^ 1 << bit) for i in range(8)])  48.9 us
    ppermute x40, waiting for transfers between devices, swap(): return lax.ppermute(array, 'gx', [(i, i ^ 1 << bit) for i in range(8)])  31.1 us
  transfers between devices with their start and end apart: 44, of which 16 were waited for; matrix products, arithmetic and copies ran while one was open for 0% of the time, Pallas kernels for 43%

profile of v3, /device:TPU:0, one launch (start us, length us, event | category | flops | bytes accessed | tf_op | source)
XLA Modules:
  0.0 171.9 jit_solution(17858188842666521720)
XLA Ops:
  0.0 1.5 slice_bitcast_fusion.1
  2.0 0.9 collective-permute-done
  2.9 3.9 %gate_up.12.refs_3_ = bf16[2,64,2048]{2,1,0:T(8,128)(2,1)S(1)} custom-call(bf16[64,1024]{1,0:T(8,128)(2,1)S(1)} %maximum_select_fusion.refs_0_.refs_3_, bf16[1024,13312]{1,0:T(8,128)(2,1)} %refs_0_.7, bf16[1024,13312]{1,0:T(8,128)(2,1)} %refs_1_.23, bf16[64,1024]{1,0:T(8,128)(2,1)S(1)} %maximum_select_fusion.refs_0_.refs_3_), custom_call_target="tpu_custom_call" | custom-call | tf_op jit(solution)/shard_map/gate_up/pallas_call | solution.py:40
  6.8 2.9 %collective-permute-start.2 = (bf16[2,64,2048]{2,1,0:T(8,128)(2,1)S(1)}, bf16[2,64,2048]{2,1,0:T(8,128)(2,1)S(1)}, u32[]{:S(2)}, u32[]{:S(2)}) collective-permute-start(bf16[2,64,2048]{2,1,0:T(8,128)(2,1)S(1)} %gate_up.12.refs_3_), channel_id=1, source_target_pairs={{0,2},{2,0},{4,6},{6,4},{8,10},{10,8},{12,14},{14,12},{1,3},{3,1},... | collective-permute-start | bytes 1572872 | tf_op jit(solution)/shard_map/ppermute | solution.py:21
  9.6 3.2 %gate_up.13.refs_3_ = bf16[2,64,1536]{2,1,0:T(8,128)(2,1)S(1)} custom-call(bf16[64,1024]{1,0:T(8,128)(2,1)S(1)} %maximum_select_fusion.refs_0_.refs_3_, bf16[1024,13312]{1,0:T(8,128)(2,1)} %refs_0_.7, bf16[1024,13312]{1,0:T(8,128)(2,1)} %refs_1_.23, bf16[2,64,2048]{2,1,0:T(8,128)(2,1)S(1)} %gate_up.12.refs_3_), custom_call_target="tpu_custom_call" | custom-call | tf_op jit(solution)/shard_map/gate_up/pallas_call | solution.py:40
  12.8 1.6 collective-permute-start.1
  14.5 3.2 %gate_up.14.refs_3_ = bf16[2,64,1536]{2,1,0:T(8,128)(2,1)S(1)} custom-call(bf16[64,1024]{1,0:T(8,128)(2,1)S(1)} %maximum_select_fusion.refs_0_.refs_3_, bf16[1024,13312]{1,0:T(8,128)(2,1)} %refs_0_.7, bf16[1024,13312]{1,0:T(8,128)(2,1)} %refs_1_.23, bf16[2,64,1536]{2,1,0:T(8,128)(2,1)S(1)} %gate_up.13.refs_3_), custom_call_target="tpu_custom_call" | custom-call | tf_op jit(solution)/shard_map/gate_up/pallas_call | solution.py:40
  17.7 0.6 collective-permute-start.3
  18.3 3.2 %gate_up.15.refs_3_ = bf16[2,64,1536]{2,1,0:T(8,128)(2,1)S(1)} custom-call(bf16[64,1024]{1,0:T(8,128)(2,1)S(1)} %maximum_select_fusion.refs_0_.refs_3_, bf16[1024,13312]{1,0:T(8,128)(2,1)} %refs_0_.7, bf16[1024,13312]{1,0:T(8,128)(2,1)} %refs_1_.23, bf16[2,64,1536]{2,1,0:T(8,128)(2,1)S(1)} %gate_up.14.refs_3_), custom_call_target="tpu_custom_call" | custom-call | tf_op jit(solution)/shard_map/gate_up/pallas_call | solution.py:40
  21.6 5.7 %gate_up.16 = (f32[2,64,2048]{2,1,0:T(8,128)S(1)}, f32[2,64,1536]{2,1,0:T(8,128)S(1)}) custom-call(bf16[64,1024]{1,0:T(8,128)(2,1)S(1)} %maximum_select_fusion.refs_0_.refs_3_, bf16[1024,13312]{1,0:T(8,128)(2,1)} %refs_0_.7, bf16[1024,13312]{1,0:T(8,128)(2,1)} %refs_1_.23, bf16[2,64,1536]{2,1,0:T(8,128)(2,1)S(1)} %gate_up.15.refs_3_), custom_call_target="tpu_custom_call" | custom-call | tf_op jit(solution)/shard_map/gate_up/pallas_call | solution.py:40
  27.5 2.0 %collective-permute-start.7 = (bf16[2,64,1024]{2,1,0:T(8,128)(2,1)S(1)}, bf16[2,64,1024]{2,1,0:T(8,128)(2,1)S(1)}, u32[]{:S(2)}, u32[]{:S(2)}) collective-permute-start(bf16[2,64,1024]{2,1,0:T(8,128)(2,1)S(1)} %get-tuple-element.67), channel_id=1, source_target_pairs={{0,4},{2,6},{4,0},{6,2},{8,12},{10,14},{12,8},{14,10},{1,5},{3,7},... | collective-permute-start | bytes 786440 | tf_op jit(solution)/shard_map/ppermute | solution.py:21
  29.6 1.6 collective-permute-start.8
  31.2 5.1 %gate_up.17 = (f32[2,64,1536]{2,1,0:T(8,128)S(1)}, f32[2,64,1536]{2,1,0:T(8,128)S(1)}) custom-call(bf16[64,1024]{1,0:T(8,128)(2,1)S(1)} %maximum_select_fusion.refs_0_.refs_3_, bf16[1024,13312]{1,0:T(8,128)(2,1)} %refs_0_.7, bf16[1024,13312]{1,0:T(8,128)(2,1)} %refs_1_.23, f32[2,64,768]{2,1,0:T(8,128)S(1)} %get-tuple-element.60.refs_3_.refs_1_), custom_call_target="tpu_custom_call" | custom-call | tf_op jit(solution)/shard_map/gate_up/pallas_call | solution.py:40
  36.6 0.6 collective-permute-start.6
  37.3 0.6 collective-permute-done.7.refs_2_
  38.0 2.6 %collective-permute-start.10 = (bf16[2,64,896]{2,1,0:T(8,128)(2,1)S(1)}, bf16[2,64,896]{2,1,0:T(8,128)(2,1)S(1)}, u32[]{:S(2)}, u32[]{:S(2)}) collective-permute-start(bf16[2,64,896]{2,1,0:T(8,128)(2,1)S(1)} %get-tuple-element.73), channel_id=1, source_target_pairs={{0,8},{2,10},{4,12},{6,14},{8,0},{10,2},{12,4},{14,6},{1,9},{3,11}... | collective-permute-start | bytes 688136 | tf_op jit(solution)/shard_map/ppermute | solution.py:21
  40.7 5.0 %fetch.4 = (bf16[4,512,1024]{2,1,0:T(8,128)(2,1)S(1)}, bf16[3,512,1024]{2,1,0:T(8,128)(2,1)S(1)}, bf16[3,512,1024]{2,1,0:T(8,128)(2,1)S(1)}, bf16[3,512,1024]{2,1,0:T(8,128)(2,1)S(1)}) custom-call(bf16[1024,13312]{1,0:T(8,128)(2,1)} %refs_0_.7, bf16[1024,13312]{1,0:T(8,128)(2,1)} %refs_1_.23, bf16[13312,1024]{1,0:T(8,128)(2,1)} %refs_3_.7, ...), custom_call_target="tpu_custom_call" | custom-call | tf_op jit(solution)/shard_map/fetch/pallas_call | solution.py:40
  45.7 1.6 copy-done.2
  47.8 5.4 %fetch.5 = (bf16[3,2,1024,512]{3,2,1,0:T(8,128)(2,1)S(1)}, bf16[3,2,1024,512]{3,2,1,0:T(8,128)(2,1)S(1)}) custom-call(bf16[1024,13312]{1,0:T(8,128)(2,1)} %refs_0_.7, bf16[1024,13312]{1,0:T(8,128)(2,1)} %refs_1_.23, bf16[13312,1024]{1,0:T(8,128)(2,1)} %refs_3_.7, f32[2,64,768]{2,1,0:T(8,128)S(1)} %get-tuple-element.71.refs_3_.refs_0_), custom_call_target="tpu_custom_call" | custom-call | tf_op jit(solution)/shard_map/fetch/pallas_call | solution.py:40
  53.4 2.1 %collective-permute-start.12 = (bf16[64,896]{1,0:T(8,128)(2,1)S(1)}, bf16[64,896]{1,0:T(8,128)(2,1)S(1)}, u32[]{:S(2)}, u32[]{:S(2)}) collective-permute-start(bf16[64,896]{1,0:T(8,128)(2,1)S(1)} %gated.4.refs_3_.refs_0_), channel_id=1, source_target_pairs={{0,8},{2,10},{4,12},{6,14},{8,0},{10,2},{12,4},{14,6},{1,9},{3,11}... | collective-permute-start | bytes 344072 | tf_op jit(solution)/shard_map/ppermute | solution.py:21
  55.4 5.4 %fetch.6 = (bf16[4,2,1024,512]{3,2,1,0:T(8,128)(2,1)S(1)}, bf16[3,2,1024,512]{3,2,1,0:T(8,128)(2,1)S(1)}) custom-call(bf16[1024,13312]{1,0:T(8,128)(2,1)} %refs_0_.7, bf16[1024,13312]{1,0:T(8,128)(2,1)} %refs_1_.23, bf16[13312,1024]{1,0:T(8,128)(2,1)} %refs_3_.7, bf16[64,896]{1,0:T(8,128)(2,1)S(1)} %gated.4.refs_3_.refs_0_), custom_call_target="tpu_custom_call" | custom-call | tf_op jit(solution)/shard_map/fetch/pallas_call | solution.py:40
  61.0 1.0 collective-permute-start.11
  62.2 5.7 %collective-permute-start.15 = (bf16[64,1024]{1,0:T(8,128)(2,1)S(1)}, bf16[64,1024]{1,0:T(8,128)(2,1)S(1)}, u32[]{:S(2)}, u32[]{:S(2)}) collective-permute-start(bf16[64,1024]{1,0:T(8,128)(2,1)S(1)} %get-tuple-element.76.refs_2_.refs_0_), channel_id=1, source_target_pairs={{0,4},{2,6},{4,0},{6,2},{8,12},{10,14},{12,8},{14,10},{1,5},{3,7},... | collective-permute-start | bytes 393224 | tf_op jit(solution)/shard_map/ppermute | solution.py:21
  68.4 5.6 %collective-permute-start.13 = (bf16[64,768]{1,0:T(8,128)(2,1)S(1)}, bf16[64,768]{1,0:T(8,128)(2,1)S(1)}, u32[]{:S(2)}, u32[]{:S(2)}) collective-permute-start(bf16[64,768]{1,0:T(8,128)(2,1)S(1)} %get-tuple-element.77.refs_2_.refs_0_), channel_id=1, source_target_pairs={{0,4},{2,6},{4,0},{6,2},{8,12},{10,14},{12,8},{14,10},{1,5},{3,7},... | collective-permute-start | bytes 294920 | tf_op jit(solution)/shard_map/ppermute | solution.py:21
  74.0 2.1 %collective-permute-start.19 = (bf16[64,2048]{1,0:T(8,128)(2,1)S(1)}, bf16[64,2048]{1,0:T(8,128)(2,1)S(1)}, u32[]{:S(2)}, u32[]{:S(2)}) collective-permute-start(bf16[64,2048]{1,0:T(8,128)(2,1)S(1)} %join.8.refs_2_.refs_0_), channel_id=1, source_target_pairs={{0,2},{2,0},{4,6},{6,4},{8,10},{10,8},{12,14},{14,12},{1,3},{3,1},... | collective-permute-start | bytes 786440 | tf_op jit(solution)/shard_map/ppermute | solution.py:21
  76.3 0.5 collective-permute-done.13.refs_1_
  76.8 1.7 %collective-permute-done.17.refs_1_ = bf16[64,768]{1,0:T(8,128)(2,1)S(1)} collective-permute-done((bf16[64,768]{1,0:T(8,128)(2,1)S(1)}, bf16[64,768]{1,0:T(8,128)(2,1)S(1)}, u32[]{:S(2)}, u32[]{:S(2)}) %collective-permute-start.17) | collective-permute-done | bytes 98336 | tf_op jit(solution)/shard_map/ppermute | solution.py:21
  79.2 5.6 %down.6.refs_2_.refs_6_ = f32[64,1024]{1,0:T(8,128)S(1)} custom-call(bf16[64,2048]{1,0:T(8,128)(2,1)S(1)} %join.8.refs_2_.refs_0_, bf16[64,1536]{1,0:T(8,128)(2,1)S(1)} %join.9.refs_2_.refs_1_, bf16[64,1536]{1,0:T(8,128)(2,1)S(1)} %join.10.refs_2_, bf16[64,1536]{1,0:T(8,128)(2,1)S(1)} %join.11.refs_3_.refs_5_, bf16[13312,1024]{1,0:T(8,128)(2,1)} %refs_3_.7, ...), custom_call_target="tpu_custom_call" | custom-call | tf_op jit(solution)/shard_map/down/pallas_call | solution.py:40
  84.9 2.1 %down.7.refs_2_.refs_6_ = f32[64,1024]{1,0:T(8,128)S(1)} custom-call(bf16[64,2048]{1,0:T(8,128)(2,1)S(1)} %collective-permute-done.19.refs_0_, bf16[64,1536]{1,0:T(8,128)(2,1)S(1)} %collective-permute-done.20.refs_1_, f32[64,1024]{1,0:T(8,128)S(1)} %down.6.refs_2_.refs_6_, bf16[13312,1024]{1,0:T(8,128)(2,1)} %refs_3_.7, ...), custom_call_target="tpu_custom_call" | custom-call | tf_op jit(solution)/shard_map/down/pallas_call | solution.py:40
  87.1 1.8 %down.8 = f32[64,1024]{1,0:T(8,128)S(1)} custom-call(bf16[64,1536]{1,0:T(8,128)(2,1)S(1)} %collective-permute-done.16.refs_0_, bf16[64,1536]{1,0:T(8,128)(2,1)S(1)} %collective-permute-done.18.refs_1_, f32[64,1024]{1,0:T(8,128)S(1)} %down.7.refs_2_.refs_6_, bf16[13312,1024]{1,0:T(8,128)(2,1)} %refs_3_.7, bf16[3,512,1024]{2,1,0:T(8,128)(2,1)S(1)} %copy-done.1, ...), custom_call_target="tpu_custom_call" | custom-call | tf_op jit(solution)/shard_map/down/pallas_call | solution.py:40
  89.0 0.5 collective-permute-start.22
  89.5 1.1 collective-permute-done.22
  90.6 1.9 %gate_up.18.refs_2_ = bf16[2,64,2048]{2,1,0:T(8,128)(2,1)S(1)} custom-call(bf16[64,1024]{1,0:T(8,128)(2,1)S(1)} %get-tuple-element.109.refs_0_.refs_2_, bf16[4,2,1024,512]{3,2,1,0:T(8,128)(2,1)S(1)} %get-tuple-element.75.refs_2_.refs_1_, bf16[64,1024]{1,0:T(8,128)(2,1)S(1)} %get-tuple-element.109.refs_0_.refs_2_), custom_call_target="tpu_custom_call" | custom-call | tf_op jit(solution)/shard_map/gate_up/pallas_call | solution.py:40
  92.6 1.4 collective-permute-start.24
  93.9 1.4 gate_up.19.refs_2_
  95.4 2.0 %collective-permute-start.23 = (bf16[2,64,1536]{2,1,0:T(8,128)(2,1)S(1)}, bf16[2,64,1536]{2,1,0:T(8,128)(2,1)S(1)}, u32[]{:S(2)}, u32[]{:S(2)}) collective-permute-start(bf16[2,64,1536]{2,1,0:T(8,128)(2,1)S(1)} %gate_up.19.refs_2_), channel_id=1, source_target_pairs={{0,4},{2,6},{4,0},{6,2},{8,12},{10,14},{12,8},{14,10},{1,5},{3,7},... | collective-permute-start | bytes 1179656 | tf_op jit(solution)/shard_map/ppermute | solution.py:21
  97.4 1.4 gate_up.20.refs_2_
  99.0 1.4 gate_up.21.refs_3_
  100.5 0.7 collective-permute-start.26
  101.2 5.7 %gate_up.22 = (f32[2,64,2048]{2,1,0:T(8,128)S(1)}, f32[2,64,1536]{2,1,0:T(8,128)S(1)}) custom-call(bf16[64,1024]{1,0:T(8,128)(2,1)S(1)} %get-tuple-element.109.refs_0_.refs_2_, bf16[1024,13312]{1,0:T(8,128)(2,1)} %refs_0_.7, bf16[1024,13312]{1,0:T(8,128)(2,1)} %refs_1_.23, bf16[2,64,1536]{2,1,0:T(8,128)(2,1)S(1)} %gate_up.21.refs_3_), custom_call_target="tpu_custom_call" | custom-call | tf_op jit(solution)/shard_map/gate_up/pallas_call | solution.py:40
  107.5 1.4 collective-permute-start.29
  109.0 2.0 %collective-permute-start.30 = (bf16[2,64,768]{2,1,0:T(8,128)(2,1)S(1)}, bf16[2,64,768]{2,1,0:T(8,128)(2,1)S(1)}, u32[]{:S(2)}, u32[]{:S(2)}) collective-permute-start(bf16[2,64,768]{2,1,0:T(8,128)(2,1)S(1)} %get-tuple-element.96), channel_id=1, source_target_pairs={{0,2},{2,0},{4,6},{6,4},{8,10},{10,8},{12,14},{14,12},{1,3},{3,1},... | collective-permute-start | bytes 589832 | tf_op jit(solution)/shard_map/ppermute | solution.py:21
  110.9 5.1 %gate_up.23 = (f32[2,64,1536]{2,1,0:T(8,128)S(1)}, f32[2,64,1536]{2,1,0:T(8,128)S(1)}) custom-call(bf16[64,1024]{1,0:T(8,128)(2,1)S(1)} %get-tuple-element.109.refs_0_.refs_2_, bf16[1024,13312]{1,0:T(8,128)(2,1)} %refs_0_.7, bf16[1024,13312]{1,0:T(8,128)(2,1)} %refs_1_.23, f32[2,64,768]{2,1,0:T(8,128)S(1)} %get-tuple-element.88.refs_3_.refs_1_), custom_call_target="tpu_custom_call" | custom-call | tf_op jit(solution)/shard_map/gate_up/pallas_call | solution.py:40
  116.3 1.1 collective-permute-start.28
  117.4 1.9 %collective-permute-start.27 = (bf16[2,64,768]{2,1,0:T(8,128)(2,1)S(1)}, bf16[2,64,768]{2,1,0:T(8,128)(2,1)S(1)}, u32[]{:S(2)}, u32[]{:S(2)}) collective-permute-start(bf16[2,64,768]{2,1,0:T(8,128)(2,1)S(1)} %get-tuple-element.93), channel_id=1, source_target_pairs={{0,4},{2,6},{4,0},{6,2},{8,12},{10,14},{12,8},{14,10},{1,5},{3,7},... | collective-permute-start | bytes 589832 | tf_op jit(solution)/shard_map/ppermute | solution.py:21
  119.3 0.7 collective-permute-done.30.refs_3_
  120.0 1.4 collective-permute-done.29.refs_2_
  121.5 0.9 collective-permute-start.32
  122.5 5.0 %fetch.7 = (bf16[4,512,1024]{2,1,0:T(8,128)(2,1)S(1)}, bf16[3,512,1024]{2,1,0:T(8,128)(2,1)S(1)}, bf16[3,512,1024]{2,1,0:T(8,128)(2,1)S(1)}, bf16[3,512,1024]{2,1,0:T(8,128)(2,1)S(1)}) custom-call(bf16[1024,13312]{1,0:T(8,128)(2,1)} %refs_0_.7, bf16[1024,13312]{1,0:T(8,128)(2,1)} %refs_1_.23, bf16[13312,1024]{1,0:T(8,128)(2,1)} %refs_3_.7, ...), custom_call_target="tpu_custom_call" | custom-call | tf_op jit(solution)/shard_map/fetch/pallas_call | solution.py:40
  127.6 2.1 %collective-permute-start.31 = (bf16[2,64,768]{2,1,0:T(8,128)(2,1)S(1)}, bf16[2,64,768]{2,1,0:T(8,128)(2,1)S(1)}, u32[]{:S(2)}, u32[]{:S(2)}) collective-permute-start(bf16[2,64,768]{2,1,0:T(8,128)(2,1)S(1)} %get-tuple-element.100), channel_id=1, source_target_pairs={{0,8},{2,10},{4,12},{6,14},{8,0},{10,2},{12,4},{14,6},{1,9},{3,11}... | collective-permute-start | bytes 589832 | tf_op jit(solution)/shard_map/ppermute | solution.py:21
  129.7 10.5 %collective-permute-done.32.refs_1_ = bf16[2,64,896]{2,1,0:T(8,128)(2,1)S(1)} collective-permute-done((bf16[2,64,896]{2,1,0:T(8,128)(2,1)S(1)}, bf16[2,64,896]{2,1,0:T(8,128)(2,1)S(1)}, u32[]{:S(2)}, u32[]{:S(2)}) %collective-permute-start.32) | collective-permute-done | bytes 229408 | tf_op jit(solution)/shard_map/ppermute | solution.py:21
  140.4 6.3 %collective-permute-done.31.refs_1_ = bf16[2,64,768]{2,1,0:T(8,128)(2,1)S(1)} collective-permute-done((bf16[2,64,768]{2,1,0:T(8,128)(2,1)S(1)}, bf16[2,64,768]{2,1,0:T(8,128)(2,1)S(1)}, u32[]{:S(2)}, u32[]{:S(2)}) %collective-permute-start.31) | collective-permute-done | bytes 196640 | tf_op jit(solution)/shard_map/ppermute | solution.py:21
  146.9 1.9 %collective-permute-done.34.refs_1_ = bf16[64,896]{1,0:T(8,128)(2,1)S(1)} collective-permute-done((bf16[64,896]{1,0:T(8,128)(2,1)S(1)}, bf16[64,896]{1,0:T(8,128)(2,1)S(1)}, u32[]{:S(2)}, u32[]{:S(2)}) %collective-permute-start.34) | collective-permute-done | bytes 114720 | tf_op jit(solution)/shard_map/ppermute | solution.py:21
  148.8 0.5 collective-permute-start.37
  149.7 2.8 %collective-permute-done.33.refs_1_ = bf16[64,768]{1,0:T(8,128)(2,1)S(1)} collective-permute-done((bf16[64,768]{1,0:T(8,128)(2,1)S(1)}, bf16[64,768]{1,0:T(8,128)(2,1)S(1)}, u32[]{:S(2)}, u32[]{:S(2)}) %collective-permute-start.33) | collective-permute-done | bytes 98336 | tf_op jit(solution)/shard_map/ppermute | solution.py:21
  153.0 2.3 %collective-permute-done.37.refs_1_ = bf16[64,1024]{1,0:T(8,128)(2,1)S(1)} collective-permute-done((bf16[64,1024]{1,0:T(8,128)(2,1)S(1)}, bf16[64,1024]{1,0:T(8,128)(2,1)S(1)}, u32[]{:S(2)}, u32[]{:S(2)}) %collective-permute-start.37) | collective-permute-done | bytes 131104 | tf_op jit(solution)/shard_map/ppermute | solution.py:21
  155.5 1.4 collective-permute-start.42
  156.9 1.5 collective-permute-done.35.refs_1_
  158.5 1.6 collective-permute-start.40
  160.2 5.3 %down.9.refs_2_.refs_6_ = f32[64,1024]{1,0:T(8,128)S(1)} custom-call(bf16[64,2048]{1,0:T(8,128)(2,1)S(1)} %join.12.refs_2_.refs_0_, bf16[64,1536]{1,0:T(8,128)(2,1)S(1)} %join.13.refs_2_.refs_1_, bf16[64,1536]{1,0:T(8,128)(2,1)S(1)} %join.14.refs_2_, bf16[64,1536]{1,0:T(8,128)(2,1)S(1)} %join.15.refs_3_.refs_5_, bf16[13312,1024]{1,0:T(8,128)(2,1)} %refs_3_.7, ...), custom_call_target="tpu_custom_call" | custom-call | tf_op jit(solution)/shard_map/down/pallas_call | solution.py:40
  165.6 2.1 %down.10.refs_2_.refs_6_ = f32[64,1024]{1,0:T(8,128)S(1)} custom-call(bf16[64,2048]{1,0:T(8,128)(2,1)S(1)} %collective-permute-done.41.refs_0_, bf16[64,1536]{1,0:T(8,128)(2,1)S(1)} %collective-permute-done.42.refs_1_, f32[64,1024]{1,0:T(8,128)S(1)} %down.9.refs_2_.refs_6_, bf16[13312,1024]{1,0:T(8,128)(2,1)} %refs_3_.7, ...), custom_call_target="tpu_custom_call" | custom-call | tf_op jit(solution)/shard_map/down/pallas_call | solution.py:40
  167.7 1.8 %down.11 = f32[64,1024]{1,0:T(8,128)S(1)} custom-call(bf16[64,1536]{1,0:T(8,128)(2,1)S(1)} %collective-permute-done.38.refs_0_, bf16[64,1536]{1,0:T(8,128)(2,1)S(1)} %collective-permute-done.40.refs_1_, f32[64,1024]{1,0:T(8,128)S(1)} %down.10.refs_2_.refs_6_, bf16[13312,1024]{1,0:T(8,128)(2,1)} %refs_3_.7, ...), custom_call_target="tpu_custom_call" | custom-call | tf_op jit(solution)/shard_map/down/pallas_call | solution.py:40
  169.7 1.5 collective-permute-done.43
  171.2 0.7 fusion.1
  (89 shorter events, 6.5 us)
Async XLA Ops:
  1.5 1.4 collective-permute-start
  6.8 20.6 %collective-permute-start.2 = (bf16[2,64,2048]{2,1,0:T(8,128)(2,1)S(1)}, bf16[2,64,2048]{2,1,0:T(8,128)(2,1)S(1)}, u32[]{:S(2)}, u32[]{:S(2)}) collective-permute-start(bf16[2,64,2048]{2,1,0:T(8,128)(2,1)S(1)} %gate_up.12.refs_3_), channel_id=1, source_target_pairs={{0,2},{2,0},{4,6},{6,4},{8,10},{10,8},{12,14},{14,12},{1,3},{3,1},... | collective-permute-start | bytes 1572872 | tf_op jit(solution)/shard_map/ppermute | solution.py:21
  12.8 16.7 %collective-permute-start.1 = (bf16[2,64,1536]{2,1,0:T(8,128)(2,1)S(1)}, bf16[2,64,1536]{2,1,0:T(8,128)(2,1)S(1)}, u32[]{:S(2)}, u32[]{:S(2)}) collective-permute-start(bf16[2,64,1536]{2,1,0:T(8,128)(2,1)S(1)} %gate_up.13.refs_3_), channel_id=1, source_target_pairs={{0,4},{2,6},{4,0},{6,2},{8,12},{10,14},{12,8},{14,10},{1,5},{3,7},... | collective-permute-start | bytes 1179656 | tf_op jit(solution)/shard_map/ppermute | solution.py:21
  17.7 18.7 %collective-permute-start.3 = (bf16[2,64,1536]{2,1,0:T(8,128)(2,1)S(1)}, bf16[2,64,1536]{2,1,0:T(8,128)(2,1)S(1)}, u32[]{:S(2)}, u32[]{:S(2)}) collective-permute-start(bf16[2,64,1536]{2,1,0:T(8,128)(2,1)S(1)} %gate_up.14.refs_3_), channel_id=1, source_target_pairs={{0,2},{2,0},{4,6},{6,4},{8,10},{10,8},{12,14},{14,12},{1,3},{3,1},... | collective-permute-start | bytes 1179656 | tf_op jit(solution)/shard_map/ppermute | solution.py:21
  21.5 14.9 %collective-permute-start.4 = (bf16[2,64,1536]{2,1,0:T(8,128)(2,1)S(1)}, bf16[2,64,1536]{2,1,0:T(8,128)(2,1)S(1)}, u32[]{:S(2)}, u32[]{:S(2)}) collective-permute-start(bf16[2,64,1536]{2,1,0:T(8,128)(2,1)S(1)} %gate_up.15.refs_3_), channel_id=1, source_target_pairs={{0,4},{2,6},{4,0},{6,2},{8,12},{10,14},{12,8},{14,10},{1,5},{3,7},... | collective-permute-start | bytes 1179656 | tf_op jit(solution)/shard_map/ppermute | solution.py:21
  27.5 10.5 %collective-permute-start.7 = (bf16[2,64,1024]{2,1,0:T(8,128)(2,1)S(1)}, bf16[2,64,1024]{2,1,0:T(8,128)(2,1)S(1)}, u32[]{:S(2)}, u32[]{:S(2)}) collective-permute-start(bf16[2,64,1024]{2,1,0:T(8,128)(2,1)S(1)} %get-tuple-element.67), channel_id=1, source_target_pairs={{0,4},{2,6},{4,0},{6,2},{8,12},{10,14},{12,8},{14,10},{1,5},{3,7},... | collective-permute-start | bytes 786440 | tf_op jit(solution)/shard_map/ppermute | solution.py:21
  29.6 7.7 %collective-permute-start.8 = (bf16[2,64,768]{2,1,0:T(8,128)(2,1)S(1)}, bf16[2,64,768]{2,1,0:T(8,128)(2,1)S(1)}, u32[]{:S(2)}, u32[]{:S(2)}) collective-permute-start(bf16[2,64,768]{2,1,0:T(8,128)(2,1)S(1)} %get-tuple-element.68), channel_id=1, source_target_pairs={{0,2},{2,0},{4,6},{6,4},{8,10},{10,8},{12,14},{14,12},{1,3},{3,1},... | collective-permute-start | bytes 589832 | tf_op jit(solution)/shard_map/ppermute | solution.py:21
  36.6 10.8 %collective-permute-start.6 = (bf16[2,64,768]{2,1,0:T(8,128)(2,1)S(1)}, bf16[2,64,768]{2,1,0:T(8,128)(2,1)S(1)}, u32[]{:S(2)}, u32[]{:S(2)}) collective-permute-start(bf16[2,64,768]{2,1,0:T(8,128)(2,1)S(1)} %get-tuple-element.66), channel_id=1, source_target_pairs={{0,2},{2,0},{4,6},{6,4},{8,10},{10,8},{12,14},{14,12},{1,3},{3,1},... | collective-permute-start | bytes 589832 | tf_op jit(solution)/shard_map/ppermute | solution.py:21
  37.1 10.2 %collective-permute-start.5 = (bf16[2,64,768]{2,1,0:T(8,128)(2,1)S(1)}, bf16[2,64,768]{2,1,0:T(8,128)(2,1)S(1)}, u32[]{:S(2)}, u32[]{:S(2)}) collective-permute-start(bf16[2,64,768]{2,1,0:T(8,128)(2,1)S(1)} %get-tuple-element.65), channel_id=1, source_target_pairs={{0,4},{2,6},{4,0},{6,2},{8,12},{10,14},{12,8},{14,10},{1,5},{3,7},... | collective-permute-start | bytes 589832 | tf_op jit(solution)/shard_map/ppermute | solution.py:21
  38.0 15.2 %collective-permute-start.10 = (bf16[2,64,896]{2,1,0:T(8,128)(2,1)S(1)}, bf16[2,64,896]{2,1,0:T(8,128)(2,1)S(1)}, u32[]{:S(2)}, u32[]{:S(2)}) collective-permute-start(bf16[2,64,896]{2,1,0:T(8,128)(2,1)S(1)} %get-tuple-element.73), channel_id=1, source_target_pairs={{0,8},{2,10},{4,12},{6,14},{8,0},{10,2},{12,4},{14,6},{1,9},{3,11}... | collective-permute-start | bytes 688136 | tf_op jit(solution)/shard_map/ppermute | solution.py:21
  45.7 1.6 copy-start.2
  47.3 5.9 %copy-start = (bf16[3,512,1024]{2,1,0:T(8,128)(2,1)}, bf16[3,512,1024]{2,1,0:T(8,128)(2,1)S(1)}, u32[]{:S(2)}) copy-start(bf16[3,512,1024]{2,1,0:T(8,128)(2,1)S(1)} %get-tuple-element.81.refs_4_) | copy-start | bytes 9437188
  47.4 13.4 %collective-permute-start.9 = (bf16[2,64,768]{2,1,0:T(8,128)(2,1)S(1)}, bf16[2,64,768]{2,1,0:T(8,128)(2,1)S(1)}, u32[]{:S(2)}, u32[]{:S(2)}) collective-permute-start(bf16[2,64,768]{2,1,0:T(8,128)(2,1)S(1)} %get-tuple-element.72), channel_id=1, source_target_pairs={{0,8},{2,10},{4,12},{6,14},{8,0},{10,2},{12,4},{14,6},{1,9},{3,11}... | collective-permute-start | bytes 589832 | tf_op jit(solution)/shard_map/ppermute | solution.py:21
  53.4 8.8 %collective-permute-start.12 = (bf16[64,896]{1,0:T(8,128)(2,1)S(1)}, bf16[64,896]{1,0:T(8,128)(2,1)S(1)}, u32[]{:S(2)}, u32[]{:S(2)}) collective-permute-start(bf16[64,896]{1,0:T(8,128)(2,1)S(1)} %gated.4.refs_3_.refs_0_), channel_id=1, source_target_pairs={{0,8},{2,10},{4,12},{6,14},{8,0},{10,2},{12,4},{14,6},{1,9},{3,11}... | collective-permute-start | bytes 344072 | tf_op jit(solution)/shard_map/ppermute | solution.py:21
  61.0 7.4 %collective-permute-start.11 = (bf16[64,768]{1,0:T(8,128)(2,1)S(1)}, bf16[64,768]{1,0:T(8,128)(2,1)S(1)}, u32[]{:S(2)}, u32[]{:S(2)}) collective-permute-start(bf16[64,768]{1,0:T(8,128)(2,1)S(1)} %gated.5.refs_2_.refs_0_), channel_id=1, source_target_pairs={{0,8},{2,10},{4,12},{6,14},{8,0},{10,2},{12,4},{14,6},{1,9},{3,11}... | collective-permute-start | bytes 294920 | tf_op jit(solution)/shard_map/ppermute | solution.py:21
  62.2 11.8 %collective-permute-start.15 = (bf16[64,1024]{1,0:T(8,128)(2,1)S(1)}, bf16[64,1024]{1,0:T(8,128)(2,1)S(1)}, u32[]{:S(2)}, u32[]{:S(2)}) collective-permute-start(bf16[64,1024]{1,0:T(8,128)(2,1)S(1)} %get-tuple-element.76.refs_2_.refs_0_), channel_id=1, source_target_pairs={{0,4},{2,6},{4,0},{6,2},{8,12},{10,14},{12,8},{14,10},{1,5},{3,7},... | collective-permute-start | bytes 393224 | tf_op jit(solution)/shard_map/ppermute | solution.py:21
  67.9 8.2 %collective-permute-start.14 = (bf16[64,768]{1,0:T(8,128)(2,1)S(1)}, bf16[64,768]{1,0:T(8,128)(2,1)S(1)}, u32[]{:S(2)}, u32[]{:S(2)}) collective-permute-start(bf16[64,768]{1,0:T(8,128)(2,1)S(1)} %get-tuple-element.78.refs_0_), channel_id=1, source_target_pairs={{0,2},{2,0},{4,6},{6,4},{8,10},{10,8},{12,14},{14,12},{1,3},{3,1},... | collective-permute-start | bytes 294920 | tf_op jit(solution)/shard_map/ppermute | solution.py:21
  68.4 8.4 %collective-permute-start.13 = (bf16[64,768]{1,0:T(8,128)(2,1)S(1)}, bf16[64,768]{1,0:T(8,128)(2,1)S(1)}, u32[]{:S(2)}, u32[]{:S(2)}) collective-permute-start(bf16[64,768]{1,0:T(8,128)(2,1)S(1)} %get-tuple-element.77.refs_2_.refs_0_), channel_id=1, source_target_pairs={{0,4},{2,6},{4,0},{6,2},{8,12},{10,14},{12,8},{14,10},{1,5},{3,7},... | collective-permute-start | bytes 294920 | tf_op jit(solution)/shard_map/ppermute | solution.py:21
  74.0 4.6 %collective-permute-start.17 = (bf16[64,768]{1,0:T(8,128)(2,1)S(1)}, bf16[64,768]{1,0:T(8,128)(2,1)S(1)}, u32[]{:S(2)}, u32[]{:S(2)}) collective-permute-start(bf16[64,768]{1,0:T(8,128)(2,1)S(1)} %get-tuple-element.79.refs_0_), channel_id=1, source_target_pairs={{0,2},{2,0},{4,6},{6,4},{8,10},{10,8},{12,14},{14,12},{1,3},{3,1},... | collective-permute-start | bytes 294920 | tf_op jit(solution)/shard_map/ppermute | solution.py:21
  74.0 10.9 %collective-permute-start.19 = (bf16[64,2048]{1,0:T(8,128)(2,1)S(1)}, bf16[64,2048]{1,0:T(8,128)(2,1)S(1)}, u32[]{:S(2)}, u32[]{:S(2)}) collective-permute-start(bf16[64,2048]{1,0:T(8,128)(2,1)S(1)} %join.8.refs_2_.refs_0_), channel_id=1, source_target_pairs={{0,2},{2,0},{4,6},{6,4},{8,10},{10,8},{12,14},{14,12},{1,3},{3,1},... | collective-permute-start | bytes 786440 | tf_op jit(solution)/shard_map/ppermute | solution.py:21
  76.1 8.7 %collective-permute-start.20 = (bf16[64,1536]{1,0:T(8,128)(2,1)S(1)}, bf16[64,1536]{1,0:T(8,128)(2,1)S(1)}, u32[]{:S(2)}, u32[]{:S(2)}) collective-permute-start(bf16[64,1536]{1,0:T(8,128)(2,1)S(1)} %join.9.refs_2_.refs_1_), channel_id=1, source_target_pairs={{0,4},{2,6},{4,0},{6,2},{8,12},{10,14},{12,8},{14,10},{1,5},{3,7},... | collective-permute-start | bytes 589832 | tf_op jit(solution)/shard_map/ppermute | solution.py:21
  78.6 6.3 %copy-start.3 = (bf16[3,512,1024]{2,1,0:T(8,128)(2,1)S(1)}, bf16[3,512,1024]{2,1,0:T(8,128)(2,1)}, u32[]{:S(2)}) copy-start(bf16[3,512,1024]{2,1,0:T(8,128)(2,1)} %copy-done.2) | copy-start | bytes 9437188
  78.6 8.4 %collective-permute-start.18 = (bf16[64,1536]{1,0:T(8,128)(2,1)S(1)}, bf16[64,1536]{1,0:T(8,128)(2,1)S(1)}, u32[]{:S(2)}, u32[]{:S(2)}) collective-permute-start(bf16[64,1536]{1,0:T(8,128)(2,1)S(1)} %join.11.refs_3_.refs_5_), channel_id=1, source_target_pairs={{0,4},{2,6},{4,0},{6,2},{8,12},{10,14},{12,8},{14,10},{1,5},{3,7},... | collective-permute-start | bytes 589832 | tf_op jit(solution)/shard_map/ppermute | solution.py:21
  78.8 8.3 %collective-permute-start.16 = (bf16[64,1536]{1,0:T(8,128)(2,1)S(1)}, bf16[64,1536]{1,0:T(8,128)(2,1)S(1)}, u32[]{:S(2)}, u32[]{:S(2)}) collective-permute-start(bf16[64,1536]{1,0:T(8,128)(2,1)S(1)} %join.10.refs_2_), channel_id=1, source_target_pairs={{0,2},{2,0},{4,6},{6,4},{8,10},{10,8},{12,14},{14,12},{1,3},{3,1},... | collective-permute-start | bytes 589832 | tf_op jit(solution)/shard_map/ppermute | solution.py:21
  84.9 2.2 %copy-start.1 = (bf16[3,512,1024]{2,1,0:T(8,128)(2,1)S(1)}, bf16[3,512,1024]{2,1,0:T(8,128)(2,1)}, u32[]{:S(2)}) copy-start(bf16[3,512,1024]{2,1,0:T(8,128)(2,1)} %copy-done) | copy-start | bytes 9437188
  87.1 1.9 %copy-start.4 = (bf16[32,1024]{1,0:T(8,128)(2,1)S(1)}, bf16[32,1024]{1,0:T(8,128)(2,1)}, u32[]{:S(2)}) copy-start(bf16[32,1024]{1,0:T(8,128)(2,1)} %get-tuple-element.112) | copy-start | bytes 196612
  88.9 1.7 collective-permute-start.21
  89.0 1.6 collective-permute-start.22
  92.6 14.8 %collective-permute-start.24 = (bf16[2,64,2048]{2,1,0:T(8,128)(2,1)S(1)}, bf16[2,64,2048]{2,1,0:T(8,128)(2,1)S(1)}, u32[]{:S(2)}, u32[]{:S(2)}) collective-permute-start(bf16[2,64,2048]{2,1,0:T(8,128)(2,1)S(1)} %gate_up.18.refs_2_), channel_id=1, source_target_pairs={{0,2},{2,0},{4,6},{6,4},{8,10},{10,8},{12,14},{14,12},{1,3},{3,1},... | collective-permute-start | bytes 1572872 | tf_op jit(solution)/shard_map/ppermute | solution.py:21
  95.4 13.5 %collective-permute-start.23 = (bf16[2,64,1536]{2,1,0:T(8,128)(2,1)S(1)}, bf16[2,64,1536]{2,1,0:T(8,128)(2,1)S(1)}, u32[]{:S(2)}, u32[]{:S(2)}) collective-permute-start(bf16[2,64,1536]{2,1,0:T(8,128)(2,1)S(1)} %gate_up.19.refs_2_), channel_id=1, source_target_pairs={{0,4},{2,6},{4,0},{6,2},{8,12},{10,14},{12,8},{14,10},{1,5},{3,7},... | collective-permute-start | bytes 1179656 | tf_op jit(solution)/shard_map/ppermute | solution.py:21
  98.8 17.3 %collective-permute-start.25 = (bf16[2,64,1536]{2,1,0:T(8,128)(2,1)S(1)}, bf16[2,64,1536]{2,1,0:T(8,128)(2,1)S(1)}, u32[]{:S(2)}, u32[]{:S(2)}) collective-permute-start(bf16[2,64,1536]{2,1,0:T(8,128)(2,1)S(1)} %gate_up.20.refs_2_), channel_id=1, source_target_pairs={{0,2},{2,0},{4,6},{6,4},{8,10},{10,8},{12,14},{14,12},{1,3},{3,1},... | collective-permute-start | bytes 1179656 | tf_op jit(solution)/shard_map/ppermute | solution.py:21
  100.5 15.7 %collective-permute-start.26 = (bf16[2,64,1536]{2,1,0:T(8,128)(2,1)S(1)}, bf16[2,64,1536]{2,1,0:T(8,128)(2,1)S(1)}, u32[]{:S(2)}, u32[]{:S(2)}) collective-permute-start(bf16[2,64,1536]{2,1,0:T(8,128)(2,1)S(1)} %gate_up.21.refs_3_), channel_id=1, source_target_pairs={{0,4},{2,6},{4,0},{6,2},{8,12},{10,14},{12,8},{14,10},{1,5},{3,7},... | collective-permute-start | bytes 1179656 | tf_op jit(solution)/shard_map/ppermute | solution.py:21
  107.5 14.0 %collective-permute-start.29 = (bf16[2,64,1024]{2,1,0:T(8,128)(2,1)S(1)}, bf16[2,64,1024]{2,1,0:T(8,128)(2,1)S(1)}, u32[]{:S(2)}, u32[]{:S(2)}) collective-permute-start(bf16[2,64,1024]{2,1,0:T(8,128)(2,1)S(1)} %get-tuple-element.95), channel_id=1, source_target_pairs={{0,4},{2,6},{4,0},{6,2},{8,12},{10,14},{12,8},{14,10},{1,5},{3,7},... | collective-permute-start | bytes 786440 | tf_op jit(solution)/shard_map/ppermute | solution.py:21
  109.0 11.1 %collective-permute-start.30 = (bf16[2,64,768]{2,1,0:T(8,128)(2,1)S(1)}, bf16[2,64,768]{2,1,0:T(8,128)(2,1)S(1)}, u32[]{:S(2)}, u32[]{:S(2)}) collective-permute-start(bf16[2,64,768]{2,1,0:T(8,128)(2,1)S(1)} %get-tuple-element.96), channel_id=1, source_target_pairs={{0,2},{2,0},{4,6},{6,4},{8,10},{10,8},{12,14},{14,12},{1,3},{3,1},... | collective-permute-start | bytes 589832 | tf_op jit(solution)/shard_map/ppermute | solution.py:21
  116.3 11.2 %collective-permute-start.28 = (bf16[2,64,768]{2,1,0:T(8,128)(2,1)S(1)}, bf16[2,64,768]{2,1,0:T(8,128)(2,1)S(1)}, u32[]{:S(2)}, u32[]{:S(2)}) collective-permute-start(bf16[2,64,768]{2,1,0:T(8,128)(2,1)S(1)} %get-tuple-element.94), channel_id=1, source_target_pairs={{0,2},{2,0},{4,6},{6,4},{8,10},{10,8},{12,14},{14,12},{1,3},{3,1},... | collective-permute-start | bytes 589832 | tf_op jit(solution)/shard_map/ppermute | solution.py:21
  117.4 10.1 %collective-permute-start.27 = (bf16[2,64,768]{2,1,0:T(8,128)(2,1)S(1)}, bf16[2,64,768]{2,1,0:T(8,128)(2,1)S(1)}, u32[]{:S(2)}, u32[]{:S(2)}) collective-permute-start(bf16[2,64,768]{2,1,0:T(8,128)(2,1)S(1)} %get-tuple-element.93), channel_id=1, source_target_pairs={{0,4},{2,6},{4,0},{6,2},{8,12},{10,14},{12,8},{14,10},{1,5},{3,7},... | collective-permute-start | bytes 589832 | tf_op jit(solution)/shard_map/ppermute | solution.py:21
  121.5 18.7 %collective-permute-start.32 = (bf16[2,64,896]{2,1,0:T(8,128)(2,1)S(1)}, bf16[2,64,896]{2,1,0:T(8,128)(2,1)S(1)}, u32[]{:S(2)}, u32[]{:S(2)}) collective-permute-start(bf16[2,64,896]{2,1,0:T(8,128)(2,1)S(1)} %get-tuple-element.101), channel_id=1, source_target_pairs={{0,8},{2,10},{4,12},{6,14},{8,0},{10,2},{12,4},{14,6},{1,9},{3,11}... | collective-permute-start | bytes 688136 | tf_op jit(solution)/shard_map/ppermute | solution.py:21
  127.6 19.1 %collective-permute-start.31 = (bf16[2,64,768]{2,1,0:T(8,128)(2,1)S(1)}, bf16[2,64,768]{2,1,0:T(8,128)(2,1)S(1)}, u32[]{:S(2)}, u32[]{:S(2)}) collective-permute-start(bf16[2,64,768]{2,1,0:T(8,128)(2,1)S(1)} %get-tuple-element.100), channel_id=1, source_target_pairs={{0,8},{2,10},{4,12},{6,14},{8,0},{10,2},{12,4},{14,6},{1,9},{3,11}... | collective-permute-start | bytes 589832 | tf_op jit(solution)/shard_map/ppermute | solution.py:21
  140.3 8.4 %collective-permute-start.34 = (bf16[64,896]{1,0:T(8,128)(2,1)S(1)}, bf16[64,896]{1,0:T(8,128)(2,1)S(1)}, u32[]{:S(2)}, u32[]{:S(2)}) collective-permute-start(bf16[64,896]{1,0:T(8,128)(2,1)S(1)} %gated.6.refs_2_.refs_0_), channel_id=1, source_target_pairs={{0,8},{2,10},{4,12},{6,14},{8,0},{10,2},{12,4},{14,6},{1,9},{3,11}... | collective-permute-start | bytes 344072 | tf_op jit(solution)/shard_map/ppermute | solution.py:21
  146.8 5.7 %collective-permute-start.33 = (bf16[64,768]{1,0:T(8,128)(2,1)S(1)}, bf16[64,768]{1,0:T(8,128)(2,1)S(1)}, u32[]{:S(2)}, u32[]{:S(2)}) collective-permute-start(bf16[64,768]{1,0:T(8,128)(2,1)S(1)} %gated.7.refs_2_.refs_0_), channel_id=1, source_target_pairs={{0,8},{2,10},{4,12},{6,14},{8,0},{10,2},{12,4},{14,6},{1,9},{3,11}... | collective-permute-start | bytes 294920 | tf_op jit(solution)/shard_map/ppermute | solution.py:21
  148.8 6.5 %collective-permute-start.37 = (bf16[64,1024]{1,0:T(8,128)(2,1)S(1)}, bf16[64,1024]{1,0:T(8,128)(2,1)S(1)}, u32[]{:S(2)}, u32[]{:S(2)}) collective-permute-start(bf16[64,1024]{1,0:T(8,128)(2,1)S(1)} %get-tuple-element.102.refs_2_.refs_0_), channel_id=1, source_target_pairs={{0,4},{2,6},{4,0},{6,2},{8,12},{10,14},{12,8},{14,10},{1,5},{3,7},... | collective-permute-start | bytes 393224 | tf_op jit(solution)/shard_map/ppermute | solution.py:21
  149.3 6.2 %collective-permute-start.36 = (bf16[64,768]{1,0:T(8,128)(2,1)S(1)}, bf16[64,768]{1,0:T(8,128)(2,1)S(1)}, u32[]{:S(2)}, u32[]{:S(2)}) collective-permute-start(bf16[64,768]{1,0:T(8,128)(2,1)S(1)} %get-tuple-element.104.refs_0_), channel_id=1, source_target_pairs={{0,2},{2,0},{4,6},{6,4},{8,10},{10,8},{12,14},{14,12},{1,3},{3,1},... | collective-permute-start | bytes 294920 | tf_op jit(solution)/shard_map/ppermute | solution.py:21
  152.6 5.8 %collective-permute-start.35 = (bf16[64,768]{1,0:T(8,128)(2,1)S(1)}, bf16[64,768]{1,0:T(8,128)(2,1)S(1)}, u32[]{:S(2)}, u32[]{:S(2)}) collective-permute-start(bf16[64,768]{1,0:T(8,128)(2,1)S(1)} %get-tuple-element.103.refs_2_.refs_0_), channel_id=1, source_target_pairs={{0,4},{2,6},{4,0},{6,2},{8,12},{10,14},{12,8},{14,10},{1,5},{3,7},... | collective-permute-start | bytes 294920 | tf_op jit(solution)/shard_map/ppermute | solution.py:21
  152.6 5.8 %collective-permute-start.39 = (bf16[64,768]{1,0:T(8,128)(2,1)S(1)}, bf16[64,768]{1,0:T(8,128)(2,1)S(1)}, u32[]{:S(2)}, u32[]{:S(2)}) collective-permute-start(bf16[64,768]{1,0:T(8,128)(2,1)S(1)} %get-tuple-element.105.refs_0_), channel_id=1, source_target_pairs={{0,2},{2,0},{4,6},{6,4},{8,10},{10,8},{12,14},{14,12},{1,3},{3,1},... | collective-permute-start | bytes 294920 | tf_op jit(solution)/shard_map/ppermute | solution.py:21
  155.4 10.2 %collective-permute-start.41 = (bf16[64,2048]{1,0:T(8,128)(2,1)S(1)}, bf16[64,2048]{1,0:T(8,128)(2,1)S(1)}, u32[]{:S(2)}, u32[]{:S(2)}) collective-permute-start(bf16[64,2048]{1,0:T(8,128)(2,1)S(1)} %join.12.refs_2_.refs_0_), channel_id=1, source_target_pairs={{0,2},{2,0},{4,6},{6,4},{8,10},{10,8},{12,14},{14,12},{1,3},{3,1},... | collective-permute-start | bytes 786440 | tf_op jit(solution)/shard_map/ppermute | solution.py:21
  155.5 10.0 %collective-permute-start.42 = (bf16[64,1536]{1,0:T(8,128)(2,1)S(1)}, bf16[64,1536]{1,0:T(8,128)(2,1)S(1)}, u32[]{:S(2)}, u32[]{:S(2)}) collective-permute-start(bf16[64,1536]{1,0:T(8,128)(2,1)S(1)} %join.13.refs_2_.refs_1_), channel_id=1, source_target_pairs={{0,4},{2,6},{4,0},{6,2},{8,12},{10,14},{12,8},{14,10},{1,5},{3,7},... | collective-permute-start | bytes 589832 | tf_op jit(solution)/shard_map/ppermute | solution.py:21
  158.5 9.3 %collective-permute-start.40 = (bf16[64,1536]{1,0:T(8,128)(2,1)S(1)}, bf16[64,1536]{1,0:T(8,128)(2,1)S(1)}, u32[]{:S(2)}, u32[]{:S(2)}) collective-permute-start(bf16[64,1536]{1,0:T(8,128)(2,1)S(1)} %join.15.refs_3_.refs_5_), channel_id=1, source_target_pairs={{0,4},{2,6},{4,0},{6,2},{8,12},{10,14},{12,8},{14,10},{1,5},{3,7},... | collective-permute-start | bytes 589832 | tf_op jit(solution)/shard_map/ppermute | solution.py:21
  160.1 7.6 %collective-permute-start.38 = (bf16[64,1536]{1,0:T(8,128)(2,1)S(1)}, bf16[64,1536]{1,0:T(8,128)(2,1)S(1)}, u32[]{:S(2)}, u32[]{:S(2)}) collective-permute-start(bf16[64,1536]{1,0:T(8,128)(2,1)S(1)} %join.14.refs_2_), channel_id=1, source_target_pairs={{0,2},{2,0},{4,6},{6,4},{8,10},{10,8},{12,14},{14,12},{1,3},{3,1},... | collective-permute-start | bytes 589832 | tf_op jit(solution)/shard_map/ppermute | solution.py:21
  169.6 1.6 collective-permute-start.43

commit v4 on v3

--- a/solution.py
+++ b/solution.py
@@ -344,9 +344,14 @@
     a.halve_far()
     _, ab_rows = fetch(order, *weights[:2], [], weights[2], a.ranges(1) + b.ranges(1))
     b.halve_far()
-    next_sends = fetch(order, *weights[:2], b.ranges(1), weights[2], [])[0] if ahead else None
+    if ahead:
+        next_sends, own_rows = fetch(order, *weights[:2], b.ranges(1), weights[2], [])[0], ()
+    else:
+        next_sends = None
+        own_rows = fetch(order, *weights[:2], [], weights[2], a.ranges(0) + b.ranges(0))[1]
     a.gated()
-    next_sends = fetch(order, *weights[:2], a.ranges(1), weights[2], [])[0] + next_sends if ahead else None
+    if ahead:
+        next_sends = fetch(order, *weights[:2], a.ranges(1), weights[2], [])[0] + next_sends
     b.gated()
     a.join_far()
     b.join_far()
@@ -354,7 +359,7 @@
     a.join(1)
     b.join(0)
     b.join(1)
-    total = down(order, None, a.hiddens(0) + b.hiddens(0), weights[2], a.ranges(0) + b.ranges(0))
+    total = down(order, None, a.hiddens(0) + b.hiddens(0), weights[2], a.ranges(0) + b.ranges(0), own_rows)
     total = down(order, total, a.hiddens(1), weights[2], a.ranges(1), ab_rows[:2])
     total = down(order, total, b.hiddens(1), weights[2], b.ranges(1), ab_rows[2:])
     return total + lax.ppermute(total, "gy", [(0, 1), (1, 0)]), next_sends

time: 172 us -> 171 us (level)
  waiting for transfers between devices: 34.6 us -> 29.5 us
  Pallas kernels: 82.8 us -> 86.4 us
    ppermute x40, waiting for transfers between devices: 31.1 us -> 26 us  [swap(): return lax.ppermute(array, 'gx', [(i, i ^ 1 << bit) for i in range(8)])]
    pallas_call x50 -> x51, Pallas kernels: 82.8 us -> 86.4 us  [call(): pl.pallas_call(ordered, out_shape=out_shape, in_specs=in_specs + [ANY], o...]
  transfers between devices with their start and end apart: 44 -> 44, of which waited for: 16 -> 16; matrix products, arithmetic and copies ran while one was open for 0% -> 0% of each run, Pallas kernels for 43% -> 45%
where the time goes in v4:
time: 171 us; the launch traced here: 170 us
  Pallas kernels  86.4 us (51%)
  starting transfers between devices  50.1 us (29%)
  waiting for transfers between devices  29.5 us (17%)
  local copies, waits for them, and re-layouts  3.16 us (2%)
    pallas_call x51, Pallas kernels, call(): pl.pallas_call(ordered, out_shape=out_shape, in_specs=in_specs + [ANY], o...  86.4 us
    ppermute x40, starting transfers between devices, swap(): return lax.ppermute(array, 'gx', [(i, i ^ 1 << bit) for i in range(8)])  49 us
    ppermute x40, waiting for transfers between devices, swap(): return lax.ppermute(array, 'gx', [(i, i ^ 1 << bit) for i in range(8)])  26 us
  transfers between devices with their start and end apart: 44, of which 16 were waited for; matrix products, arithmetic and copies ran while one was open for 0% of the time, Pallas kernels for 45%

profile of v4, /device:TPU:0, one launch (start us, length us, event | category | flops | bytes accessed | tf_op | source)
XLA Modules:
  0.0 170.5 jit_solution(11787458047797403245)
XLA Ops:
  0.0 1.5 slice_bitcast_fusion.1
  2.0 0.9 collective-permute-done
  2.9 3.9 %gate_up.12.refs_3_ = bf16[2,64,2048]{2,1,0:T(8,128)(2,1)S(1)} custom-call(bf16[64,1024]{1,0:T(8,128)(2,1)S(1)} %maximum_select_fusion.refs_0_.refs_3_, bf16[1024,13312]{1,0:T(8,128)(2,1)} %refs_0_.9, bf16[1024,13312]{1,0:T(8,128)(2,1)} %refs_1_.25, bf16[64,1024]{1,0:T(8,128)(2,1)S(1)} %maximum_select_fusion.refs_0_.refs_3_), custom_call_target="tpu_custom_call" | custom-call | tf_op jit(solution)/shard_map/gate_up/pallas_call | solution.py:40
  6.8 2.9 %collective-permute-start.2 = (bf16[2,64,2048]{2,1,0:T(8,128)(2,1)S(1)}, bf16[2,64,2048]{2,1,0:T(8,128)(2,1)S(1)}, u32[]{:S(2)}, u32[]{:S(2)}) collective-permute-start(bf16[2,64,2048]{2,1,0:T(8,128)(2,1)S(1)} %gate_up.12.refs_3_), channel_id=1, source_target_pairs={{0,2},{2,0},{4,6},{6,4},{8,10},{10,8},{12,14},{14,12},{1,3},{3,1},... | collective-permute-start | bytes 1572872 | tf_op jit(solution)/shard_map/ppermute | solution.py:21
  9.6 3.2 %gate_up.13.refs_3_ = bf16[2,64,1536]{2,1,0:T(8,128)(2,1)S(1)} custom-call(bf16[64,1024]{1,0:T(8,128)(2,1)S(1)} %maximum_select_fusion.refs_0_.refs_3_, bf16[1024,13312]{1,0:T(8,128)(2,1)} %refs_0_.9, bf16[1024,13312]{1,0:T(8,128)(2,1)} %refs_1_.25, bf16[2,64,2048]{2,1,0:T(8,128)(2,1)S(1)} %gate_up.12.refs_3_), custom_call_target="tpu_custom_call" | custom-call | tf_op jit(solution)/shard_map/gate_up/pallas_call | solution.py:40
  12.8 1.6 collective-permute-start.1
  14.5 3.2 %gate_up.14.refs_3_ = bf16[2,64,1536]{2,1,0:T(8,128)(2,1)S(1)} custom-call(bf16[64,1024]{1,0:T(8,128)(2,1)S(1)} %maximum_select_fusion.refs_0_.refs_3_, bf16[1024,13312]{1,0:T(8,128)(2,1)} %refs_0_.9, bf16[1024,13312]{1,0:T(8,128)(2,1)} %refs_1_.25, bf16[2,64,1536]{2,1,0:T(8,128)(2,1)S(1)} %gate_up.13.refs_3_), custom_call_target="tpu_custom_call" | custom-call | tf_op jit(solution)/shard_map/gate_up/pallas_call | solution.py:40
  17.7 0.6 collective-permute-start.3
  18.3 3.2 %gate_up.15.refs_3_ = bf16[2,64,1536]{2,1,0:T(8,128)(2,1)S(1)} custom-call(bf16[64,1024]{1,0:T(8,128)(2,1)S(1)} %maximum_select_fusion.refs_0_.refs_3_, bf16[1024,13312]{1,0:T(8,128)(2,1)} %refs_0_.9, bf16[1024,13312]{1,0:T(8,128)(2,1)} %refs_1_.25, bf16[2,64,1536]{2,1,0:T(8,128)(2,1)S(1)} %gate_up.14.refs_3_), custom_call_target="tpu_custom_call" | custom-call | tf_op jit(solution)/shard_map/gate_up/pallas_call | solution.py:40
  21.6 5.7 %gate_up.16 = (f32[2,64,2048]{2,1,0:T(8,128)S(1)}, f32[2,64,1536]{2,1,0:T(8,128)S(1)}) custom-call(bf16[64,1024]{1,0:T(8,128)(2,1)S(1)} %maximum_select_fusion.refs_0_.refs_3_, bf16[1024,13312]{1,0:T(8,128)(2,1)} %refs_0_.9, bf16[1024,13312]{1,0:T(8,128)(2,1)} %refs_1_.25, bf16[2,64,1536]{2,1,0:T(8,128)(2,1)S(1)} %gate_up.15.refs_3_), custom_call_target="tpu_custom_call" | custom-call | tf_op jit(solution)/shard_map/gate_up/pallas_call | solution.py:40
  27.5 2.0 %collective-permute-start.7 = (bf16[2,64,1024]{2,1,0:T(8,128)(2,1)S(1)}, bf16[2,64,1024]{2,1,0:T(8,128)(2,1)S(1)}, u32[]{:S(2)}, u32[]{:S(2)}) collective-permute-start(bf16[2,64,1024]{2,1,0:T(8,128)(2,1)S(1)} %get-tuple-element.71), channel_id=1, source_target_pairs={{0,4},{2,6},{4,0},{6,2},{8,12},{10,14},{12,8},{14,10},{1,5},{3,7},... | collective-permute-start | bytes 786440 | tf_op jit(solution)/shard_map/ppermute | solution.py:21
  29.6 1.6 collective-permute-start.8
  31.2 5.1 %gate_up.17 = (f32[2,64,1536]{2,1,0:T(8,128)S(1)}, f32[2,64,1536]{2,1,0:T(8,128)S(1)}) custom-call(bf16[64,1024]{1,0:T(8,128)(2,1)S(1)} %maximum_select_fusion.refs_0_.refs_3_, bf16[1024,13312]{1,0:T(8,128)(2,1)} %refs_0_.9, bf16[1024,13312]{1,0:T(8,128)(2,1)} %refs_1_.25, f32[2,64,768]{2,1,0:T(8,128)S(1)} %get-tuple-element.64.refs_3_.refs_1_), custom_call_target="tpu_custom_call" | custom-call | tf_op jit(solution)/shard_map/gate_up/pallas_call | solution.py:40
  36.6 0.6 collective-permute-start.6
  37.3 0.6 collective-permute-done.7.refs_2_
  38.0 2.6 %collective-permute-start.10 = (bf16[2,64,896]{2,1,0:T(8,128)(2,1)S(1)}, bf16[2,64,896]{2,1,0:T(8,128)(2,1)S(1)}, u32[]{:S(2)}, u32[]{:S(2)}) collective-permute-start(bf16[2,64,896]{2,1,0:T(8,128)(2,1)S(1)} %get-tuple-element.77), channel_id=1, source_target_pairs={{0,8},{2,10},{4,12},{6,14},{8,0},{10,2},{12,4},{14,6},{1,9},{3,11}... | collective-permute-start | bytes 688136 | tf_op jit(solution)/shard_map/ppermute | solution.py:21
  40.7 5.0 %fetch.5 = (bf16[4,512,1024]{2,1,0:T(8,128)(2,1)S(1)}, bf16[3,512,1024]{2,1,0:T(8,128)(2,1)S(1)}, bf16[3,512,1024]{2,1,0:T(8,128)(2,1)S(1)}, bf16[3,512,1024]{2,1,0:T(8,128)(2,1)S(1)}) custom-call(bf16[1024,13312]{1,0:T(8,128)(2,1)} %refs_0_.9, bf16[1024,13312]{1,0:T(8,128)(2,1)} %refs_1_.25, bf16[13312,1024]{1,0:T(8,128)(2,1)} %refs_3_.7, ...), custom_call_target="tpu_custom_call" | custom-call | tf_op jit(solution)/shard_map/fetch/pallas_call | solution.py:40
  45.7 1.6 copy-done.2
  47.8 5.4 %fetch.6 = (bf16[3,2,1024,512]{3,2,1,0:T(8,128)(2,1)S(1)}, bf16[3,2,1024,512]{3,2,1,0:T(8,128)(2,1)S(1)}) custom-call(bf16[1024,13312]{1,0:T(8,128)(2,1)} %refs_0_.9, bf16[1024,13312]{1,0:T(8,128)(2,1)} %refs_1_.25, bf16[13312,1024]{1,0:T(8,128)(2,1)} %refs_3_.7, f32[2,64,768]{2,1,0:T(8,128)S(1)} %get-tuple-element.75.refs_3_.refs_0_), custom_call_target="tpu_custom_call" | custom-call | tf_op jit(solution)/shard_map/fetch/pallas_call | solution.py:40
  53.4 2.1 %collective-permute-start.12 = (bf16[64,896]{1,0:T(8,128)(2,1)S(1)}, bf16[64,896]{1,0:T(8,128)(2,1)S(1)}, u32[]{:S(2)}, u32[]{:S(2)}) collective-permute-start(bf16[64,896]{1,0:T(8,128)(2,1)S(1)} %gated.4.refs_3_.refs_0_), channel_id=1, source_target_pairs={{0,8},{2,10},{4,12},{6,14},{8,0},{10,2},{12,4},{14,6},{1,9},{3,11}... | collective-permute-start | bytes 344072 | tf_op jit(solution)/shard_map/ppermute | solution.py:21
  55.4 5.4 %fetch.7 = (bf16[4,2,1024,512]{3,2,1,0:T(8,128)(2,1)S(1)}, bf16[3,2,1024,512]{3,2,1,0:T(8,128)(2,1)S(1)}) custom-call(bf16[1024,13312]{1,0:T(8,128)(2,1)} %refs_0_.9, bf16[1024,13312]{1,0:T(8,128)(2,1)} %refs_1_.25, bf16[13312,1024]{1,0:T(8,128)(2,1)} %refs_3_.7, bf16[64,896]{1,0:T(8,128)(2,1)S(1)} %gated.4.refs_3_.refs_0_), custom_call_target="tpu_custom_call" | custom-call | tf_op jit(solution)/shard_map/fetch/pallas_call | solution.py:40
  61.0 1.0 collective-permute-start.11
  62.2 5.7 %collective-permute-start.15 = (bf16[64,1024]{1,0:T(8,128)(2,1)S(1)}, bf16[64,1024]{1,0:T(8,128)(2,1)S(1)}, u32[]{:S(2)}, u32[]{:S(2)}) collective-permute-start(bf16[64,1024]{1,0:T(8,128)(2,1)S(1)} %get-tuple-element.80.refs_2_.refs_0_), channel_id=1, source_target_pairs={{0,4},{2,6},{4,0},{6,2},{8,12},{10,14},{12,8},{14,10},{1,5},{3,7},... | collective-permute-start | bytes 393224 | tf_op jit(solution)/shard_map/ppermute | solution.py:21
  68.4 5.6 %collective-permute-start.13 = (bf16[64,768]{1,0:T(8,128)(2,1)S(1)}, bf16[64,768]{1,0:T(8,128)(2,1)S(1)}, u32[]{:S(2)}, u32[]{:S(2)}) collective-permute-start(bf16[64,768]{1,0:T(8,128)(2,1)S(1)} %get-tuple-element.81.refs_2_.refs_0_), channel_id=1, source_target_pairs={{0,4},{2,6},{4,0},{6,2},{8,12},{10,14},{12,8},{14,10},{1,5},{3,7},... | collective-permute-start | bytes 294920 | tf_op jit(solution)/shard_map/ppermute | solution.py:21
  74.0 2.1 %collective-permute-start.19 = (bf16[64,2048]{1,0:T(8,128)(2,1)S(1)}, bf16[64,2048]{1,0:T(8,128)(2,1)S(1)}, u32[]{:S(2)}, u32[]{:S(2)}) collective-permute-start(bf16[64,2048]{1,0:T(8,128)(2,1)S(1)} %join.8.refs_2_.refs_0_), channel_id=1, source_target_pairs={{0,2},{2,0},{4,6},{6,4},{8,10},{10,8},{12,14},{14,12},{1,3},{3,1},... | collective-permute-start | bytes 786440 | tf_op jit(solution)/shard_map/ppermute | solution.py:21
  76.3 0.5 collective-permute-done.13.refs_1_
  76.8 1.7 %collective-permute-done.17.refs_1_ = bf16[64,768]{1,0:T(8,128)(2,1)S(1)} collective-permute-done((bf16[64,768]{1,0:T(8,128)(2,1)S(1)}, bf16[64,768]{1,0:T(8,128)(2,1)S(1)}, u32[]{:S(2)}, u32[]{:S(2)}) %collective-permute-start.17) | collective-permute-done | bytes 98336 | tf_op jit(solution)/shard_map/ppermute | solution.py:21
  79.2 5.6 %down.6.refs_2_.refs_6_ = f32[64,1024]{1,0:T(8,128)S(1)} custom-call(bf16[64,2048]{1,0:T(8,128)(2,1)S(1)} %join.8.refs_2_.refs_0_, bf16[64,1536]{1,0:T(8,128)(2,1)S(1)} %join.9.refs_2_.refs_1_, bf16[64,1536]{1,0:T(8,128)(2,1)S(1)} %join.10.refs_2_, bf16[64,1536]{1,0:T(8,128)(2,1)S(1)} %join.11.refs_3_.refs_5_, bf16[13312,1024]{1,0:T(8,128)(2,1)} %refs_3_.7, ...), custom_call_target="tpu_custom_call" | custom-call | tf_op jit(solution)/shard_map/down/pallas_call | solution.py:40
  84.9 2.1 %down.7.refs_2_.refs_6_ = f32[64,1024]{1,0:T(8,128)S(1)} custom-call(bf16[64,2048]{1,0:T(8,128)(2,1)S(1)} %collective-permute-done.19.refs_0_, bf16[64,1536]{1,0:T(8,128)(2,1)S(1)} %collective-permute-done.20.refs_1_, f32[64,1024]{1,0:T(8,128)S(1)} %down.6.refs_2_.refs_6_, bf16[13312,1024]{1,0:T(8,128)(2,1)} %refs_3_.7, ...), custom_call_target="tpu_custom_call" | custom-call | tf_op jit(solution)/shard_map/down/pallas_call | solution.py:40
  87.1 1.8 %down.8 = f32[64,1024]{1,0:T(8,128)S(1)} custom-call(bf16[64,1536]{1,0:T(8,128)(2,1)S(1)} %collective-permute-done.16.refs_0_, bf16[64,1536]{1,0:T(8,128)(2,1)S(1)} %collective-permute-done.18.refs_1_, f32[64,1024]{1,0:T(8,128)S(1)} %down.7.refs_2_.refs_6_, bf16[13312,1024]{1,0:T(8,128)(2,1)} %refs_3_.7, bf16[3,512,1024]{2,1,0:T(8,128)(2,1)S(1)} %copy-done.1, ...), custom_call_target="tpu_custom_call" | custom-call | tf_op jit(solution)/shard_map/down/pallas_call | solution.py:40
  89.5 1.1 collective-permute-done.22
  90.6 1.9 %gate_up.18.refs_2_ = bf16[2,64,2048]{2,1,0:T(8,128)(2,1)S(1)} custom-call(bf16[64,1024]{1,0:T(8,128)(2,1)S(1)} %get-tuple-element.117.refs_0_.refs_2_, bf16[4,2,1024,512]{3,2,1,0:T(8,128)(2,1)S(1)} %get-tuple-element.79.refs_2_.refs_1_, bf16[64,1024]{1,0:T(8,128)(2,1)S(1)} %get-tuple-element.117.refs_0_.refs_2_), custom_call_target="tpu_custom_call" | custom-call | tf_op jit(solution)/shard_map/gate_up/pallas_call | solution.py:40
  92.6 1.4 collective-permute-start.24
  93.9 1.4 gate_up.19.refs_2_
  95.4 2.0 %collective-permute-start.23 = (bf16[2,64,1536]{2,1,0:T(8,128)(2,1)S(1)}, bf16[2,64,1536]{2,1,0:T(8,128)(2,1)S(1)}, u32[]{:S(2)}, u32[]{:S(2)}) collective-permute-start(bf16[2,64,1536]{2,1,0:T(8,128)(2,1)S(1)} %gate_up.19.refs_2_), channel_id=1, source_target_pairs={{0,4},{2,6},{4,0},{6,2},{8,12},{10,14},{12,8},{14,10},{1,5},{3,7},... | collective-permute-start | bytes 1179656 | tf_op jit(solution)/shard_map/ppermute | solution.py:21
  97.4 1.4 gate_up.20.refs_2_
  99.0 1.4 gate_up.21.refs_3_
  100.5 0.7 collective-permute-start.26
  101.2 5.7 %gate_up.22 = (f32[2,64,2048]{2,1,0:T(8,128)S(1)}, f32[2,64,1536]{2,1,0:T(8,128)S(1)}) custom-call(bf16[64,1024]{1,0:T(8,128)(2,1)S(1)} %get-tuple-element.117.refs_0_.refs_2_, bf16[1024,13312]{1,0:T(8,128)(2,1)} %refs_0_.9, bf16[1024,13312]{1,0:T(8,128)(2,1)} %refs_1_.25, bf16[2,64,1536]{2,1,0:T(8,128)(2,1)S(1)} %gate_up.21.refs_3_), custom_call_target="tpu_custom_call" | custom-call | tf_op jit(solution)/shard_map/gate_up/pallas_call | solution.py:40
  107.5 1.4 collective-permute-start.29
  109.0 2.0 %collective-permute-start.30 = (bf16[2,64,768]{2,1,0:T(8,128)(2,1)S(1)}, bf16[2,64,768]{2,1,0:T(8,128)(2,1)S(1)}, u32[]{:S(2)}, u32[]{:S(2)}) collective-permute-start(bf16[2,64,768]{2,1,0:T(8,128)(2,1)S(1)} %get-tuple-element.100), channel_id=1, source_target_pairs={{0,2},{2,0},{4,6},{6,4},{8,10},{10,8},{12,14},{14,12},{1,3},{3,1},... | collective-permute-start | bytes 589832 | tf_op jit(solution)/shard_map/ppermute | solution.py:21
  110.9 5.1 %gate_up.23 = (f32[2,64,1536]{2,1,0:T(8,128)S(1)}, f32[2,64,1536]{2,1,0:T(8,128)S(1)}) custom-call(bf16[64,1024]{1,0:T(8,128)(2,1)S(1)} %get-tuple-element.117.refs_0_.refs_2_, bf16[1024,13312]{1,0:T(8,128)(2,1)} %refs_0_.9, bf16[1024,13312]{1,0:T(8,128)(2,1)} %refs_1_.25, f32[2,64,768]{2,1,0:T(8,128)S(1)} %get-tuple-element.92.refs_3_.refs_1_), custom_call_target="tpu_custom_call" | custom-call | tf_op jit(solution)/shard_map/gate_up/pallas_call | solution.py:40
  116.3 1.1 collective-permute-start.28
  117.4 1.9 %collective-permute-start.27 = (bf16[2,64,768]{2,1,0:T(8,128)(2,1)S(1)}, bf16[2,64,768]{2,1,0:T(8,128)(2,1)S(1)}, u32[]{:S(2)}, u32[]{:S(2)}) collective-permute-start(bf16[2,64,768]{2,1,0:T(8,128)(2,1)S(1)} %get-tuple-element.97), channel_id=1, source_target_pairs={{0,4},{2,6},{4,0},{6,2},{8,12},{10,14},{12,8},{14,10},{1,5},{3,7},... | collective-permute-start | bytes 589832 | tf_op jit(solution)/shard_map/ppermute | solution.py:21
  119.3 0.7 collective-permute-done.30.refs_3_
  120.0 1.4 collective-permute-done.29.refs_2_
  121.5 0.9 collective-permute-start.32
  122.5 5.0 %fetch.8 = (bf16[4,512,1024]{2,1,0:T(8,128)(2,1)S(1)}, bf16[3,512,1024]{2,1,0:T(8,128)(2,1)S(1)}, bf16[3,512,1024]{2,1,0:T(8,128)(2,1)S(1)}, bf16[3,512,1024]{2,1,0:T(8,128)(2,1)S(1)}) custom-call(bf16[1024,13312]{1,0:T(8,128)(2,1)} %refs_0_.9, bf16[1024,13312]{1,0:T(8,128)(2,1)} %refs_1_.25, bf16[13312,1024]{1,0:T(8,128)(2,1)} %refs_3_.7, ...), custom_call_target="tpu_custom_call" | custom-call | tf_op jit(solution)/shard_map/fetch/pallas_call | solution.py:40
  127.6 2.1 %collective-permute-start.31 = (bf16[2,64,768]{2,1,0:T(8,128)(2,1)S(1)}, bf16[2,64,768]{2,1,0:T(8,128)(2,1)S(1)}, u32[]{:S(2)}, u32[]{:S(2)}) collective-permute-start(bf16[2,64,768]{2,1,0:T(8,128)(2,1)S(1)} %get-tuple-element.104), channel_id=1, source_target_pairs={{0,8},{2,10},{4,12},{6,14},{8,0},{10,2},{12,4},{14,6},{1,9},{3,11}... | collective-permute-start | bytes 589832 | tf_op jit(solution)/shard_map/ppermute | solution.py:21
  129.7 5.0 %fetch.9 = (bf16[4,512,1024]{2,1,0:T(8,128)(2,1)S(1)}, bf16[3,512,1024]{2,1,0:T(8,128)(2,1)S(1)}, bf16[3,512,1024]{2,1,0:T(8,128)(2,1)S(1)}, bf16[3,512,1024]{2,1,0:T(8,128)(2,1)S(1)}) custom-call(bf16[1024,13312]{1,0:T(8,128)(2,1)} %refs_0_.9, bf16[1024,13312]{1,0:T(8,128)(2,1)} %refs_1_.25, bf16[13312,1024]{1,0:T(8,128)(2,1)} %refs_3_.7, ...), custom_call_target="tpu_custom_call" | custom-call | tf_op jit(solution)/shard_map/fetch/pallas_call | solution.py:40
  134.7 5.5 %collective-permute-done.32.refs_1_ = bf16[2,64,896]{2,1,0:T(8,128)(2,1)S(1)} collective-permute-done((bf16[2,64,896]{2,1,0:T(8,128)(2,1)S(1)}, bf16[2,64,896]{2,1,0:T(8,128)(2,1)S(1)}, u32[]{:S(2)}, u32[]{:S(2)}) %collective-permute-start.32) | collective-permute-done | bytes 229408 | tf_op jit(solution)/shard_map/ppermute | solution.py:21
  140.4 6.3 %collective-permute-done.31.refs_1_ = bf16[2,64,768]{2,1,0:T(8,128)(2,1)S(1)} collective-permute-done((bf16[2,64,768]{2,1,0:T(8,128)(2,1)S(1)}, bf16[2,64,768]{2,1,0:T(8,128)(2,1)S(1)}, u32[]{:S(2)}, u32[]{:S(2)}) %collective-permute-start.31) | collective-permute-done | bytes 196640 | tf_op jit(solution)/shard_map/ppermute | solution.py:21
  146.9 1.9 %collective-permute-done.34.refs_1_ = bf16[64,896]{1,0:T(8,128)(2,1)S(1)} collective-permute-done((bf16[64,896]{1,0:T(8,128)(2,1)S(1)}, bf16[64,896]{1,0:T(8,128)(2,1)S(1)}, u32[]{:S(2)}, u32[]{:S(2)}) %collective-permute-start.34) | collective-permute-done | bytes 114720 | tf_op jit(solution)/shard_map/ppermute | solution.py:21
  149.0 0.7 collective-permute-start.36
  149.7 2.8 %collective-permute-done.33.refs_1_ = bf16[64,768]{1,0:T(8,128)(2,1)S(1)} collective-permute-done((bf16[64,768]{1,0:T(8,128)(2,1)S(1)}, bf16[64,768]{1,0:T(8,128)(2,1)S(1)}, u32[]{:S(2)}, u32[]{:S(2)}) %collective-permute-start.33) | collective-permute-done | bytes 98336 | tf_op jit(solution)/shard_map/ppermute | solution.py:21
  153.0 2.3 %collective-permute-done.37.refs_1_ = bf16[64,1024]{1,0:T(8,128)(2,1)S(1)} collective-permute-done((bf16[64,1024]{1,0:T(8,128)(2,1)S(1)}, bf16[64,1024]{1,0:T(8,128)(2,1)S(1)}, u32[]{:S(2)}, u32[]{:S(2)}) %collective-permute-start.37) | collective-permute-done | bytes 131104 | tf_op jit(solution)/shard_map/ppermute | solution.py:21
  155.5 1.3 collective-permute-start.42
  156.8 1.5 collective-permute-done.35.refs_1_
  158.4 1.6 collective-permute-start.40
  160.2 3.9 %down.9.refs_2_.refs_6_ = f32[64,1024]{1,0:T(8,128)S(1)} custom-call(bf16[64,2048]{1,0:T(8,128)(2,1)S(1)} %join.12.refs_2_.refs_0_, bf16[64,1536]{1,0:T(8,128)(2,1)S(1)} %join.13.refs_2_.refs_1_, bf16[64,1536]{1,0:T(8,128)(2,1)S(1)} %join.14.refs_2_, bf16[64,1536]{1,0:T(8,128)(2,1)S(1)} %join.15.refs_3_.refs_9_, bf16[13312,1024]{1,0:T(8,128)(2,1)} %refs_3_.7, ...), custom_call_target="tpu_custom_call" | custom-call | tf_op jit(solution)/shard_map/down/pallas_call | solution.py:40
  164.2 2.1 %down.10.refs_2_.refs_6_ = f32[64,1024]{1,0:T(8,128)S(1)} custom-call(bf16[64,2048]{1,0:T(8,128)(2,1)S(1)} %collective-permute-done.41.refs_0_, bf16[64,1536]{1,0:T(8,128)(2,1)S(1)} %collective-permute-done.42.refs_1_, f32[64,1024]{1,0:T(8,128)S(1)} %down.9.refs_2_.refs_6_, bf16[13312,1024]{1,0:T(8,128)(2,1)} %refs_3_.7, ...), custom_call_target="tpu_custom_call" | custom-call | tf_op jit(solution)/shard_map/down/pallas_call | solution.py:40
  166.3 1.8 %down.11 = f32[64,1024]{1,0:T(8,128)S(1)} custom-call(bf16[64,1536]{1,0:T(8,128)(2,1)S(1)} %collective-permute-done.38.refs_0_, bf16[64,1536]{1,0:T(8,128)(2,1)S(1)} %collective-permute-done.40.refs_1_, f32[64,1024]{1,0:T(8,128)S(1)} %down.10.refs_2_.refs_6_, bf16[13312,1024]{1,0:T(8,128)(2,1)} %refs_3_.7, ...), custom_call_target="tpu_custom_call" | custom-call | tf_op jit(solution)/shard_map/down/pallas_call | solution.py:40
  168.2 1.5 collective-permute-done.43
  169.8 0.7 fusion.1
  (90 shorter events, 7.0 us)
Async XLA Ops:
  1.5 1.4 collective-permute-start
  6.8 20.6 %collective-permute-start.2 = (bf16[2,64,2048]{2,1,0:T(8,128)(2,1)S(1)}, bf16[2,64,2048]{2,1,0:T(8,128)(2,1)S(1)}, u32[]{:S(2)}, u32[]{:S(2)}) collective-permute-start(bf16[2,64,2048]{2,1,0:T(8,128)(2,1)S(1)} %gate_up.12.refs_3_), channel_id=1, source_target_pairs={{0,2},{2,0},{4,6},{6,4},{8,10},{10,8},{12,14},{14,12},{1,3},{3,1},... | collective-permute-start | bytes 1572872 | tf_op jit(solution)/shard_map/ppermute | solution.py:21
  12.8 16.7 %collective-permute-start.1 = (bf16[2,64,1536]{2,1,0:T(8,128)(2,1)S(1)}, bf16[2,64,1536]{2,1,0:T(8,128)(2,1)S(1)}, u32[]{:S(2)}, u32[]{:S(2)}) collective-permute-start(bf16[2,64,1536]{2,1,0:T(8,128)(2,1)S(1)} %gate_up.13.refs_3_), channel_id=1, source_target_pairs={{0,4},{2,6},{4,0},{6,2},{8,12},{10,14},{12,8},{14,10},{1,5},{3,7},... | collective-permute-start | bytes 1179656 | tf_op jit(solution)/shard_map/ppermute | solution.py:21
  17.7 18.7 %collective-permute-start.3 = (bf16[2,64,1536]{2,1,0:T(8,128)(2,1)S(1)}, bf16[2,64,1536]{2,1,0:T(8,128)(2,1)S(1)}, u32[]{:S(2)}, u32[]{:S(2)}) collective-permute-start(bf16[2,64,1536]{2,1,0:T(8,128)(2,1)S(1)} %gate_up.14.refs_3_), channel_id=1, source_target_pairs={{0,2},{2,0},{4,6},{6,4},{8,10},{10,8},{12,14},{14,12},{1,3},{3,1},... | collective-permute-start | bytes 1179656 | tf_op jit(solution)/shard_map/ppermute | solution.py:21
  21.5 14.9 %collective-permute-start.4 = (bf16[2,64,1536]{2,1,0:T(8,128)(2,1)S(1)}, bf16[2,64,1536]{2,1,0:T(8,128)(2,1)S(1)}, u32[]{:S(2)}, u32[]{:S(2)}) collective-permute-start(bf16[2,64,1536]{2,1,0:T(8,128)(2,1)S(1)} %gate_up.15.refs_3_), channel_id=1, source_target_pairs={{0,4},{2,6},{4,0},{6,2},{8,12},{10,14},{12,8},{14,10},{1,5},{3,7},... | collective-permute-start | bytes 1179656 | tf_op jit(solution)/shard_map/ppermute | solution.py:21
  27.5 10.5 %collective-permute-start.7 = (bf16[2,64,1024]{2,1,0:T(8,128)(2,1)S(1)}, bf16[2,64,1024]{2,1,0:T(8,128)(2,1)S(1)}, u32[]{:S(2)}, u32[]{:S(2)}) collective-permute-start(bf16[2,64,1024]{2,1,0:T(8,128)(2,1)S(1)} %get-tuple-element.71), channel_id=1, source_target_pairs={{0,4},{2,6},{4,0},{6,2},{8,12},{10,14},{12,8},{14,10},{1,5},{3,7},... | collective-permute-start | bytes 786440 | tf_op jit(solution)/shard_map/ppermute | solution.py:21
  29.6 7.7 %collective-permute-start.8 = (bf16[2,64,768]{2,1,0:T(8,128)(2,1)S(1)}, bf16[2,64,768]{2,1,0:T(8,128)(2,1)S(1)}, u32[]{:S(2)}, u32[]{:S(2)}) collective-permute-start(bf16[2,64,768]{2,1,0:T(8,128)(2,1)S(1)} %get-tuple-element.72), channel_id=1, source_target_pairs={{0,2},{2,0},{4,6},{6,4},{8,10},{10,8},{12,14},{14,12},{1,3},{3,1},... | collective-permute-start | bytes 589832 | tf_op jit(solution)/shard_map/ppermute | solution.py:21
  36.6 10.8 %collective-permute-start.6 = (bf16[2,64,768]{2,1,0:T(8,128)(2,1)S(1)}, bf16[2,64,768]{2,1,0:T(8,128)(2,1)S(1)}, u32[]{:S(2)}, u32[]{:S(2)}) collective-permute-start(bf16[2,64,768]{2,1,0:T(8,128)(2,1)S(1)} %get-tuple-element.70), channel_id=1, source_target_pairs={{0,2},{2,0},{4,6},{6,4},{8,10},{10,8},{12,14},{14,12},{1,3},{3,1},... | collective-permute-start | bytes 589832 | tf_op jit(solution)/shard_map/ppermute | solution.py:21
  37.1 10.2 %collective-permute-start.5 = (bf16[2,64,768]{2,1,0:T(8,128)(2,1)S(1)}, bf16[2,64,768]{2,1,0:T(8,128)(2,1)S(1)}, u32[]{:S(2)}, u32[]{:S(2)}) collective-permute-start(bf16[2,64,768]{2,1,0:T(8,128)(2,1)S(1)} %get-tuple-element.69), channel_id=1, source_target_pairs={{0,4},{2,6},{4,0},{6,2},{8,12},{10,14},{12,8},{14,10},{1,5},{3,7},... | collective-permute-start | bytes 589832 | tf_op jit(solution)/shard_map/ppermute | solution.py:21
  38.0 15.2 %collective-permute-start.10 = (bf16[2,64,896]{2,1,0:T(8,128)(2,1)S(1)}, bf16[2,64,896]{2,1,0:T(8,128)(2,1)S(1)}, u32[]{:S(2)}, u32[]{:S(2)}) collective-permute-start(bf16[2,64,896]{2,1,0:T(8,128)(2,1)S(1)} %get-tuple-element.77), channel_id=1, source_target_pairs={{0,8},{2,10},{4,12},{6,14},{8,0},{10,2},{12,4},{14,6},{1,9},{3,11}... | collective-permute-start | bytes 688136 | tf_op jit(solution)/shard_map/ppermute | solution.py:21
  45.7 1.6 copy-start.2
  47.3 5.9 %copy-start = (bf16[3,512,1024]{2,1,0:T(8,128)(2,1)}, bf16[3,512,1024]{2,1,0:T(8,128)(2,1)S(1)}, u32[]{:S(2)}) copy-start(bf16[3,512,1024]{2,1,0:T(8,128)(2,1)S(1)} %get-tuple-element.85.refs_4_) | copy-start | bytes 9437188
  47.4 13.4 %collective-permute-start.9 = (bf16[2,64,768]{2,1,0:T(8,128)(2,1)S(1)}, bf16[2,64,768]{2,1,0:T(8,128)(2,1)S(1)}, u32[]{:S(2)}, u32[]{:S(2)}) collective-permute-start(bf16[2,64,768]{2,1,0:T(8,128)(2,1)S(1)} %get-tuple-element.76), channel_id=1, source_target_pairs={{0,8},{2,10},{4,12},{6,14},{8,0},{10,2},{12,4},{14,6},{1,9},{3,11}... | collective-permute-start | bytes 589832 | tf_op jit(solution)/shard_map/ppermute | solution.py:21
  53.4 8.8 %collective-permute-start.12 = (bf16[64,896]{1,0:T(8,128)(2,1)S(1)}, bf16[64,896]{1,0:T(8,128)(2,1)S(1)}, u32[]{:S(2)}, u32[]{:S(2)}) collective-permute-start(bf16[64,896]{1,0:T(8,128)(2,1)S(1)} %gated.4.refs_3_.refs_0_), channel_id=1, source_target_pairs={{0,8},{2,10},{4,12},{6,14},{8,0},{10,2},{12,4},{14,6},{1,9},{3,11}... | collective-permute-start | bytes 344072 | tf_op jit(solution)/shard_map/ppermute | solution.py:21
  61.0 7.4 %collective-permute-start.11 = (bf16[64,768]{1,0:T(8,128)(2,1)S(1)}, bf16[64,768]{1,0:T(8,128)(2,1)S(1)}, u32[]{:S(2)}, u32[]{:S(2)}) collective-permute-start(bf16[64,768]{1,0:T(8,128)(2,1)S(1)} %gated.5.refs_2_.refs_0_), channel_id=1, source_target_pairs={{0,8},{2,10},{4,12},{6,14},{8,0},{10,2},{12,4},{14,6},{1,9},{3,11}... | collective-permute-start | bytes 294920 | tf_op jit(solution)/shard_map/ppermute | solution.py:21
  62.2 11.8 %collective-permute-start.15 = (bf16[64,1024]{1,0:T(8,128)(2,1)S(1)}, bf16[64,1024]{1,0:T(8,128)(2,1)S(1)}, u32[]{:S(2)}, u32[]{:S(2)}) collective-permute-start(bf16[64,1024]{1,0:T(8,128)(2,1)S(1)} %get-tuple-element.80.refs_2_.refs_0_), channel_id=1, source_target_pairs={{0,4},{2,6},{4,0},{6,2},{8,12},{10,14},{12,8},{14,10},{1,5},{3,7},... | collective-permute-start | bytes 393224 | tf_op jit(solution)/shard_map/ppermute | solution.py:21
  67.9 8.2 %collective-permute-start.14 = (bf16[64,768]{1,0:T(8,128)(2,1)S(1)}, bf16[64,768]{1,0:T(8,128)(2,1)S(1)}, u32[]{:S(2)}, u32[]{:S(2)}) collective-permute-start(bf16[64,768]{1,0:T(8,128)(2,1)S(1)} %get-tuple-element.82.refs_0_), channel_id=1, source_target_pairs={{0,2},{2,0},{4,6},{6,4},{8,10},{10,8},{12,14},{14,12},{1,3},{3,1},... | collective-permute-start | bytes 294920 | tf_op jit(solution)/shard_map/ppermute | solution.py:21
  68.4 8.4 %collective-permute-start.13 = (bf16[64,768]{1,0:T(8,128)(2,1)S(1)}, bf16[64,768]{1,0:T(8,128)(2,1)S(1)}, u32[]{:S(2)}, u32[]{:S(2)}) collective-permute-start(bf16[64,768]{1,0:T(8,128)(2,1)S(1)} %get-tuple-element.81.refs_2_.refs_0_), channel_id=1, source_target_pairs={{0,4},{2,6},{4,0},{6,2},{8,12},{10,14},{12,8},{14,10},{1,5},{3,7},... | collective-permute-start | bytes 294920 | tf_op jit(solution)/shard_map/ppermute | solution.py:21
  74.0 4.6 %collective-permute-start.17 = (bf16[64,768]{1,0:T(8,128)(2,1)S(1)}, bf16[64,768]{1,0:T(8,128)(2,1)S(1)}, u32[]{:S(2)}, u32[]{:S(2)}) collective-permute-start(bf16[64,768]{1,0:T(8,128)(2,1)S(1)} %get-tuple-element.83.refs_0_), channel_id=1, source_target_pairs={{0,2},{2,0},{4,6},{6,4},{8,10},{10,8},{12,14},{14,12},{1,3},{3,1},... | collective-permute-start | bytes 294920 | tf_op jit(solution)/shard_map/ppermute | solution.py:21
  74.0 10.9 %collective-permute-start.19 = (bf16[64,2048]{1,0:T(8,128)(2,1)S(1)}, bf16[64,2048]{1,0:T(8,128)(2,1)S(1)}, u32[]{:S(2)}, u32[]{:S(2)}) collective-permute-start(bf16[64,2048]{1,0:T(8,128)(2,1)S(1)} %join.8.refs_2_.refs_0_), channel_id=1, source_target_pairs={{0,2},{2,0},{4,6},{6,4},{8,10},{10,8},{12,14},{14,12},{1,3},{3,1},... | collective-permute-start | bytes 786440 | tf_op jit(solution)/shard_map/ppermute | solution.py:21
  76.1 8.7 %collective-permute-start.20 = (bf16[64,1536]{1,0:T(8,128)(2,1)S(1)}, bf16[64,1536]{1,0:T(8,128)(2,1)S(1)}, u32[]{:S(2)}, u32[]{:S(2)}) collective-permute-start(bf16[64,1536]{1,0:T(8,128)(2,1)S(1)} %join.9.refs_2_.refs_1_), channel_id=1, source_target_pairs={{0,4},{2,6},{4,0},{6,2},{8,12},{10,14},{12,8},{14,10},{1,5},{3,7},... | collective-permute-start | bytes 589832 | tf_op jit(solution)/shard_map/ppermute | solution.py:21
  78.6 6.3 %copy-start.3 = (bf16[3,512,1024]{2,1,0:T(8,128)(2,1)S(1)}, bf16[3,512,1024]{2,1,0:T(8,128)(2,1)}, u32[]{:S(2)}) copy-start(bf16[3,512,1024]{2,1,0:T(8,128)(2,1)} %copy-done.2) | copy-start | bytes 9437188
  78.6 8.4 %collective-permute-start.18 = (bf16[64,1536]{1,0:T(8,128)(2,1)S(1)}, bf16[64,1536]{1,0:T(8,128)(2,1)S(1)}, u32[]{:S(2)}, u32[]{:S(2)}) collective-permute-start(bf16[64,1536]{1,0:T(8,128)(2,1)S(1)} %join.11.refs_3_.refs_5_), channel_id=1, source_target_pairs={{0,4},{2,6},{4,0},{6,2},{8,12},{10,14},{12,8},{14,10},{1,5},{3,7},... | collective-permute-start | bytes 589832 | tf_op jit(solution)/shard_map/ppermute | solution.py:21
  78.8 8.3 %collective-permute-start.16 = (bf16[64,1536]{1,0:T(8,128)(2,1)S(1)}, bf16[64,1536]{1,0:T(8,128)(2,1)S(1)}, u32[]{:S(2)}, u32[]{:S(2)}) collective-permute-start(bf16[64,1536]{1,0:T(8,128)(2,1)S(1)} %join.10.refs_2_), channel_id=1, source_target_pairs={{0,2},{2,0},{4,6},{6,4},{8,10},{10,8},{12,14},{14,12},{1,3},{3,1},... | collective-permute-start | bytes 589832 | tf_op jit(solution)/shard_map/ppermute | solution.py:21
  84.9 2.2 %copy-start.1 = (bf16[3,512,1024]{2,1,0:T(8,128)(2,1)S(1)}, bf16[3,512,1024]{2,1,0:T(8,128)(2,1)}, u32[]{:S(2)}) copy-start(bf16[3,512,1024]{2,1,0:T(8,128)(2,1)} %copy-done) | copy-start | bytes 9437188
  87.1 1.9 %copy-start.4 = (bf16[32,1024]{1,0:T(8,128)(2,1)S(1)}, bf16[32,1024]{1,0:T(8,128)(2,1)}, u32[]{:S(2)}) copy-start(bf16[32,1024]{1,0:T(8,128)(2,1)} %get-tuple-element.120) | copy-start | bytes 196612
  88.9 1.7 collective-permute-start.21
  89.0 1.6 collective-permute-start.22
  92.6 14.8 %collective-permute-start.24 = (bf16[2,64,2048]{2,1,0:T(8,128)(2,1)S(1)}, bf16[2,64,2048]{2,1,0:T(8,128)(2,1)S(1)}, u32[]{:S(2)}, u32[]{:S(2)}) collective-permute-start(bf16[2,64,2048]{2,1,0:T(8,128)(2,1)S(1)} %gate_up.18.refs_2_), channel_id=1, source_target_pairs={{0,2},{2,0},{4,6},{6,4},{8,10},{10,8},{12,14},{14,12},{1,3},{3,1},... | collective-permute-start | bytes 1572872 | tf_op jit(solution)/shard_map/ppermute | solution.py:21
  95.4 13.5 %collective-permute-start.23 = (bf16[2,64,1536]{2,1,0:T(8,128)(2,1)S(1)}, bf16[2,64,1536]{2,1,0:T(8,128)(2,1)S(1)}, u32[]{:S(2)}, u32[]{:S(2)}) collective-permute-start(bf16[2,64,1536]{2,1,0:T(8,128)(2,1)S(1)} %gate_up.19.refs_2_), channel_id=1, source_target_pairs={{0,4},{2,6},{4,0},{6,2},{8,12},{10,14},{12,8},{14,10},{1,5},{3,7},... | collective-permute-start | bytes 1179656 | tf_op jit(solution)/shard_map/ppermute | solution.py:21
  98.8 17.3 %collective-permute-start.25 = (bf16[2,64,1536]{2,1,0:T(8,128)(2,1)S(1)}, bf16[2,64,1536]{2,1,0:T(8,128)(2,1)S(1)}, u32[]{:S(2)}, u32[]{:S(2)}) collective-permute-start(bf16[2,64,1536]{2,1,0:T(8,128)(2,1)S(1)} %gate_up.20.refs_2_), channel_id=1, source_target_pairs={{0,2},{2,0},{4,6},{6,4},{8,10},{10,8},{12,14},{14,12},{1,3},{3,1},... | collective-permute-start | bytes 1179656 | tf_op jit(solution)/shard_map/ppermute | solution.py:21
  100.5 15.7 %collective-permute-start.26 = (bf16[2,64,1536]{2,1,0:T(8,128)(2,1)S(1)}, bf16[2,64,1536]{2,1,0:T(8,128)(2,1)S(1)}, u32[]{:S(2)}, u32[]{:S(2)}) collective-permute-start(bf16[2,64,1536]{2,1,0:T(8,128)(2,1)S(1)} %gate_up.21.refs_3_), channel_id=1, source_target_pairs={{0,4},{2,6},{4,0},{6,2},{8,12},{10,14},{12,8},{14,10},{1,5},{3,7},... | collective-permute-start | bytes 1179656 | tf_op jit(solution)/shard_map/ppermute | solution.py:21
  107.5 14.0 %collective-permute-start.29 = (bf16[2,64,1024]{2,1,0:T(8,128)(2,1)S(1)}, bf16[2,64,1024]{2,1,0:T(8,128)(2,1)S(1)}, u32[]{:S(2)}, u32[]{:S(2)}) collective-permute-start(bf16[2,64,1024]{2,1,0:T(8,128)(2,1)S(1)} %get-tuple-element.99), channel_id=1, source_target_pairs={{0,4},{2,6},{4,0},{6,2},{8,12},{10,14},{12,8},{14,10},{1,5},{3,7},... | collective-permute-start | bytes 786440 | tf_op jit(solution)/shard_map/ppermute | solution.py:21
  109.0 11.1 %collective-permute-start.30 = (bf16[2,64,768]{2,1,0:T(8,128)(2,1)S(1)}, bf16[2,64,768]{2,1,0:T(8,128)(2,1)S(1)}, u32[]{:S(2)}, u32[]{:S(2)}) collective-permute-start(bf16[2,64,768]{2,1,0:T(8,128)(2,1)S(1)} %get-tuple-element.100), channel_id=1, source_target_pairs={{0,2},{2,0},{4,6},{6,4},{8,10},{10,8},{12,14},{14,12},{1,3},{3,1},... | collective-permute-start | bytes 589832 | tf_op jit(solution)/shard_map/ppermute | solution.py:21
  116.3 11.2 %collective-permute-start.28 = (bf16[2,64,768]{2,1,0:T(8,128)(2,1)S(1)}, bf16[2,64,768]{2,1,0:T(8,128)(2,1)S(1)}, u32[]{:S(2)}, u32[]{:S(2)}) collective-permute-start(bf16[2,64,768]{2,1,0:T(8,128)(2,1)S(1)} %get-tuple-element.98), channel_id=1, source_target_pairs={{0,2},{2,0},{4,6},{6,4},{8,10},{10,8},{12,14},{14,12},{1,3},{3,1},... | collective-permute-start | bytes 589832 | tf_op jit(solution)/shard_map/ppermute | solution.py:21
  117.4 10.1 %collective-permute-start.27 = (bf16[2,64,768]{2,1,0:T(8,128)(2,1)S(1)}, bf16[2,64,768]{2,1,0:T(8,128)(2,1)S(1)}, u32[]{:S(2)}, u32[]{:S(2)}) collective-permute-start(bf16[2,64,768]{2,1,0:T(8,128)(2,1)S(1)} %get-tuple-element.97), channel_id=1, source_target_pairs={{0,4},{2,6},{4,0},{6,2},{8,12},{10,14},{12,8},{14,10},{1,5},{3,7},... | collective-permute-start | bytes 589832 | tf_op jit(solution)/shard_map/ppermute | solution.py:21
  121.5 18.7 %collective-permute-start.32 = (bf16[2,64,896]{2,1,0:T(8,128)(2,1)S(1)}, bf16[2,64,896]{2,1,0:T(8,128)(2,1)S(1)}, u32[]{:S(2)}, u32[]{:S(2)}) collective-permute-start(bf16[2,64,896]{2,1,0:T(8,128)(2,1)S(1)} %get-tuple-element.105), channel_id=1, source_target_pairs={{0,8},{2,10},{4,12},{6,14},{8,0},{10,2},{12,4},{14,6},{1,9},{3,11}... | collective-permute-start | bytes 688136 | tf_op jit(solution)/shard_map/ppermute | solution.py:21
  127.6 19.1 %collective-permute-start.31 = (bf16[2,64,768]{2,1,0:T(8,128)(2,1)S(1)}, bf16[2,64,768]{2,1,0:T(8,128)(2,1)S(1)}, u32[]{:S(2)}, u32[]{:S(2)}) collective-permute-start(bf16[2,64,768]{2,1,0:T(8,128)(2,1)S(1)} %get-tuple-element.104), channel_id=1, source_target_pairs={{0,8},{2,10},{4,12},{6,14},{8,0},{10,2},{12,4},{14,6},{1,9},{3,11}... | collective-permute-start | bytes 589832 | tf_op jit(solution)/shard_map/ppermute | solution.py:21
  140.3 8.4 %collective-permute-start.34 = (bf16[64,896]{1,0:T(8,128)(2,1)S(1)}, bf16[64,896]{1,0:T(8,128)(2,1)S(1)}, u32[]{:S(2)}, u32[]{:S(2)}) collective-permute-start(bf16[64,896]{1,0:T(8,128)(2,1)S(1)} %gated.6.refs_2_.refs_0_), channel_id=1, source_target_pairs={{0,8},{2,10},{4,12},{6,14},{8,0},{10,2},{12,4},{14,6},{1,9},{3,11}... | collective-permute-start | bytes 344072 | tf_op jit(solution)/shard_map/ppermute | solution.py:21
  146.8 5.7 %collective-permute-start.33 = (bf16[64,768]{1,0:T(8,128)(2,1)S(1)}, bf16[64,768]{1,0:T(8,128)(2,1)S(1)}, u32[]{:S(2)}, u32[]{:S(2)}) collective-permute-start(bf16[64,768]{1,0:T(8,128)(2,1)S(1)} %gated.7.refs_2_.refs_0_), channel_id=1, source_target_pairs={{0,8},{2,10},{4,12},{6,14},{8,0},{10,2},{12,4},{14,6},{1,9},{3,11}... | collective-permute-start | bytes 294920 | tf_op jit(solution)/shard_map/ppermute | solution.py:21
  148.8 6.5 %collective-permute-start.37 = (bf16[64,1024]{1,0:T(8,128)(2,1)S(1)}, bf16[64,1024]{1,0:T(8,128)(2,1)S(1)}, u32[]{:S(2)}, u32[]{:S(2)}) collective-permute-start(bf16[64,1024]{1,0:T(8,128)(2,1)S(1)} %get-tuple-element.107.refs_2_.refs_0_), channel_id=1, source_target_pairs={{0,4},{2,6},{4,0},{6,2},{8,12},{10,14},{12,8},{14,10},{1,5},{3,7},... | collective-permute-start | bytes 393224 | tf_op jit(solution)/shard_map/ppermute | solution.py:21
  149.0 6.4 %collective-permute-start.36 = (bf16[64,768]{1,0:T(8,128)(2,1)S(1)}, bf16[64,768]{1,0:T(8,128)(2,1)S(1)}, u32[]{:S(2)}, u32[]{:S(2)}) collective-permute-start(bf16[64,768]{1,0:T(8,128)(2,1)S(1)} %get-tuple-element.109.refs_0_), channel_id=1, source_target_pairs={{0,2},{2,0},{4,6},{6,4},{8,10},{10,8},{12,14},{14,12},{1,3},{3,1},... | collective-permute-start | bytes 294920 | tf_op jit(solution)/shard_map/ppermute | solution.py:21
  152.5 5.8 %collective-permute-start.35 = (bf16[64,768]{1,0:T(8,128)(2,1)S(1)}, bf16[64,768]{1,0:T(8,128)(2,1)S(1)}, u32[]{:S(2)}, u32[]{:S(2)}) collective-permute-start(bf16[64,768]{1,0:T(8,128)(2,1)S(1)} %get-tuple-element.108.refs_2_.refs_0_), channel_id=1, source_target_pairs={{0,4},{2,6},{4,0},{6,2},{8,12},{10,14},{12,8},{14,10},{1,5},{3,7},... | collective-permute-start | bytes 294920 | tf_op jit(solution)/shard_map/ppermute | solution.py:21
  152.6 5.8 %collective-permute-start.39 = (bf16[64,768]{1,0:T(8,128)(2,1)S(1)}, bf16[64,768]{1,0:T(8,128)(2,1)S(1)}, u32[]{:S(2)}, u32[]{:S(2)}) collective-permute-start(bf16[64,768]{1,0:T(8,128)(2,1)S(1)} %get-tuple-element.110.refs_0_), channel_id=1, source_target_pairs={{0,2},{2,0},{4,6},{6,4},{8,10},{10,8},{12,14},{14,12},{1,3},{3,1},... | collective-permute-start | bytes 294920 | tf_op jit(solution)/shard_map/ppermute | solution.py:21
  155.3 8.9 %collective-permute-start.41 = (bf16[64,2048]{1,0:T(8,128)(2,1)S(1)}, bf16[64,2048]{1,0:T(8,128)(2,1)S(1)}, u32[]{:S(2)}, u32[]{:S(2)}) collective-permute-start(bf16[64,2048]{1,0:T(8,128)(2,1)S(1)} %join.12.refs_2_.refs_0_), channel_id=1, source_target_pairs={{0,2},{2,0},{4,6},{6,4},{8,10},{10,8},{12,14},{14,12},{1,3},{3,1},... | collective-permute-start | bytes 786440 | tf_op jit(solution)/shard_map/ppermute | solution.py:21
  155.5 8.7 %collective-permute-start.42 = (bf16[64,1536]{1,0:T(8,128)(2,1)S(1)}, bf16[64,1536]{1,0:T(8,128)(2,1)S(1)}, u32[]{:S(2)}, u32[]{:S(2)}) collective-permute-start(bf16[64,1536]{1,0:T(8,128)(2,1)S(1)} %join.13.refs_2_.refs_1_), channel_id=1, source_target_pairs={{0,4},{2,6},{4,0},{6,2},{8,12},{10,14},{12,8},{14,10},{1,5},{3,7},... | collective-permute-start | bytes 589832 | tf_op jit(solution)/shard_map/ppermute | solution.py:21
  158.4 7.9 %collective-permute-start.40 = (bf16[64,1536]{1,0:T(8,128)(2,1)S(1)}, bf16[64,1536]{1,0:T(8,128)(2,1)S(1)}, u32[]{:S(2)}, u32[]{:S(2)}) collective-permute-start(bf16[64,1536]{1,0:T(8,128)(2,1)S(1)} %join.15.refs_3_.refs_9_), channel_id=1, source_target_pairs={{0,4},{2,6},{4,0},{6,2},{8,12},{10,14},{12,8},{14,10},{1,5},{3,7},... | collective-permute-start | bytes 589832 | tf_op jit(solution)/shard_map/ppermute | solution.py:21
  160.0 6.3 %collective-permute-start.38 = (bf16[64,1536]{1,0:T(8,128)(2,1)S(1)}, bf16[64,1536]{1,0:T(8,128)(2,1)S(1)}, u32[]{:S(2)}, u32[]{:S(2)}) collective-permute-start(bf16[64,1536]{1,0:T(8,128)(2,1)S(1)} %join.14.refs_2_), channel_id=1, source_target_pairs={{0,2},{2,0},{4,6},{6,4},{8,10},{10,8},{12,14},{14,12},{1,3},{3,1},... | collective-permute-start | bytes 589832 | tf_op jit(solution)/shard_map/ppermute | solution.py:21
  168.2 1.6 collective-permute-start.43

commit v5 on v4

--- a/solution.py
+++ b/solution.py
@@ -14,7 +14,7 @@
 VMEM = pl.BlockSpec(memory_space=pltpu.VMEM)
 ANY = pl.BlockSpec(memory_space=pl.ANY)
 HBM = pl.BlockSpec(memory_space=pltpu.HBM)
-PARAMS = pltpu.CompilerParams(vmem_limit_bytes=18 * 2**20)
+PARAMS = pltpu.CompilerParams(vmem_limit_bytes=16 * 2**20)
 
 
 def swap(array, bit):

time: 171 us -> 170 us (level)
  starting transfers between devices: 50.1 us -> 54 us
  waiting for transfers between devices: 29.5 us -> 27.6 us
    ppermute x40, starting transfers between devices: 49 us -> 52.9 us  [swap(): return lax.ppermute(array, 'gx', [(i, i ^ 1 << bit) for i in range(8)])]
    ppermute x40, waiting for transfers between devices: 26 us -> 24.1 us  [swap(): return lax.ppermute(array, 'gx', [(i, i ^ 1 << bit) for i in range(8)])]
  transfers between devices with their start and end apart: 44 -> 44, of which waited for: 16 -> 15; matrix products, arithmetic and copies ran while one was open for 0% -> 0% of each run, Pallas kernels for 45% -> 45%
where the time goes in v5:
time: 170 us
  Pallas kernels  85.5 us (50%)
  starting transfers between devices  54 us (32%)
  waiting for transfers between devices  27.6 us (16%)
    pallas_call x51, Pallas kernels, call(): pl.pallas_call(ordered, out_shape=out_shape, in_specs=in_specs + [ANY], o...  85.5 us
    ppermute x40, starting transfers between devices, swap(): return lax.ppermute(array, 'gx', [(i, i ^ 1 << bit) for i in range(8)])  52.9 us
    ppermute x40, waiting for transfers between devices, swap(): return lax.ppermute(array, 'gx', [(i, i ^ 1 << bit) for i in range(8)])  24.1 us
  transfers between devices with their start and end apart: 44, of which 15 were waited for; matrix products, arithmetic and copies ran while one was open for 0% of the time, Pallas kernels for 45%

profile of v5, /device:TPU:0, one launch (start us, length us, event | category | flops | bytes accessed | tf_op | source)
XLA Modules:
  0.0 169.9 jit_solution(17083873219100718997)
XLA Ops:
  0.0 1.5 slice_bitcast_fusion.1
  2.0 0.9 collective-permute-done
  2.9 3.9 %gate_up.12.refs_3_ = bf16[2,64,2048]{2,1,0:T(8,128)(2,1)S(1)} custom-call(bf16[64,1024]{1,0:T(8,128)(2,1)S(1)} %maximum_select_fusion.refs_0_.refs_3_, bf16[1024,13312]{1,0:T(8,128)(2,1)} %refs_0_.9, bf16[1024,13312]{1,0:T(8,128)(2,1)} %refs_1_.25, bf16[64,1024]{1,0:T(8,128)(2,1)S(1)} %maximum_select_fusion.refs_0_.refs_3_), custom_call_target="tpu_custom_call" | custom-call | tf_op jit(solution)/shard_map/gate_up/pallas_call | solution.py:40
  6.8 2.9 %collective-permute-start.2 = (bf16[2,64,2048]{2,1,0:T(8,128)(2,1)S(1)}, bf16[2,64,2048]{2,1,0:T(8,128)(2,1)S(1)}, u32[]{:S(2)}, u32[]{:S(2)}) collective-permute-start(bf16[2,64,2048]{2,1,0:T(8,128)(2,1)S(1)} %gate_up.12.refs_3_), channel_id=1, source_target_pairs={{0,2},{2,0},{4,6},{6,4},{8,10},{10,8},{12,14},{14,12},{1,3},{3,1},... | collective-permute-start | bytes 1572872 | tf_op jit(solution)/shard_map/ppermute | solution.py:21
  9.6 3.2 %gate_up.13.refs_3_ = bf16[2,64,1536]{2,1,0:T(8,128)(2,1)S(1)} custom-call(bf16[64,1024]{1,0:T(8,128)(2,1)S(1)} %maximum_select_fusion.refs_0_.refs_3_, bf16[1024,13312]{1,0:T(8,128)(2,1)} %refs_0_.9, bf16[1024,13312]{1,0:T(8,128)(2,1)} %refs_1_.25, bf16[2,64,2048]{2,1,0:T(8,128)(2,1)S(1)} %gate_up.12.refs_3_), custom_call_target="tpu_custom_call" | custom-call | tf_op jit(solution)/shard_map/gate_up/pallas_call | solution.py:40
  12.8 1.6 collective-permute-start.1
  14.5 3.2 %gate_up.14.refs_3_ = bf16[2,64,1536]{2,1,0:T(8,128)(2,1)S(1)} custom-call(bf16[64,1024]{1,0:T(8,128)(2,1)S(1)} %maximum_select_fusion.refs_0_.refs_3_, bf16[1024,13312]{1,0:T(8,128)(2,1)} %refs_0_.9, bf16[1024,13312]{1,0:T(8,128)(2,1)} %refs_1_.25, bf16[2,64,1536]{2,1,0:T(8,128)(2,1)S(1)} %gate_up.13.refs_3_), custom_call_target="tpu_custom_call" | custom-call | tf_op jit(solution)/shard_map/gate_up/pallas_call | solution.py:40
  17.7 0.6 collective-permute-start.3
  18.3 3.2 %gate_up.15.refs_3_ = bf16[2,64,1536]{2,1,0:T(8,128)(2,1)S(1)} custom-call(bf16[64,1024]{1,0:T(8,128)(2,1)S(1)} %maximum_select_fusion.refs_0_.refs_3_, bf16[1024,13312]{1,0:T(8,128)(2,1)} %refs_0_.9, bf16[1024,13312]{1,0:T(8,128)(2,1)} %refs_1_.25, bf16[2,64,1536]{2,1,0:T(8,128)(2,1)S(1)} %gate_up.14.refs_3_), custom_call_target="tpu_custom_call" | custom-call | tf_op jit(solution)/shard_map/gate_up/pallas_call | solution.py:40
  21.6 5.7 %gate_up.16 = (f32[2,64,2048]{2,1,0:T(8,128)S(1)}, f32[2,64,1536]{2,1,0:T(8,128)S(1)}) custom-call(bf16[64,1024]{1,0:T(8,128)(2,1)S(1)} %maximum_select_fusion.refs_0_.refs_3_, bf16[1024,13312]{1,0:T(8,128)(2,1)} %refs_0_.9, bf16[1024,13312]{1,0:T(8,128)(2,1)} %refs_1_.25, bf16[2,64,1536]{2,1,0:T(8,128)(2,1)S(1)} %gate_up.15.refs_3_), custom_call_target="tpu_custom_call" | custom-call | tf_op jit(solution)/shard_map/gate_up/pallas_call | solution.py:40
  27.5 2.0 %collective-permute-start.7 = (bf16[2,64,1024]{2,1,0:T(8,128)(2,1)S(1)}, bf16[2,64,1024]{2,1,0:T(8,128)(2,1)S(1)}, u32[]{:S(2)}, u32[]{:S(2)}) collective-permute-start(bf16[2,64,1024]{2,1,0:T(8,128)(2,1)S(1)} %get-tuple-element.71), channel_id=1, source_target_pairs={{0,4},{2,6},{4,0},{6,2},{8,12},{10,14},{12,8},{14,10},{1,5},{3,7},... | collective-permute-start | bytes 786440 | tf_op jit(solution)/shard_map/ppermute | solution.py:21
  29.6 1.6 collective-permute-start.8
  31.2 5.1 %gate_up.17 = (f32[2,64,1536]{2,1,0:T(8,128)S(1)}, f32[2,64,1536]{2,1,0:T(8,128)S(1)}) custom-call(bf16[64,1024]{1,0:T(8,128)(2,1)S(1)} %maximum_select_fusion.refs_0_.refs_3_, bf16[1024,13312]{1,0:T(8,128)(2,1)} %refs_0_.9, bf16[1024,13312]{1,0:T(8,128)(2,1)} %refs_1_.25, f32[2,64,768]{2,1,0:T(8,128)S(1)} %get-tuple-element.64.refs_3_.refs_1_), custom_call_target="tpu_custom_call" | custom-call | tf_op jit(solution)/shard_map/gate_up/pallas_call | solution.py:40
  36.6 0.6 collective-permute-start.6
  37.3 0.6 collective-permute-done.7.refs_2_
  38.0 2.6 %collective-permute-start.10 = (bf16[2,64,896]{2,1,0:T(8,128)(2,1)S(1)}, bf16[2,64,896]{2,1,0:T(8,128)(2,1)S(1)}, u32[]{:S(2)}, u32[]{:S(2)}) collective-permute-start(bf16[2,64,896]{2,1,0:T(8,128)(2,1)S(1)} %get-tuple-element.77), channel_id=1, source_target_pairs={{0,8},{2,10},{4,12},{6,14},{8,0},{10,2},{12,4},{14,6},{1,9},{3,11}... | collective-permute-start | bytes 688136 | tf_op jit(solution)/shard_map/ppermute | solution.py:21
  40.7 5.0 %fetch.5 = (bf16[4,512,1024]{2,1,0:T(8,128)(2,1)S(1)}, bf16[3,512,1024]{2,1,0:T(8,128)(2,1)S(1)}, bf16[3,512,1024]{2,1,0:T(8,128)(2,1)S(1)}, bf16[3,512,1024]{2,1,0:T(8,128)(2,1)S(1)}) custom-call(bf16[1024,13312]{1,0:T(8,128)(2,1)} %refs_0_.9, bf16[1024,13312]{1,0:T(8,128)(2,1)} %refs_1_.25, bf16[13312,1024]{1,0:T(8,128)(2,1)} %refs_3_.7, ...), custom_call_target="tpu_custom_call" | custom-call | tf_op jit(solution)/shard_map/fetch/pallas_call | solution.py:40
  45.8 1.5 collective-permute-start.9
  47.3 4.8 %fetch.6 = (bf16[3,2,1024,512]{3,2,1,0:T(8,128)(2,1)S(1)}, bf16[3,2,1024,512]{3,2,1,0:T(8,128)(2,1)S(1)}) custom-call(bf16[1024,13312]{1,0:T(8,128)(2,1)} %refs_0_.9, bf16[1024,13312]{1,0:T(8,128)(2,1)} %refs_1_.25, bf16[13312,1024]{1,0:T(8,128)(2,1)} %refs_3_.7, f32[2,64,768]{2,1,0:T(8,128)S(1)} %get-tuple-element.75.refs_3_.refs_0_), custom_call_target="tpu_custom_call" | custom-call | tf_op jit(solution)/shard_map/fetch/pallas_call | solution.py:40
  52.1 3.0 %collective-permute-done.10.refs_1_ = bf16[2,64,896]{2,1,0:T(8,128)(2,1)S(1)} collective-permute-done((bf16[2,64,896]{2,1,0:T(8,128)(2,1)S(1)}, bf16[2,64,896]{2,1,0:T(8,128)(2,1)S(1)}, u32[]{:S(2)}, u32[]{:S(2)}) %collective-permute-start.10) | collective-permute-done | bytes 229408 | tf_op jit(solution)/shard_map/ppermute | solution.py:21
  55.3 5.4 %fetch.7 = (bf16[4,2,1024,512]{3,2,1,0:T(8,128)(2,1)S(1)}, bf16[3,2,1024,512]{3,2,1,0:T(8,128)(2,1)S(1)}) custom-call(bf16[1024,13312]{1,0:T(8,128)(2,1)} %refs_0_.9, bf16[1024,13312]{1,0:T(8,128)(2,1)} %refs_1_.25, bf16[13312,1024]{1,0:T(8,128)(2,1)} %refs_3_.7, bf16[64,896]{1,0:T(8,128)(2,1)S(1)} %gated.4.refs_3_.refs_0_), custom_call_target="tpu_custom_call" | custom-call | tf_op jit(solution)/shard_map/fetch/pallas_call | solution.py:40
  60.9 3.0 %collective-permute-start.11 = (bf16[64,768]{1,0:T(8,128)(2,1)S(1)}, bf16[64,768]{1,0:T(8,128)(2,1)S(1)}, u32[]{:S(2)}, u32[]{:S(2)}) collective-permute-start(bf16[64,768]{1,0:T(8,128)(2,1)S(1)} %gated.5.refs_2_.refs_0_), channel_id=1, source_target_pairs={{0,8},{2,10},{4,12},{6,14},{8,0},{10,2},{12,4},{14,6},{1,9},{3,11}... | collective-permute-start | bytes 294920 | tf_op jit(solution)/shard_map/ppermute | solution.py:21
  63.9 4.8 %collective-permute-start.15 = (bf16[64,1024]{1,0:T(8,128)(2,1)S(1)}, bf16[64,1024]{1,0:T(8,128)(2,1)S(1)}, u32[]{:S(2)}, u32[]{:S(2)}) collective-permute-start(bf16[64,1024]{1,0:T(8,128)(2,1)S(1)} %get-tuple-element.80.refs_2_.refs_0_), channel_id=1, source_target_pairs={{0,4},{2,6},{4,0},{6,2},{8,12},{10,14},{12,8},{14,10},{1,5},{3,7},... | collective-permute-start | bytes 393224 | tf_op jit(solution)/shard_map/ppermute | solution.py:21
  68.7 5.7 %collective-permute-start.13 = (bf16[64,768]{1,0:T(8,128)(2,1)S(1)}, bf16[64,768]{1,0:T(8,128)(2,1)S(1)}, u32[]{:S(2)}, u32[]{:S(2)}) collective-permute-start(bf16[64,768]{1,0:T(8,128)(2,1)S(1)} %get-tuple-element.81.refs_2_.refs_0_), channel_id=1, source_target_pairs={{0,4},{2,6},{4,0},{6,2},{8,12},{10,14},{12,8},{14,10},{1,5},{3,7},... | collective-permute-start | bytes 294920 | tf_op jit(solution)/shard_map/ppermute | solution.py:21
  74.5 2.1 %collective-permute-start.19 = (bf16[64,2048]{1,0:T(8,128)(2,1)S(1)}, bf16[64,2048]{1,0:T(8,128)(2,1)S(1)}, u32[]{:S(2)}, u32[]{:S(2)}) collective-permute-start(bf16[64,2048]{1,0:T(8,128)(2,1)S(1)} %join.8.refs_2_.refs_0_), channel_id=1, source_target_pairs={{0,2},{2,0},{4,6},{6,4},{8,10},{10,8},{12,14},{14,12},{1,3},{3,1},... | collective-permute-start | bytes 786440 | tf_op jit(solution)/shard_map/ppermute | solution.py:21
  76.8 1.0 collective-permute-done.13.refs_1_
  77.7 1.3 collective-permute-done.17.refs_1_
  79.8 5.3 %down.6.refs_2_.refs_6_ = f32[64,1024]{1,0:T(8,128)S(1)} custom-call(bf16[64,2048]{1,0:T(8,128)(2,1)S(1)} %join.8.refs_2_.refs_0_, bf16[64,1536]{1,0:T(8,128)(2,1)S(1)} %join.9.refs_2_.refs_1_, bf16[64,1536]{1,0:T(8,128)(2,1)S(1)} %join.10.refs_2_, bf16[64,1536]{1,0:T(8,128)(2,1)S(1)} %join.11.refs_3_.refs_5_, bf16[13312,1024]{1,0:T(8,128)(2,1)} %refs_3_.7, ...), custom_call_target="tpu_custom_call" | custom-call | tf_op jit(solution)/shard_map/down/pallas_call | solution.py:40
  85.2 2.1 %down.7.refs_2_.refs_6_ = f32[64,1024]{1,0:T(8,128)S(1)} custom-call(bf16[64,2048]{1,0:T(8,128)(2,1)S(1)} %collective-permute-done.19.refs_0_, bf16[64,1536]{1,0:T(8,128)(2,1)S(1)} %collective-permute-done.20.refs_1_, f32[64,1024]{1,0:T(8,128)S(1)} %down.6.refs_2_.refs_6_, bf16[13312,1024]{1,0:T(8,128)(2,1)} %refs_3_.7, ...), custom_call_target="tpu_custom_call" | custom-call | tf_op jit(solution)/shard_map/down/pallas_call | solution.py:40
  87.4 1.8 %down.8 = f32[64,1024]{1,0:T(8,128)S(1)} custom-call(bf16[64,1536]{1,0:T(8,128)(2,1)S(1)} %collective-permute-done.16.refs_0_, bf16[64,1536]{1,0:T(8,128)(2,1)S(1)} %collective-permute-done.18.refs_1_, f32[64,1024]{1,0:T(8,128)S(1)} %down.7.refs_2_.refs_6_, bf16[13312,1024]{1,0:T(8,128)(2,1)} %refs_3_.7, ...), custom_call_target="tpu_custom_call" | custom-call | tf_op jit(solution)/shard_map/down/pallas_call | solution.py:40
  89.8 1.1 collective-permute-done.22
  91.0 1.9 %gate_up.18.refs_2_ = bf16[2,64,2048]{2,1,0:T(8,128)(2,1)S(1)} custom-call(bf16[64,1024]{1,0:T(8,128)(2,1)S(1)} %get-tuple-element.117.refs_0_.refs_2_, bf16[4,2,1024,512]{3,2,1,0:T(8,128)(2,1)S(1)} %get-tuple-element.79.refs_2_.refs_1_, bf16[64,1024]{1,0:T(8,128)(2,1)S(1)} %get-tuple-element.117.refs_0_.refs_2_), custom_call_target="tpu_custom_call" | custom-call | tf_op jit(solution)/shard_map/gate_up/pallas_call | solution.py:40
  92.9 1.8 %collective-permute-start.24 = (bf16[2,64,2048]{2,1,0:T(8,128)(2,1)S(1)}, bf16[2,64,2048]{2,1,0:T(8,128)(2,1)S(1)}, u32[]{:S(2)}, u32[]{:S(2)}) collective-permute-start(bf16[2,64,2048]{2,1,0:T(8,128)(2,1)S(1)} %gate_up.18.refs_2_), channel_id=1, source_target_pairs={{0,2},{2,0},{4,6},{6,4},{8,10},{10,8},{12,14},{14,12},{1,3},{3,1},... | collective-permute-start | bytes 1572872 | tf_op jit(solution)/shard_map/ppermute | solution.py:21
  94.7 1.4 gate_up.19.refs_2_
  96.1 1.7 %collective-permute-start.23 = (bf16[2,64,1536]{2,1,0:T(8,128)(2,1)S(1)}, bf16[2,64,1536]{2,1,0:T(8,128)(2,1)S(1)}, u32[]{:S(2)}, u32[]{:S(2)}) collective-permute-start(bf16[2,64,1536]{2,1,0:T(8,128)(2,1)S(1)} %gate_up.19.refs_2_), channel_id=1, source_target_pairs={{0,4},{2,6},{4,0},{6,2},{8,12},{10,14},{12,8},{14,10},{1,5},{3,7},... | collective-permute-start | bytes 1179656 | tf_op jit(solution)/shard_map/ppermute | solution.py:21
  97.8 1.4 gate_up.20.refs_2_
  99.5 1.4 gate_up.21.refs_3_
  101.5 5.7 %gate_up.22 = (f32[2,64,2048]{2,1,0:T(8,128)S(1)}, f32[2,64,1536]{2,1,0:T(8,128)S(1)}) custom-call(bf16[64,1024]{1,0:T(8,128)(2,1)S(1)} %get-tuple-element.117.refs_0_.refs_2_, bf16[1024,13312]{1,0:T(8,128)(2,1)} %refs_0_.9, bf16[1024,13312]{1,0:T(8,128)(2,1)} %refs_1_.25, bf16[2,64,1536]{2,1,0:T(8,128)(2,1)S(1)} %gate_up.21.refs_3_), custom_call_target="tpu_custom_call" | custom-call | tf_op jit(solution)/shard_map/gate_up/pallas_call | solution.py:40
  107.8 1.6 collective-permute-start.29
  109.5 1.9 %collective-permute-start.30 = (bf16[2,64,768]{2,1,0:T(8,128)(2,1)S(1)}, bf16[2,64,768]{2,1,0:T(8,128)(2,1)S(1)}, u32[]{:S(2)}, u32[]{:S(2)}) collective-permute-start(bf16[2,64,768]{2,1,0:T(8,128)(2,1)S(1)} %get-tuple-element.100), channel_id=1, source_target_pairs={{0,2},{2,0},{4,6},{6,4},{8,10},{10,8},{12,14},{14,12},{1,3},{3,1},... | collective-permute-start | bytes 589832 | tf_op jit(solution)/shard_map/ppermute | solution.py:21
  111.4 5.1 %gate_up.23 = (f32[2,64,1536]{2,1,0:T(8,128)S(1)}, f32[2,64,1536]{2,1,0:T(8,128)S(1)}) custom-call(bf16[64,1024]{1,0:T(8,128)(2,1)S(1)} %get-tuple-element.117.refs_0_.refs_2_, bf16[1024,13312]{1,0:T(8,128)(2,1)} %refs_0_.9, bf16[1024,13312]{1,0:T(8,128)(2,1)} %refs_1_.25, f32[2,64,768]{2,1,0:T(8,128)S(1)} %get-tuple-element.92.refs_3_.refs_1_), custom_call_target="tpu_custom_call" | custom-call | tf_op jit(solution)/shard_map/gate_up/pallas_call | solution.py:40
  116.7 1.4 collective-permute-start.28
  118.1 1.6 collective-permute-start.27
  119.8 0.6 collective-permute-done.30.refs_3_
  120.3 1.9 %collective-permute-done.29.refs_2_ = bf16[2,64,1024]{2,1,0:T(8,128)(2,1)S(1)} collective-permute-done((bf16[2,64,1024]{2,1,0:T(8,128)(2,1)S(1)}, bf16[2,64,1024]{2,1,0:T(8,128)(2,1)S(1)}, u32[]{:S(2)}, u32[]{:S(2)}) %collective-permute-start.29) | collective-permute-done | bytes 262176 | tf_op jit(solution)/shard_map/ppermute | solution.py:21
  122.3 0.7 collective-permute-start.32
  123.1 5.0 %fetch.8 = (bf16[4,512,1024]{2,1,0:T(8,128)(2,1)S(1)}, bf16[3,512,1024]{2,1,0:T(8,128)(2,1)S(1)}, bf16[3,512,1024]{2,1,0:T(8,128)(2,1)S(1)}, bf16[3,512,1024]{2,1,0:T(8,128)(2,1)S(1)}) custom-call(bf16[1024,13312]{1,0:T(8,128)(2,1)} %refs_0_.9, bf16[1024,13312]{1,0:T(8,128)(2,1)} %refs_1_.25, bf16[13312,1024]{1,0:T(8,128)(2,1)} %refs_3_.7, ...), custom_call_target="tpu_custom_call" | custom-call | tf_op jit(solution)/shard_map/fetch/pallas_call | solution.py:40
  128.2 2.3 %collective-permute-start.31 = (bf16[2,64,768]{2,1,0:T(8,128)(2,1)S(1)}, bf16[2,64,768]{2,1,0:T(8,128)(2,1)S(1)}, u32[]{:S(2)}, u32[]{:S(2)}) collective-permute-start(bf16[2,64,768]{2,1,0:T(8,128)(2,1)S(1)} %get-tuple-element.104), channel_id=1, source_target_pairs={{0,8},{2,10},{4,12},{6,14},{8,0},{10,2},{12,4},{14,6},{1,9},{3,11}... | collective-permute-start | bytes 589832 | tf_op jit(solution)/shard_map/ppermute | solution.py:21
  130.5 5.0 %fetch.9 = (bf16[4,512,1024]{2,1,0:T(8,128)(2,1)S(1)}, bf16[3,512,1024]{2,1,0:T(8,128)(2,1)S(1)}, bf16[3,512,1024]{2,1,0:T(8,128)(2,1)S(1)}, bf16[3,512,1024]{2,1,0:T(8,128)(2,1)S(1)}) custom-call(bf16[1024,13312]{1,0:T(8,128)(2,1)} %refs_0_.9, bf16[1024,13312]{1,0:T(8,128)(2,1)} %refs_1_.25, bf16[13312,1024]{1,0:T(8,128)(2,1)} %refs_3_.7, ...), custom_call_target="tpu_custom_call" | custom-call | tf_op jit(solution)/shard_map/fetch/pallas_call | solution.py:40
  135.5 5.5 %collective-permute-done.32.refs_1_ = bf16[2,64,896]{2,1,0:T(8,128)(2,1)S(1)} collective-permute-done((bf16[2,64,896]{2,1,0:T(8,128)(2,1)S(1)}, bf16[2,64,896]{2,1,0:T(8,128)(2,1)S(1)}, u32[]{:S(2)}, u32[]{:S(2)}) %collective-permute-start.32) | collective-permute-done | bytes 229408 | tf_op jit(solution)/shard_map/ppermute | solution.py:21
  141.2 3.4 %collective-permute-done.31.refs_1_ = bf16[2,64,768]{2,1,0:T(8,128)(2,1)S(1)} collective-permute-done((bf16[2,64,768]{2,1,0:T(8,128)(2,1)S(1)}, bf16[2,64,768]{2,1,0:T(8,128)(2,1)S(1)}, u32[]{:S(2)}, u32[]{:S(2)}) %collective-permute-start.31) | collective-permute-done | bytes 196640 | tf_op jit(solution)/shard_map/ppermute | solution.py:21
  144.7 4.5 %collective-permute-done.34.refs_1_ = bf16[64,896]{1,0:T(8,128)(2,1)S(1)} collective-permute-done((bf16[64,896]{1,0:T(8,128)(2,1)S(1)}, bf16[64,896]{1,0:T(8,128)(2,1)S(1)}, u32[]{:S(2)}, u32[]{:S(2)}) %collective-permute-start.34) | collective-permute-done | bytes 114720 | tf_op jit(solution)/shard_map/ppermute | solution.py:21
  149.6 0.8 collective-permute-start.36
  150.4 1.8 %collective-permute-start.35 = (bf16[64,768]{1,0:T(8,128)(2,1)S(1)}, bf16[64,768]{1,0:T(8,128)(2,1)S(1)}, u32[]{:S(2)}, u32[]{:S(2)}) collective-permute-start(bf16[64,768]{1,0:T(8,128)(2,1)S(1)} %get-tuple-element.108.refs_2_.refs_0_), channel_id=1, source_target_pairs={{0,4},{2,6},{4,0},{6,2},{8,12},{10,14},{12,8},{14,10},{1,5},{3,7},... | collective-permute-start | bytes 294920 | tf_op jit(solution)/shard_map/ppermute | solution.py:21
  152.2 1.3 collective-permute-start.39
  153.4 1.1 collective-permute-done.37.refs_1_
  154.9 2.2 %collective-permute-start.42 = (bf16[64,1536]{1,0:T(8,128)(2,1)S(1)}, bf16[64,1536]{1,0:T(8,128)(2,1)S(1)}, u32[]{:S(2)}, u32[]{:S(2)}) collective-permute-start(bf16[64,1536]{1,0:T(8,128)(2,1)S(1)} %join.13.refs_2_.refs_1_), channel_id=1, source_target_pairs={{0,4},{2,6},{4,0},{6,2},{8,12},{10,14},{12,8},{14,10},{1,5},{3,7},... | collective-permute-start | bytes 589832 | tf_op jit(solution)/shard_map/ppermute | solution.py:21
  157.2 0.8 collective-permute-done.39.refs_1_
  157.9 1.3 collective-permute-start.40
  159.7 3.9 %down.9.refs_2_.refs_6_ = f32[64,1024]{1,0:T(8,128)S(1)} custom-call(bf16[64,2048]{1,0:T(8,128)(2,1)S(1)} %join.12.refs_2_.refs_0_, bf16[64,1536]{1,0:T(8,128)(2,1)S(1)} %join.13.refs_2_.refs_1_, bf16[64,1536]{1,0:T(8,128)(2,1)S(1)} %join.14.refs_2_, bf16[64,1536]{1,0:T(8,128)(2,1)S(1)} %join.15.refs_3_.refs_9_, bf16[13312,1024]{1,0:T(8,128)(2,1)} %refs_3_.7, ...), custom_call_target="tpu_custom_call" | custom-call | tf_op jit(solution)/shard_map/down/pallas_call | solution.py:40
  163.6 2.1 %down.10.refs_2_.refs_6_ = f32[64,1024]{1,0:T(8,128)S(1)} custom-call(bf16[64,2048]{1,0:T(8,128)(2,1)S(1)} %collective-permute-done.41.refs_0_, bf16[64,1536]{1,0:T(8,128)(2,1)S(1)} %collective-permute-done.42.refs_1_, f32[64,1024]{1,0:T(8,128)S(1)} %down.9.refs_2_.refs_6_, bf16[13312,1024]{1,0:T(8,128)(2,1)} %refs_3_.7, ...), custom_call_target="tpu_custom_call" | custom-call | tf_op jit(solution)/shard_map/down/pallas_call | solution.py:40
  165.8 1.8 %down.11 = f32[64,1024]{1,0:T(8,128)S(1)} custom-call(bf16[64,1536]{1,0:T(8,128)(2,1)S(1)} %collective-permute-done.38.refs_0_, bf16[64,1536]{1,0:T(8,128)(2,1)S(1)} %collective-permute-done.40.refs_1_, f32[64,1024]{1,0:T(8,128)S(1)} %down.10.refs_2_.refs_6_, bf16[13312,1024]{1,0:T(8,128)(2,1)} %refs_3_.7, ...), custom_call_target="tpu_custom_call" | custom-call | tf_op jit(solution)/shard_map/down/pallas_call | solution.py:40
  167.7 1.5 collective-permute-done.43
  169.2 0.7 fusion.1
  (82 shorter events, 6.7 us)
Async XLA Ops:
  1.5 1.4 collective-permute-start
  6.8 20.6 %collective-permute-start.2 = (bf16[2,64,2048]{2,1,0:T(8,128)(2,1)S(1)}, bf16[2,64,2048]{2,1,0:T(8,128)(2,1)S(1)}, u32[]{:S(2)}, u32[]{:S(2)}) collective-permute-start(bf16[2,64,2048]{2,1,0:T(8,128)(2,1)S(1)} %gate_up.12.refs_3_), channel_id=1, source_target_pairs={{0,2},{2,0},{4,6},{6,4},{8,10},{10,8},{12,14},{14,12},{1,3},{3,1},... | collective-permute-start | bytes 1572872 | tf_op jit(solution)/shard_map/ppermute | solution.py:21
  12.8 16.7 %collective-permute-start.1 = (bf16[2,64,1536]{2,1,0:T(8,128)(2,1)S(1)}, bf16[2,64,1536]{2,1,0:T(8,128)(2,1)S(1)}, u32[]{:S(2)}, u32[]{:S(2)}) collective-permute-start(bf16[2,64,1536]{2,1,0:T(8,128)(2,1)S(1)} %gate_up.13.refs_3_), channel_id=1, source_target_pairs={{0,4},{2,6},{4,0},{6,2},{8,12},{10,14},{12,8},{14,10},{1,5},{3,7},... | collective-permute-start | bytes 1179656 | tf_op jit(solution)/shard_map/ppermute | solution.py:21
  17.7 18.7 %collective-permute-start.3 = (bf16[2,64,1536]{2,1,0:T(8,128)(2,1)S(1)}, bf16[2,64,1536]{2,1,0:T(8,128)(2,1)S(1)}, u32[]{:S(2)}, u32[]{:S(2)}) collective-permute-start(bf16[2,64,1536]{2,1,0:T(8,128)(2,1)S(1)} %gate_up.14.refs_3_), channel_id=1, source_target_pairs={{0,2},{2,0},{4,6},{6,4},{8,10},{10,8},{12,14},{14,12},{1,3},{3,1},... | collective-permute-start | bytes 1179656 | tf_op jit(solution)/shard_map/ppermute | solution.py:21
  21.5 14.9 %collective-permute-start.4 = (bf16[2,64,1536]{2,1,0:T(8,128)(2,1)S(1)}, bf16[2,64,1536]{2,1,0:T(8,128)(2,1)S(1)}, u32[]{:S(2)}, u32[]{:S(2)}) collective-permute-start(bf16[2,64,1536]{2,1,0:T(8,128)(2,1)S(1)} %gate_up.15.refs_3_), channel_id=1, source_target_pairs={{0,4},{2,6},{4,0},{6,2},{8,12},{10,14},{12,8},{14,10},{1,5},{3,7},... | collective-permute-start | bytes 1179656 | tf_op jit(solution)/shard_map/ppermute | solution.py:21
  27.5 10.5 %collective-permute-start.7 = (bf16[2,64,1024]{2,1,0:T(8,128)(2,1)S(1)}, bf16[2,64,1024]{2,1,0:T(8,128)(2,1)S(1)}, u32[]{:S(2)}, u32[]{:S(2)}) collective-permute-start(bf16[2,64,1024]{2,1,0:T(8,128)(2,1)S(1)} %get-tuple-element.71), channel_id=1, source_target_pairs={{0,4},{2,6},{4,0},{6,2},{8,12},{10,14},{12,8},{14,10},{1,5},{3,7},... | collective-permute-start | bytes 786440 | tf_op jit(solution)/shard_map/ppermute | solution.py:21
  29.6 7.7 %collective-permute-start.8 = (bf16[2,64,768]{2,1,0:T(8,128)(2,1)S(1)}, bf16[2,64,768]{2,1,0:T(8,128)(2,1)S(1)}, u32[]{:S(2)}, u32[]{:S(2)}) collective-permute-start(bf16[2,64,768]{2,1,0:T(8,128)(2,1)S(1)} %get-tuple-element.72), channel_id=1, source_target_pairs={{0,2},{2,0},{4,6},{6,4},{8,10},{10,8},{12,14},{14,12},{1,3},{3,1},... | collective-permute-start | bytes 589832 | tf_op jit(solution)/shard_map/ppermute | solution.py:21
  36.6 9.1 %collective-permute-start.6 = (bf16[2,64,768]{2,1,0:T(8,128)(2,1)S(1)}, bf16[2,64,768]{2,1,0:T(8,128)(2,1)S(1)}, u32[]{:S(2)}, u32[]{:S(2)}) collective-permute-start(bf16[2,64,768]{2,1,0:T(8,128)(2,1)S(1)} %get-tuple-element.70), channel_id=1, source_target_pairs={{0,2},{2,0},{4,6},{6,4},{8,10},{10,8},{12,14},{14,12},{1,3},{3,1},... | collective-permute-start | bytes 589832 | tf_op jit(solution)/shard_map/ppermute | solution.py:21
  37.1 8.6 %collective-permute-start.5 = (bf16[2,64,768]{2,1,0:T(8,128)(2,1)S(1)}, bf16[2,64,768]{2,1,0:T(8,128)(2,1)S(1)}, u32[]{:S(2)}, u32[]{:S(2)}) collective-permute-start(bf16[2,64,768]{2,1,0:T(8,128)(2,1)S(1)} %get-tuple-element.69), channel_id=1, source_target_pairs={{0,4},{2,6},{4,0},{6,2},{8,12},{10,14},{12,8},{14,10},{1,5},{3,7},... | collective-permute-start | bytes 589832 | tf_op jit(solution)/shard_map/ppermute | solution.py:21
  38.0 17.1 %collective-permute-start.10 = (bf16[2,64,896]{2,1,0:T(8,128)(2,1)S(1)}, bf16[2,64,896]{2,1,0:T(8,128)(2,1)S(1)}, u32[]{:S(2)}, u32[]{:S(2)}) collective-permute-start(bf16[2,64,896]{2,1,0:T(8,128)(2,1)S(1)} %get-tuple-element.77), channel_id=1, source_target_pairs={{0,8},{2,10},{4,12},{6,14},{8,0},{10,2},{12,4},{14,6},{1,9},{3,11}... | collective-permute-start | bytes 688136 | tf_op jit(solution)/shard_map/ppermute | solution.py:21
  45.8 15.0 %collective-permute-start.9 = (bf16[2,64,768]{2,1,0:T(8,128)(2,1)S(1)}, bf16[2,64,768]{2,1,0:T(8,128)(2,1)S(1)}, u32[]{:S(2)}, u32[]{:S(2)}) collective-permute-start(bf16[2,64,768]{2,1,0:T(8,128)(2,1)S(1)} %get-tuple-element.76), channel_id=1, source_target_pairs={{0,8},{2,10},{4,12},{6,14},{8,0},{10,2},{12,4},{14,6},{1,9},{3,11}... | collective-permute-start | bytes 589832 | tf_op jit(solution)/shard_map/ppermute | solution.py:21
  55.2 8.6 %collective-permute-start.12 = (bf16[64,896]{1,0:T(8,128)(2,1)S(1)}, bf16[64,896]{1,0:T(8,128)(2,1)S(1)}, u32[]{:S(2)}, u32[]{:S(2)}) collective-permute-start(bf16[64,896]{1,0:T(8,128)(2,1)S(1)} %gated.4.refs_3_.refs_0_), channel_id=1, source_target_pairs={{0,8},{2,10},{4,12},{6,14},{8,0},{10,2},{12,4},{14,6},{1,9},{3,11}... | collective-permute-start | bytes 344072 | tf_op jit(solution)/shard_map/ppermute | solution.py:21
  60.9 7.8 %collective-permute-start.11 = (bf16[64,768]{1,0:T(8,128)(2,1)S(1)}, bf16[64,768]{1,0:T(8,128)(2,1)S(1)}, u32[]{:S(2)}, u32[]{:S(2)}) collective-permute-start(bf16[64,768]{1,0:T(8,128)(2,1)S(1)} %gated.5.refs_2_.refs_0_), channel_id=1, source_target_pairs={{0,8},{2,10},{4,12},{6,14},{8,0},{10,2},{12,4},{14,6},{1,9},{3,11}... | collective-permute-start | bytes 294920 | tf_op jit(solution)/shard_map/ppermute | solution.py:21
  63.9 10.6 %collective-permute-start.15 = (bf16[64,1024]{1,0:T(8,128)(2,1)S(1)}, bf16[64,1024]{1,0:T(8,128)(2,1)S(1)}, u32[]{:S(2)}, u32[]{:S(2)}) collective-permute-start(bf16[64,1024]{1,0:T(8,128)(2,1)S(1)} %get-tuple-element.80.refs_2_.refs_0_), channel_id=1, source_target_pairs={{0,4},{2,6},{4,0},{6,2},{8,12},{10,14},{12,8},{14,10},{1,5},{3,7},... | collective-permute-start | bytes 393224 | tf_op jit(solution)/shard_map/ppermute | solution.py:21
  68.7 7.9 %collective-permute-start.14 = (bf16[64,768]{1,0:T(8,128)(2,1)S(1)}, bf16[64,768]{1,0:T(8,128)(2,1)S(1)}, u32[]{:S(2)}, u32[]{:S(2)}) collective-permute-start(bf16[64,768]{1,0:T(8,128)(2,1)S(1)} %get-tuple-element.82.refs_0_), channel_id=1, source_target_pairs={{0,2},{2,0},{4,6},{6,4},{8,10},{10,8},{12,14},{14,12},{1,3},{3,1},... | collective-permute-start | bytes 294920 | tf_op jit(solution)/shard_map/ppermute | solution.py:21
  68.7 9.0 %collective-permute-start.13 = (bf16[64,768]{1,0:T(8,128)(2,1)S(1)}, bf16[64,768]{1,0:T(8,128)(2,1)S(1)}, u32[]{:S(2)}, u32[]{:S(2)}) collective-permute-start(bf16[64,768]{1,0:T(8,128)(2,1)S(1)} %get-tuple-element.81.refs_2_.refs_0_), channel_id=1, source_target_pairs={{0,4},{2,6},{4,0},{6,2},{8,12},{10,14},{12,8},{14,10},{1,5},{3,7},... | collective-permute-start | bytes 294920 | tf_op jit(solution)/shard_map/ppermute | solution.py:21
  74.5 4.6 %collective-permute-start.17 = (bf16[64,768]{1,0:T(8,128)(2,1)S(1)}, bf16[64,768]{1,0:T(8,128)(2,1)S(1)}, u32[]{:S(2)}, u32[]{:S(2)}) collective-permute-start(bf16[64,768]{1,0:T(8,128)(2,1)S(1)} %get-tuple-element.83.refs_0_), channel_id=1, source_target_pairs={{0,2},{2,0},{4,6},{6,4},{8,10},{10,8},{12,14},{14,12},{1,3},{3,1},... | collective-permute-start | bytes 294920 | tf_op jit(solution)/shard_map/ppermute | solution.py:21
  74.5 10.7 %collective-permute-start.19 = (bf16[64,2048]{1,0:T(8,128)(2,1)S(1)}, bf16[64,2048]{1,0:T(8,128)(2,1)S(1)}, u32[]{:S(2)}, u32[]{:S(2)}) collective-permute-start(bf16[64,2048]{1,0:T(8,128)(2,1)S(1)} %join.8.refs_2_.refs_0_), channel_id=1, source_target_pairs={{0,2},{2,0},{4,6},{6,4},{8,10},{10,8},{12,14},{14,12},{1,3},{3,1},... | collective-permute-start | bytes 786440 | tf_op jit(solution)/shard_map/ppermute | solution.py:21
  76.6 8.6 %collective-permute-start.20 = (bf16[64,1536]{1,0:T(8,128)(2,1)S(1)}, bf16[64,1536]{1,0:T(8,128)(2,1)S(1)}, u32[]{:S(2)}, u32[]{:S(2)}) collective-permute-start(bf16[64,1536]{1,0:T(8,128)(2,1)S(1)} %join.9.refs_2_.refs_1_), channel_id=1, source_target_pairs={{0,4},{2,6},{4,0},{6,2},{8,12},{10,14},{12,8},{14,10},{1,5},{3,7},... | collective-permute-start | bytes 589832 | tf_op jit(solution)/shard_map/ppermute | solution.py:21
  79.1 8.2 %collective-permute-start.18 = (bf16[64,1536]{1,0:T(8,128)(2,1)S(1)}, bf16[64,1536]{1,0:T(8,128)(2,1)S(1)}, u32[]{:S(2)}, u32[]{:S(2)}) collective-permute-start(bf16[64,1536]{1,0:T(8,128)(2,1)S(1)} %join.11.refs_3_.refs_5_), channel_id=1, source_target_pairs={{0,4},{2,6},{4,0},{6,2},{8,12},{10,14},{12,8},{14,10},{1,5},{3,7},... | collective-permute-start | bytes 589832 | tf_op jit(solution)/shard_map/ppermute | solution.py:21
  79.6 7.8 %collective-permute-start.16 = (bf16[64,1536]{1,0:T(8,128)(2,1)S(1)}, bf16[64,1536]{1,0:T(8,128)(2,1)S(1)}, u32[]{:S(2)}, u32[]{:S(2)}) collective-permute-start(bf16[64,1536]{1,0:T(8,128)(2,1)S(1)} %join.10.refs_2_), channel_id=1, source_target_pairs={{0,2},{2,0},{4,6},{6,4},{8,10},{10,8},{12,14},{14,12},{1,3},{3,1},... | collective-permute-start | bytes 589832 | tf_op jit(solution)/shard_map/ppermute | solution.py:21
  87.4 1.9 %copy-start = (bf16[32,1024]{1,0:T(8,128)(2,1)S(1)}, bf16[32,1024]{1,0:T(8,128)(2,1)}, u32[]{:S(2)}) copy-start(bf16[32,1024]{1,0:T(8,128)(2,1)} %get-tuple-element.120) | copy-start | bytes 196612
  89.2 1.7 collective-permute-start.21
  89.3 1.6 collective-permute-start.22
  92.9 14.8 %collective-permute-start.24 = (bf16[2,64,2048]{2,1,0:T(8,128)(2,1)S(1)}, bf16[2,64,2048]{2,1,0:T(8,128)(2,1)S(1)}, u32[]{:S(2)}, u32[]{:S(2)}) collective-permute-start(bf16[2,64,2048]{2,1,0:T(8,128)(2,1)S(1)} %gate_up.18.refs_2_), channel_id=1, source_target_pairs={{0,2},{2,0},{4,6},{6,4},{8,10},{10,8},{12,14},{14,12},{1,3},{3,1},... | collective-permute-start | bytes 1572872 | tf_op jit(solution)/shard_map/ppermute | solution.py:21
  96.1 13.3 %collective-permute-start.23 = (bf16[2,64,1536]{2,1,0:T(8,128)(2,1)S(1)}, bf16[2,64,1536]{2,1,0:T(8,128)(2,1)S(1)}, u32[]{:S(2)}, u32[]{:S(2)}) collective-permute-start(bf16[2,64,1536]{2,1,0:T(8,128)(2,1)S(1)} %gate_up.19.refs_2_), channel_id=1, source_target_pairs={{0,4},{2,6},{4,0},{6,2},{8,12},{10,14},{12,8},{14,10},{1,5},{3,7},... | collective-permute-start | bytes 1179656 | tf_op jit(solution)/shard_map/ppermute | solution.py:21
  99.3 17.3 %collective-permute-start.25 = (bf16[2,64,1536]{2,1,0:T(8,128)(2,1)S(1)}, bf16[2,64,1536]{2,1,0:T(8,128)(2,1)S(1)}, u32[]{:S(2)}, u32[]{:S(2)}) collective-permute-start(bf16[2,64,1536]{2,1,0:T(8,128)(2,1)S(1)} %gate_up.20.refs_2_), channel_id=1, source_target_pairs={{0,2},{2,0},{4,6},{6,4},{8,10},{10,8},{12,14},{14,12},{1,3},{3,1},... | collective-permute-start | bytes 1179656 | tf_op jit(solution)/shard_map/ppermute | solution.py:21
  100.9 15.7 %collective-permute-start.26 = (bf16[2,64,1536]{2,1,0:T(8,128)(2,1)S(1)}, bf16[2,64,1536]{2,1,0:T(8,128)(2,1)S(1)}, u32[]{:S(2)}, u32[]{:S(2)}) collective-permute-start(bf16[2,64,1536]{2,1,0:T(8,128)(2,1)S(1)} %gate_up.21.refs_3_), channel_id=1, source_target_pairs={{0,4},{2,6},{4,0},{6,2},{8,12},{10,14},{12,8},{14,10},{1,5},{3,7},... | collective-permute-start | bytes 1179656 | tf_op jit(solution)/shard_map/ppermute | solution.py:21
  107.8 14.4 %collective-permute-start.29 = (bf16[2,64,1024]{2,1,0:T(8,128)(2,1)S(1)}, bf16[2,64,1024]{2,1,0:T(8,128)(2,1)S(1)}, u32[]{:S(2)}, u32[]{:S(2)}) collective-permute-start(bf16[2,64,1024]{2,1,0:T(8,128)(2,1)S(1)} %get-tuple-element.99), channel_id=1, source_target_pairs={{0,4},{2,6},{4,0},{6,2},{8,12},{10,14},{12,8},{14,10},{1,5},{3,7},... | collective-permute-start | bytes 786440 | tf_op jit(solution)/shard_map/ppermute | solution.py:21
  109.5 10.9 %collective-permute-start.30 = (bf16[2,64,768]{2,1,0:T(8,128)(2,1)S(1)}, bf16[2,64,768]{2,1,0:T(8,128)(2,1)S(1)}, u32[]{:S(2)}, u32[]{:S(2)}) collective-permute-start(bf16[2,64,768]{2,1,0:T(8,128)(2,1)S(1)} %get-tuple-element.100), channel_id=1, source_target_pairs={{0,2},{2,0},{4,6},{6,4},{8,10},{10,8},{12,14},{14,12},{1,3},{3,1},... | collective-permute-start | bytes 589832 | tf_op jit(solution)/shard_map/ppermute | solution.py:21
  116.7 11.4 %collective-permute-start.28 = (bf16[2,64,768]{2,1,0:T(8,128)(2,1)S(1)}, bf16[2,64,768]{2,1,0:T(8,128)(2,1)S(1)}, u32[]{:S(2)}, u32[]{:S(2)}) collective-permute-start(bf16[2,64,768]{2,1,0:T(8,128)(2,1)S(1)} %get-tuple-element.98), channel_id=1, source_target_pairs={{0,2},{2,0},{4,6},{6,4},{8,10},{10,8},{12,14},{14,12},{1,3},{3,1},... | collective-permute-start | bytes 589832 | tf_op jit(solution)/shard_map/ppermute | solution.py:21
  118.1 10.0 %collective-permute-start.27 = (bf16[2,64,768]{2,1,0:T(8,128)(2,1)S(1)}, bf16[2,64,768]{2,1,0:T(8,128)(2,1)S(1)}, u32[]{:S(2)}, u32[]{:S(2)}) collective-permute-start(bf16[2,64,768]{2,1,0:T(8,128)(2,1)S(1)} %get-tuple-element.97), channel_id=1, source_target_pairs={{0,4},{2,6},{4,0},{6,2},{8,12},{10,14},{12,8},{14,10},{1,5},{3,7},... | collective-permute-start | bytes 589832 | tf_op jit(solution)/shard_map/ppermute | solution.py:21
  122.3 18.7 %collective-permute-start.32 = (bf16[2,64,896]{2,1,0:T(8,128)(2,1)S(1)}, bf16[2,64,896]{2,1,0:T(8,128)(2,1)S(1)}, u32[]{:S(2)}, u32[]{:S(2)}) collective-permute-start(bf16[2,64,896]{2,1,0:T(8,128)(2,1)S(1)} %get-tuple-element.105), channel_id=1, source_target_pairs={{0,8},{2,10},{4,12},{6,14},{8,0},{10,2},{12,4},{14,6},{1,9},{3,11}... | collective-permute-start | bytes 688136 | tf_op jit(solution)/shard_map/ppermute | solution.py:21
  128.2 16.3 %collective-permute-start.31 = (bf16[2,64,768]{2,1,0:T(8,128)(2,1)S(1)}, bf16[2,64,768]{2,1,0:T(8,128)(2,1)S(1)}, u32[]{:S(2)}, u32[]{:S(2)}) collective-permute-start(bf16[2,64,768]{2,1,0:T(8,128)(2,1)S(1)} %get-tuple-element.104), channel_id=1, source_target_pairs={{0,8},{2,10},{4,12},{6,14},{8,0},{10,2},{12,4},{14,6},{1,9},{3,11}... | collective-permute-start | bytes 589832 | tf_op jit(solution)/shard_map/ppermute | solution.py:21
  141.1 8.1 %collective-permute-start.34 = (bf16[64,896]{1,0:T(8,128)(2,1)S(1)}, bf16[64,896]{1,0:T(8,128)(2,1)S(1)}, u32[]{:S(2)}, u32[]{:S(2)}) collective-permute-start(bf16[64,896]{1,0:T(8,128)(2,1)S(1)} %gated.6.refs_2_.refs_0_), channel_id=1, source_target_pairs={{0,8},{2,10},{4,12},{6,14},{8,0},{10,2},{12,4},{14,6},{1,9},{3,11}... | collective-permute-start | bytes 344072 | tf_op jit(solution)/shard_map/ppermute | solution.py:21
  144.6 5.7 %collective-permute-start.33 = (bf16[64,768]{1,0:T(8,128)(2,1)S(1)}, bf16[64,768]{1,0:T(8,128)(2,1)S(1)}, u32[]{:S(2)}, u32[]{:S(2)}) collective-permute-start(bf16[64,768]{1,0:T(8,128)(2,1)S(1)} %gated.7.refs_2_.refs_0_), channel_id=1, source_target_pairs={{0,8},{2,10},{4,12},{6,14},{8,0},{10,2},{12,4},{14,6},{1,9},{3,11}... | collective-permute-start | bytes 294920 | tf_op jit(solution)/shard_map/ppermute | solution.py:21
  149.2 5.3 %collective-permute-start.37 = (bf16[64,1024]{1,0:T(8,128)(2,1)S(1)}, bf16[64,1024]{1,0:T(8,128)(2,1)S(1)}, u32[]{:S(2)}, u32[]{:S(2)}) collective-permute-start(bf16[64,1024]{1,0:T(8,128)(2,1)S(1)} %get-tuple-element.107.refs_2_.refs_0_), channel_id=1, source_target_pairs={{0,4},{2,6},{4,0},{6,2},{8,12},{10,14},{12,8},{14,10},{1,5},{3,7},... | collective-permute-start | bytes 393224 | tf_op jit(solution)/shard_map/ppermute | solution.py:21
  149.6 5.3 %collective-permute-start.36 = (bf16[64,768]{1,0:T(8,128)(2,1)S(1)}, bf16[64,768]{1,0:T(8,128)(2,1)S(1)}, u32[]{:S(2)}, u32[]{:S(2)}) collective-permute-start(bf16[64,768]{1,0:T(8,128)(2,1)S(1)} %get-tuple-element.109.refs_0_), channel_id=1, source_target_pairs={{0,2},{2,0},{4,6},{6,4},{8,10},{10,8},{12,14},{14,12},{1,3},{3,1},... | collective-permute-start | bytes 294920 | tf_op jit(solution)/shard_map/ppermute | solution.py:21
  150.4 6.7 %collective-permute-start.35 = (bf16[64,768]{1,0:T(8,128)(2,1)S(1)}, bf16[64,768]{1,0:T(8,128)(2,1)S(1)}, u32[]{:S(2)}, u32[]{:S(2)}) collective-permute-start(bf16[64,768]{1,0:T(8,128)(2,1)S(1)} %get-tuple-element.108.refs_2_.refs_0_), channel_id=1, source_target_pairs={{0,4},{2,6},{4,0},{6,2},{8,12},{10,14},{12,8},{14,10},{1,5},{3,7},... | collective-permute-start | bytes 294920 | tf_op jit(solution)/shard_map/ppermute | solution.py:21
  152.2 5.7 %collective-permute-start.39 = (bf16[64,768]{1,0:T(8,128)(2,1)S(1)}, bf16[64,768]{1,0:T(8,128)(2,1)S(1)}, u32[]{:S(2)}, u32[]{:S(2)}) collective-permute-start(bf16[64,768]{1,0:T(8,128)(2,1)S(1)} %get-tuple-element.110.refs_0_), channel_id=1, source_target_pairs={{0,2},{2,0},{4,6},{6,4},{8,10},{10,8},{12,14},{14,12},{1,3},{3,1},... | collective-permute-start | bytes 294920 | tf_op jit(solution)/shard_map/ppermute | solution.py:21
  154.6 9.1 %collective-permute-start.41 = (bf16[64,2048]{1,0:T(8,128)(2,1)S(1)}, bf16[64,2048]{1,0:T(8,128)(2,1)S(1)}, u32[]{:S(2)}, u32[]{:S(2)}) collective-permute-start(bf16[64,2048]{1,0:T(8,128)(2,1)S(1)} %join.12.refs_2_.refs_0_), channel_id=1, source_target_pairs={{0,2},{2,0},{4,6},{6,4},{8,10},{10,8},{12,14},{14,12},{1,3},{3,1},... | collective-permute-start | bytes 786440 | tf_op jit(solution)/shard_map/ppermute | solution.py:21
  154.9 8.7 %collective-permute-start.42 = (bf16[64,1536]{1,0:T(8,128)(2,1)S(1)}, bf16[64,1536]{1,0:T(8,128)(2,1)S(1)}, u32[]{:S(2)}, u32[]{:S(2)}) collective-permute-start(bf16[64,1536]{1,0:T(8,128)(2,1)S(1)} %join.13.refs_2_.refs_1_), channel_id=1, source_target_pairs={{0,4},{2,6},{4,0},{6,2},{8,12},{10,14},{12,8},{14,10},{1,5},{3,7},... | collective-permute-start | bytes 589832 | tf_op jit(solution)/shard_map/ppermute | solution.py:21
  157.9 7.8 %collective-permute-start.40 = (bf16[64,1536]{1,0:T(8,128)(2,1)S(1)}, bf16[64,1536]{1,0:T(8,128)(2,1)S(1)}, u32[]{:S(2)}, u32[]{:S(2)}) collective-permute-start(bf16[64,1536]{1,0:T(8,128)(2,1)S(1)} %join.15.refs_3_.refs_9_), channel_id=1, source_target_pairs={{0,4},{2,6},{4,0},{6,2},{8,12},{10,14},{12,8},{14,10},{1,5},{3,7},... | collective-permute-start | bytes 589832 | tf_op jit(solution)/shard_map/ppermute | solution.py:21
  159.2 6.5 %collective-permute-start.38 = (bf16[64,1536]{1,0:T(8,128)(2,1)S(1)}, bf16[64,1536]{1,0:T(8,128)(2,1)S(1)}, u32[]{:S(2)}, u32[]{:S(2)}) collective-permute-start(bf16[64,1536]{1,0:T(8,128)(2,1)S(1)} %join.14.refs_2_), channel_id=1, source_target_pairs={{0,2},{2,0},{4,6},{6,4},{8,10},{10,8},{12,14},{14,12},{1,3},{3,1},... | collective-permute-start | bytes 589832 | tf_op jit(solution)/shard_map/ppermute | solution.py:21
  167.6 1.6 collective-permute-start.43

commit v6 on v5

--- a/solution.py
+++ b/solution.py
@@ -362,7 +362,7 @@
     total = down(order, None, a.hiddens(0) + b.hiddens(0), weights[2], a.ranges(0) + b.ranges(0), own_rows)
     total = down(order, total, a.hiddens(1), weights[2], a.ranges(1), ab_rows[:2])
     total = down(order, total, b.hiddens(1), weights[2], b.ranges(1), ab_rows[2:])
-    return total + lax.ppermute(total, "gy", [(0, 1), (1, 0)]), next_sends
+    return total, next_sends
 
 
 def pair_rows(own, gy):
@@ -375,12 +375,15 @@
     gy = lax.axis_index("gy")
     weights = [pltpu.with_memory_space_constraint(w, pltpu.HBM) for w in weights]
     rows = [pair_rows(t, gy) for t in tokens]
-    first_sum, fetched = fast_layer(rows[0], weights, ahead=True)
-    first_out = first_sum.astype(BF16)
+    total, fetched = fast_layer(rows[0], weights, ahead=True)
+    first_out = (total + lax.ppermute(total, "gy", [(0, 1), (1, 0)])).astype(BF16)
     second_input = (rows[1].astype(F32) + first_out.astype(F32)).astype(BF16)
-    second_sum, _ = fast_layer(second_input, weights, fetched)
-    outs = jnp.stack([first_out, second_sum.astype(BF16)])
-    return lax.dynamic_slice_in_dim(outs, gy * own_rows, own_rows, axis=1)
+    total, _ = fast_layer(second_input, weights, fetched)
+    first_out = jnp.where(gy == 0, first_out[:own_rows], first_out[own_rows:])
+    own = jnp.where(gy == 0, total[:own_rows], total[own_rows:])
+    other = jnp.where(gy == 0, total[own_rows:], total[:own_rows])
+    second_out = (own + lax.ppermute(other, "gy", [(0, 1), (1, 0)])).astype(BF16)
+    return jnp.stack([first_out, second_out])
 
 
 def plain_body(tokens, gate_weight, up_weight, down_weight):

time: 170 us -> 170 us (level)
  no operation moved by 1% of the time
where the time goes in v6:
time: 170 us
  Pallas kernels  85.5 us (50%)
  starting transfers between devices  54 us (32%)
  waiting for transfers between devices  27.4 us (16%)
    pallas_call x51, Pallas kernels, call(): pl.pallas_call(ordered, out_shape=out_shape, in_specs=in_specs + [ANY], o...  85.5 us
    ppermute x40, starting transfers between devices, swap(): return lax.ppermute(array, 'gx', [(i, i ^ 1 << bit) for i in range(8)])  52.9 us
    ppermute x40, waiting for transfers between devices, swap(): return lax.ppermute(array, 'gx', [(i, i ^ 1 << bit) for i in range(8)])  24.1 us
  transfers between devices with their start and end apart: 44, of which 15 were waited for; matrix products, arithmetic and copies ran while one was open for 0% of the time, Pallas kernels for 45%

profile of v6, /device:TPU:0, one launch (start us, length us, event | category | flops | bytes accessed | tf_op | source)
XLA Modules:
  0.0 169.7 jit_solution(11914177708294227429)
XLA Ops:
  0.0 1.5 slice_bitcast_fusion.1
  2.0 0.9 collective-permute-done
  2.9 3.9 %gate_up.12.refs_3_ = bf16[2,64,2048]{2,1,0:T(8,128)(2,1)S(1)} custom-call(bf16[64,1024]{1,0:T(8,128)(2,1)S(1)} %maximum_select_fusion.refs_0_.refs_3_, bf16[1024,13312]{1,0:T(8,128)(2,1)} %refs_0_.9, bf16[1024,13312]{1,0:T(8,128)(2,1)} %refs_1_.25, bf16[64,1024]{1,0:T(8,128)(2,1)S(1)} %maximum_select_fusion.refs_0_.refs_3_), custom_call_target="tpu_custom_call" | custom-call | tf_op jit(solution)/shard_map/gate_up/pallas_call | solution.py:40
  6.8 2.9 %collective-permute-start.2 = (bf16[2,64,2048]{2,1,0:T(8,128)(2,1)S(1)}, bf16[2,64,2048]{2,1,0:T(8,128)(2,1)S(1)}, u32[]{:S(2)}, u32[]{:S(2)}) collective-permute-start(bf16[2,64,2048]{2,1,0:T(8,128)(2,1)S(1)} %gate_up.12.refs_3_), channel_id=1, source_target_pairs={{0,2},{2,0},{4,6},{6,4},{8,10},{10,8},{12,14},{14,12},{1,3},{3,1},... | collective-permute-start | bytes 1572872 | tf_op jit(solution)/shard_map/ppermute | solution.py:21
  9.6 3.2 %gate_up.13.refs_3_ = bf16[2,64,1536]{2,1,0:T(8,128)(2,1)S(1)} custom-call(bf16[64,1024]{1,0:T(8,128)(2,1)S(1)} %maximum_select_fusion.refs_0_.refs_3_, bf16[1024,13312]{1,0:T(8,128)(2,1)} %refs_0_.9, bf16[1024,13312]{1,0:T(8,128)(2,1)} %refs_1_.25, bf16[2,64,2048]{2,1,0:T(8,128)(2,1)S(1)} %gate_up.12.refs_3_), custom_call_target="tpu_custom_call" | custom-call | tf_op jit(solution)/shard_map/gate_up/pallas_call | solution.py:40
  12.8 1.6 collective-permute-start.1
  14.5 3.2 %gate_up.14.refs_3_ = bf16[2,64,1536]{2,1,0:T(8,128)(2,1)S(1)} custom-call(bf16[64,1024]{1,0:T(8,128)(2,1)S(1)} %maximum_select_fusion.refs_0_.refs_3_, bf16[1024,13312]{1,0:T(8,128)(2,1)} %refs_0_.9, bf16[1024,13312]{1,0:T(8,128)(2,1)} %refs_1_.25, bf16[2,64,1536]{2,1,0:T(8,128)(2,1)S(1)} %gate_up.13.refs_3_), custom_call_target="tpu_custom_call" | custom-call | tf_op jit(solution)/shard_map/gate_up/pallas_call | solution.py:40
  17.7 0.6 collective-permute-start.3
  18.3 3.2 %gate_up.15.refs_3_ = bf16[2,64,1536]{2,1,0:T(8,128)(2,1)S(1)} custom-call(bf16[64,1024]{1,0:T(8,128)(2,1)S(1)} %maximum_select_fusion.refs_0_.refs_3_, bf16[1024,13312]{1,0:T(8,128)(2,1)} %refs_0_.9, bf16[1024,13312]{1,0:T(8,128)(2,1)} %refs_1_.25, bf16[2,64,1536]{2,1,0:T(8,128)(2,1)S(1)} %gate_up.14.refs_3_), custom_call_target="tpu_custom_call" | custom-call | tf_op jit(solution)/shard_map/gate_up/pallas_call | solution.py:40
  21.6 5.7 %gate_up.16 = (f32[2,64,2048]{2,1,0:T(8,128)S(1)}, f32[2,64,1536]{2,1,0:T(8,128)S(1)}) custom-call(bf16[64,1024]{1,0:T(8,128)(2,1)S(1)} %maximum_select_fusion.refs_0_.refs_3_, bf16[1024,13312]{1,0:T(8,128)(2,1)} %refs_0_.9, bf16[1024,13312]{1,0:T(8,128)(2,1)} %refs_1_.25, bf16[2,64,1536]{2,1,0:T(8,128)(2,1)S(1)} %gate_up.15.refs_3_), custom_call_target="tpu_custom_call" | custom-call | tf_op jit(solution)/shard_map/gate_up/pallas_call | solution.py:40
  27.5 2.0 %collective-permute-start.7 = (bf16[2,64,1024]{2,1,0:T(8,128)(2,1)S(1)}, bf16[2,64,1024]{2,1,0:T(8,128)(2,1)S(1)}, u32[]{:S(2)}, u32[]{:S(2)}) collective-permute-start(bf16[2,64,1024]{2,1,0:T(8,128)(2,1)S(1)} %get-tuple-element.71), channel_id=1, source_target_pairs={{0,4},{2,6},{4,0},{6,2},{8,12},{10,14},{12,8},{14,10},{1,5},{3,7},... | collective-permute-start | bytes 786440 | tf_op jit(solution)/shard_map/ppermute | solution.py:21
  29.6 1.6 collective-permute-start.8
  31.2 5.1 %gate_up.17 = (f32[2,64,1536]{2,1,0:T(8,128)S(1)}, f32[2,64,1536]{2,1,0:T(8,128)S(1)}) custom-call(bf16[64,1024]{1,0:T(8,128)(2,1)S(1)} %maximum_select_fusion.refs_0_.refs_3_, bf16[1024,13312]{1,0:T(8,128)(2,1)} %refs_0_.9, bf16[1024,13312]{1,0:T(8,128)(2,1)} %refs_1_.25, f32[2,64,768]{2,1,0:T(8,128)S(1)} %get-tuple-element.64.refs_3_.refs_1_), custom_call_target="tpu_custom_call" | custom-call | tf_op jit(solution)/shard_map/gate_up/pallas_call | solution.py:40
  36.6 0.6 collective-permute-start.6
  37.3 0.6 collective-permute-done.7.refs_2_
  38.0 2.6 %collective-permute-start.10 = (bf16[2,64,896]{2,1,0:T(8,128)(2,1)S(1)}, bf16[2,64,896]{2,1,0:T(8,128)(2,1)S(1)}, u32[]{:S(2)}, u32[]{:S(2)}) collective-permute-start(bf16[2,64,896]{2,1,0:T(8,128)(2,1)S(1)} %get-tuple-element.77), channel_id=1, source_target_pairs={{0,8},{2,10},{4,12},{6,14},{8,0},{10,2},{12,4},{14,6},{1,9},{3,11}... | collective-permute-start | bytes 688136 | tf_op jit(solution)/shard_map/ppermute | solution.py:21
  40.7 5.0 %fetch.5 = (bf16[4,512,1024]{2,1,0:T(8,128)(2,1)S(1)}, bf16[3,512,1024]{2,1,0:T(8,128)(2,1)S(1)}, bf16[3,512,1024]{2,1,0:T(8,128)(2,1)S(1)}, bf16[3,512,1024]{2,1,0:T(8,128)(2,1)S(1)}) custom-call(bf16[1024,13312]{1,0:T(8,128)(2,1)} %refs_0_.9, bf16[1024,13312]{1,0:T(8,128)(2,1)} %refs_1_.25, bf16[13312,1024]{1,0:T(8,128)(2,1)} %refs_3_.7, ...), custom_call_target="tpu_custom_call" | custom-call | tf_op jit(solution)/shard_map/fetch/pallas_call | solution.py:40
  45.8 1.5 collective-permute-start.9
  47.3 4.8 %fetch.6 = (bf16[3,2,1024,512]{3,2,1,0:T(8,128)(2,1)S(1)}, bf16[3,2,1024,512]{3,2,1,0:T(8,128)(2,1)S(1)}) custom-call(bf16[1024,13312]{1,0:T(8,128)(2,1)} %refs_0_.9, bf16[1024,13312]{1,0:T(8,128)(2,1)} %refs_1_.25, bf16[13312,1024]{1,0:T(8,128)(2,1)} %refs_3_.7, f32[2,64,768]{2,1,0:T(8,128)S(1)} %get-tuple-element.75.refs_3_.refs_0_), custom_call_target="tpu_custom_call" | custom-call | tf_op jit(solution)/shard_map/fetch/pallas_call | solution.py:40
  52.1 3.0 %collective-permute-done.10.refs_1_ = bf16[2,64,896]{2,1,0:T(8,128)(2,1)S(1)} collective-permute-done((bf16[2,64,896]{2,1,0:T(8,128)(2,1)S(1)}, bf16[2,64,896]{2,1,0:T(8,128)(2,1)S(1)}, u32[]{:S(2)}, u32[]{:S(2)}) %collective-permute-start.10) | collective-permute-done | bytes 229408 | tf_op jit(solution)/shard_map/ppermute | solution.py:21
  55.3 5.4 %fetch.7 = (bf16[4,2,1024,512]{3,2,1,0:T(8,128)(2,1)S(1)}, bf16[3,2,1024,512]{3,2,1,0:T(8,128)(2,1)S(1)}) custom-call(bf16[1024,13312]{1,0:T(8,128)(2,1)} %refs_0_.9, bf16[1024,13312]{1,0:T(8,128)(2,1)} %refs_1_.25, bf16[13312,1024]{1,0:T(8,128)(2,1)} %refs_3_.7, bf16[64,896]{1,0:T(8,128)(2,1)S(1)} %gated.4.refs_3_.refs_0_), custom_call_target="tpu_custom_call" | custom-call | tf_op jit(solution)/shard_map/fetch/pallas_call | solution.py:40
  60.9 3.0 %collective-permute-start.11 = (bf16[64,768]{1,0:T(8,128)(2,1)S(1)}, bf16[64,768]{1,0:T(8,128)(2,1)S(1)}, u32[]{:S(2)}, u32[]{:S(2)}) collective-permute-start(bf16[64,768]{1,0:T(8,128)(2,1)S(1)} %gated.5.refs_2_.refs_0_), channel_id=1, source_target_pairs={{0,8},{2,10},{4,12},{6,14},{8,0},{10,2},{12,4},{14,6},{1,9},{3,11}... | collective-permute-start | bytes 294920 | tf_op jit(solution)/shard_map/ppermute | solution.py:21
  63.9 4.8 %collective-permute-start.15 = (bf16[64,1024]{1,0:T(8,128)(2,1)S(1)}, bf16[64,1024]{1,0:T(8,128)(2,1)S(1)}, u32[]{:S(2)}, u32[]{:S(2)}) collective-permute-start(bf16[64,1024]{1,0:T(8,128)(2,1)S(1)} %get-tuple-element.80.refs_2_.refs_0_), channel_id=1, source_target_pairs={{0,4},{2,6},{4,0},{6,2},{8,12},{10,14},{12,8},{14,10},{1,5},{3,7},... | collective-permute-start | bytes 393224 | tf_op jit(solution)/shard_map/ppermute | solution.py:21
  68.7 5.7 %collective-permute-start.13 = (bf16[64,768]{1,0:T(8,128)(2,1)S(1)}, bf16[64,768]{1,0:T(8,128)(2,1)S(1)}, u32[]{:S(2)}, u32[]{:S(2)}) collective-permute-start(bf16[64,768]{1,0:T(8,128)(2,1)S(1)} %get-tuple-element.81.refs_2_.refs_0_), channel_id=1, source_target_pairs={{0,4},{2,6},{4,0},{6,2},{8,12},{10,14},{12,8},{14,10},{1,5},{3,7},... | collective-permute-start | bytes 294920 | tf_op jit(solution)/shard_map/ppermute | solution.py:21
  74.5 2.1 %collective-permute-start.19 = (bf16[64,2048]{1,0:T(8,128)(2,1)S(1)}, bf16[64,2048]{1,0:T(8,128)(2,1)S(1)}, u32[]{:S(2)}, u32[]{:S(2)}) collective-permute-start(bf16[64,2048]{1,0:T(8,128)(2,1)S(1)} %join.8.refs_2_.refs_0_), channel_id=1, source_target_pairs={{0,2},{2,0},{4,6},{6,4},{8,10},{10,8},{12,14},{14,12},{1,3},{3,1},... | collective-permute-start | bytes 786440 | tf_op jit(solution)/shard_map/ppermute | solution.py:21
  76.8 1.0 collective-permute-done.13.refs_1_
  77.7 1.3 collective-permute-done.17.refs_1_
  79.8 5.3 %down.6.refs_2_.refs_6_ = f32[64,1024]{1,0:T(8,128)S(1)} custom-call(bf16[64,2048]{1,0:T(8,128)(2,1)S(1)} %join.8.refs_2_.refs_0_, bf16[64,1536]{1,0:T(8,128)(2,1)S(1)} %join.9.refs_2_.refs_1_, bf16[64,1536]{1,0:T(8,128)(2,1)S(1)} %join.10.refs_2_, bf16[64,1536]{1,0:T(8,128)(2,1)S(1)} %join.11.refs_3_.refs_5_, bf16[13312,1024]{1,0:T(8,128)(2,1)} %refs_3_.7, ...), custom_call_target="tpu_custom_call" | custom-call | tf_op jit(solution)/shard_map/down/pallas_call | solution.py:40
  85.2 2.1 %down.7.refs_2_.refs_6_ = f32[64,1024]{1,0:T(8,128)S(1)} custom-call(bf16[64,2048]{1,0:T(8,128)(2,1)S(1)} %collective-permute-done.19.refs_0_, bf16[64,1536]{1,0:T(8,128)(2,1)S(1)} %collective-permute-done.20.refs_1_, f32[64,1024]{1,0:T(8,128)S(1)} %down.6.refs_2_.refs_6_, bf16[13312,1024]{1,0:T(8,128)(2,1)} %refs_3_.7, ...), custom_call_target="tpu_custom_call" | custom-call | tf_op jit(solution)/shard_map/down/pallas_call | solution.py:40
  87.4 1.8 %down.8 = f32[64,1024]{1,0:T(8,128)S(1)} custom-call(bf16[64,1536]{1,0:T(8,128)(2,1)S(1)} %collective-permute-done.16.refs_0_, bf16[64,1536]{1,0:T(8,128)(2,1)S(1)} %collective-permute-done.18.refs_1_, f32[64,1024]{1,0:T(8,128)S(1)} %down.7.refs_2_.refs_6_, bf16[13312,1024]{1,0:T(8,128)(2,1)} %refs_3_.7, ...), custom_call_target="tpu_custom_call" | custom-call | tf_op jit(solution)/shard_map/down/pallas_call | solution.py:40
  89.8 1.1 collective-permute-done.22
  91.0 1.9 %gate_up.18.refs_2_ = bf16[2,64,2048]{2,1,0:T(8,128)(2,1)S(1)} custom-call(bf16[64,1024]{1,0:T(8,128)(2,1)S(1)} %get-tuple-element.117.refs_0_.refs_2_, bf16[4,2,1024,512]{3,2,1,0:T(8,128)(2,1)S(1)} %get-tuple-element.79.refs_2_.refs_1_, bf16[64,1024]{1,0:T(8,128)(2,1)S(1)} %get-tuple-element.117.refs_0_.refs_2_), custom_call_target="tpu_custom_call" | custom-call | tf_op jit(solution)/shard_map/gate_up/pallas_call | solution.py:40
  92.9 1.8 %collective-permute-start.24 = (bf16[2,64,2048]{2,1,0:T(8,128)(2,1)S(1)}, bf16[2,64,2048]{2,1,0:T(8,128)(2,1)S(1)}, u32[]{:S(2)}, u32[]{:S(2)}) collective-permute-start(bf16[2,64,2048]{2,1,0:T(8,128)(2,1)S(1)} %gate_up.18.refs_2_), channel_id=1, source_target_pairs={{0,2},{2,0},{4,6},{6,4},{8,10},{10,8},{12,14},{14,12},{1,3},{3,1},... | collective-permute-start | bytes 1572872 | tf_op jit(solution)/shard_map/ppermute | solution.py:21
  94.7 1.4 gate_up.19.refs_2_
  96.1 1.7 %collective-permute-start.23 = (bf16[2,64,1536]{2,1,0:T(8,128)(2,1)S(1)}, bf16[2,64,1536]{2,1,0:T(8,128)(2,1)S(1)}, u32[]{:S(2)}, u32[]{:S(2)}) collective-permute-start(bf16[2,64,1536]{2,1,0:T(8,128)(2,1)S(1)} %gate_up.19.refs_2_), channel_id=1, source_target_pairs={{0,4},{2,6},{4,0},{6,2},{8,12},{10,14},{12,8},{14,10},{1,5},{3,7},... | collective-permute-start | bytes 1179656 | tf_op jit(solution)/shard_map/ppermute | solution.py:21
  97.8 1.4 gate_up.20.refs_2_
  99.5 1.4 gate_up.21.refs_3_
  101.5 5.7 %gate_up.22 = (f32[2,64,2048]{2,1,0:T(8,128)S(1)}, f32[2,64,1536]{2,1,0:T(8,128)S(1)}) custom-call(bf16[64,1024]{1,0:T(8,128)(2,1)S(1)} %get-tuple-element.117.refs_0_.refs_2_, bf16[1024,13312]{1,0:T(8,128)(2,1)} %refs_0_.9, bf16[1024,13312]{1,0:T(8,128)(2,1)} %refs_1_.25, bf16[2,64,1536]{2,1,0:T(8,128)(2,1)S(1)} %gate_up.21.refs_3_), custom_call_target="tpu_custom_call" | custom-call | tf_op jit(solution)/shard_map/gate_up/pallas_call | solution.py:40
  107.8 1.6 collective-permute-start.29
  109.5 1.9 %collective-permute-start.30 = (bf16[2,64,768]{2,1,0:T(8,128)(2,1)S(1)}, bf16[2,64,768]{2,1,0:T(8,128)(2,1)S(1)}, u32[]{:S(2)}, u32[]{:S(2)}) collective-permute-start(bf16[2,64,768]{2,1,0:T(8,128)(2,1)S(1)} %get-tuple-element.100), channel_id=1, source_target_pairs={{0,2},{2,0},{4,6},{6,4},{8,10},{10,8},{12,14},{14,12},{1,3},{3,1},... | collective-permute-start | bytes 589832 | tf_op jit(solution)/shard_map/ppermute | solution.py:21
  111.4 5.1 %gate_up.23 = (f32[2,64,1536]{2,1,0:T(8,128)S(1)}, f32[2,64,1536]{2,1,0:T(8,128)S(1)}) custom-call(bf16[64,1024]{1,0:T(8,128)(2,1)S(1)} %get-tuple-element.117.refs_0_.refs_2_, bf16[1024,13312]{1,0:T(8,128)(2,1)} %refs_0_.9, bf16[1024,13312]{1,0:T(8,128)(2,1)} %refs_1_.25, f32[2,64,768]{2,1,0:T(8,128)S(1)} %get-tuple-element.92.refs_3_.refs_1_), custom_call_target="tpu_custom_call" | custom-call | tf_op jit(solution)/shard_map/gate_up/pallas_call | solution.py:40
  116.7 1.4 collective-permute-start.28
  118.1 1.6 collective-permute-start.27
  119.8 0.6 collective-permute-done.30.refs_3_
  120.4 1.9 %collective-permute-done.29.refs_2_ = bf16[2,64,1024]{2,1,0:T(8,128)(2,1)S(1)} collective-permute-done((bf16[2,64,1024]{2,1,0:T(8,128)(2,1)S(1)}, bf16[2,64,1024]{2,1,0:T(8,128)(2,1)S(1)}, u32[]{:S(2)}, u32[]{:S(2)}) %collective-permute-start.29) | collective-permute-done | bytes 262176 | tf_op jit(solution)/shard_map/ppermute | solution.py:21
  122.3 0.7 collective-permute-start.32
  123.1 5.0 %fetch.8 = (bf16[4,512,1024]{2,1,0:T(8,128)(2,1)S(1)}, bf16[3,512,1024]{2,1,0:T(8,128)(2,1)S(1)}, bf16[3,512,1024]{2,1,0:T(8,128)(2,1)S(1)}, bf16[3,512,1024]{2,1,0:T(8,128)(2,1)S(1)}) custom-call(bf16[1024,13312]{1,0:T(8,128)(2,1)} %refs_0_.9, bf16[1024,13312]{1,0:T(8,128)(2,1)} %refs_1_.25, bf16[13312,1024]{1,0:T(8,128)(2,1)} %refs_3_.7, ...), custom_call_target="tpu_custom_call" | custom-call | tf_op jit(solution)/shard_map/fetch/pallas_call | solution.py:40
  128.2 2.3 %collective-permute-start.31 = (bf16[2,64,768]{2,1,0:T(8,128)(2,1)S(1)}, bf16[2,64,768]{2,1,0:T(8,128)(2,1)S(1)}, u32[]{:S(2)}, u32[]{:S(2)}) collective-permute-start(bf16[2,64,768]{2,1,0:T(8,128)(2,1)S(1)} %get-tuple-element.104), channel_id=1, source_target_pairs={{0,8},{2,10},{4,12},{6,14},{8,0},{10,2},{12,4},{14,6},{1,9},{3,11}... | collective-permute-start | bytes 589832 | tf_op jit(solution)/shard_map/ppermute | solution.py:21
  130.5 5.0 %fetch.9 = (bf16[4,512,1024]{2,1,0:T(8,128)(2,1)S(1)}, bf16[3,512,1024]{2,1,0:T(8,128)(2,1)S(1)}, bf16[3,512,1024]{2,1,0:T(8,128)(2,1)S(1)}, bf16[3,512,1024]{2,1,0:T(8,128)(2,1)S(1)}) custom-call(bf16[1024,13312]{1,0:T(8,128)(2,1)} %refs_0_.9, bf16[1024,13312]{1,0:T(8,128)(2,1)} %refs_1_.25, bf16[13312,1024]{1,0:T(8,128)(2,1)} %refs_3_.7, ...), custom_call_target="tpu_custom_call" | custom-call | tf_op jit(solution)/shard_map/fetch/pallas_call | solution.py:40
  135.5 5.5 %collective-permute-done.32.refs_1_ = bf16[2,64,896]{2,1,0:T(8,128)(2,1)S(1)} collective-permute-done((bf16[2,64,896]{2,1,0:T(8,128)(2,1)S(1)}, bf16[2,64,896]{2,1,0:T(8,128)(2,1)S(1)}, u32[]{:S(2)}, u32[]{:S(2)}) %collective-permute-start.32) | collective-permute-done | bytes 229408 | tf_op jit(solution)/shard_map/ppermute | solution.py:21
  141.2 3.4 %collective-permute-done.31.refs_1_ = bf16[2,64,768]{2,1,0:T(8,128)(2,1)S(1)} collective-permute-done((bf16[2,64,768]{2,1,0:T(8,128)(2,1)S(1)}, bf16[2,64,768]{2,1,0:T(8,128)(2,1)S(1)}, u32[]{:S(2)}, u32[]{:S(2)}) %collective-permute-start.31) | collective-permute-done | bytes 196640 | tf_op jit(solution)/shard_map/ppermute | solution.py:21
  144.7 4.5 %collective-permute-done.34.refs_1_ = bf16[64,896]{1,0:T(8,128)(2,1)S(1)} collective-permute-done((bf16[64,896]{1,0:T(8,128)(2,1)S(1)}, bf16[64,896]{1,0:T(8,128)(2,1)S(1)}, u32[]{:S(2)}, u32[]{:S(2)}) %collective-permute-start.34) | collective-permute-done | bytes 114720 | tf_op jit(solution)/shard_map/ppermute | solution.py:21
  149.6 0.8 collective-permute-start.36
  150.4 1.8 %collective-permute-start.35 = (bf16[64,768]{1,0:T(8,128)(2,1)S(1)}, bf16[64,768]{1,0:T(8,128)(2,1)S(1)}, u32[]{:S(2)}, u32[]{:S(2)}) collective-permute-start(bf16[64,768]{1,0:T(8,128)(2,1)S(1)} %get-tuple-element.108.refs_2_.refs_0_), channel_id=1, source_target_pairs={{0,4},{2,6},{4,0},{6,2},{8,12},{10,14},{12,8},{14,10},{1,5},{3,7},... | collective-permute-start | bytes 294920 | tf_op jit(solution)/shard_map/ppermute | solution.py:21
  152.2 1.3 collective-permute-start.39
  153.4 1.1 collective-permute-done.37.refs_1_
  154.9 2.2 %collective-permute-start.42 = (bf16[64,1536]{1,0:T(8,128)(2,1)S(1)}, bf16[64,1536]{1,0:T(8,128)(2,1)S(1)}, u32[]{:S(2)}, u32[]{:S(2)}) collective-permute-start(bf16[64,1536]{1,0:T(8,128)(2,1)S(1)} %join.13.refs_2_.refs_1_), channel_id=1, source_target_pairs={{0,4},{2,6},{4,0},{6,2},{8,12},{10,14},{12,8},{14,10},{1,5},{3,7},... | collective-permute-start | bytes 589832 | tf_op jit(solution)/shard_map/ppermute | solution.py:21
  157.2 0.8 collective-permute-done.39.refs_1_
  157.9 1.3 collective-permute-start.40
  159.7 3.9 %down.9.refs_2_.refs_6_ = f32[64,1024]{1,0:T(8,128)S(1)} custom-call(bf16[64,2048]{1,0:T(8,128)(2,1)S(1)} %join.12.refs_2_.refs_0_, bf16[64,1536]{1,0:T(8,128)(2,1)S(1)} %join.13.refs_2_.refs_1_, bf16[64,1536]{1,0:T(8,128)(2,1)S(1)} %join.14.refs_2_, bf16[64,1536]{1,0:T(8,128)(2,1)S(1)} %join.15.refs_3_.refs_9_, bf16[13312,1024]{1,0:T(8,128)(2,1)} %refs_3_.7, ...), custom_call_target="tpu_custom_call" | custom-call | tf_op jit(solution)/shard_map/down/pallas_call | solution.py:40
  163.6 2.1 %down.10.refs_2_.refs_6_ = f32[64,1024]{1,0:T(8,128)S(1)} custom-call(bf16[64,2048]{1,0:T(8,128)(2,1)S(1)} %collective-permute-done.41.refs_0_, bf16[64,1536]{1,0:T(8,128)(2,1)S(1)} %collective-permute-done.42.refs_1_, f32[64,1024]{1,0:T(8,128)S(1)} %down.9.refs_2_.refs_6_, bf16[13312,1024]{1,0:T(8,128)(2,1)} %refs_3_.7, ...), custom_call_target="tpu_custom_call" | custom-call | tf_op jit(solution)/shard_map/down/pallas_call | solution.py:40
  165.8 1.8 %down.11 = f32[64,1024]{1,0:T(8,128)S(1)} custom-call(bf16[64,1536]{1,0:T(8,128)(2,1)S(1)} %collective-permute-done.38.refs_0_, bf16[64,1536]{1,0:T(8,128)(2,1)S(1)} %collective-permute-done.40.refs_1_, f32[64,1024]{1,0:T(8,128)S(1)} %down.10.refs_2_.refs_6_, bf16[13312,1024]{1,0:T(8,128)(2,1)} %refs_3_.7, ...), custom_call_target="tpu_custom_call" | custom-call | tf_op jit(solution)/shard_map/down/pallas_call | solution.py:40
  167.7 1.3 collective-permute-done.43
  169.1 0.7 pad_maximum_fusion
  (84 shorter events, 6.8 us)
Async XLA Ops:
  1.5 1.4 collective-permute-start
  6.8 20.6 %collective-permute-start.2 = (bf16[2,64,2048]{2,1,0:T(8,128)(2,1)S(1)}, bf16[2,64,2048]{2,1,0:T(8,128)(2,1)S(1)}, u32[]{:S(2)}, u32[]{:S(2)}) collective-permute-start(bf16[2,64,2048]{2,1,0:T(8,128)(2,1)S(1)} %gate_up.12.refs_3_), channel_id=1, source_target_pairs={{0,2},{2,0},{4,6},{6,4},{8,10},{10,8},{12,14},{14,12},{1,3},{3,1},... | collective-permute-start | bytes 1572872 | tf_op jit(solution)/shard_map/ppermute | solution.py:21
  12.8 16.7 %collective-permute-start.1 = (bf16[2,64,1536]{2,1,0:T(8,128)(2,1)S(1)}, bf16[2,64,1536]{2,1,0:T(8,128)(2,1)S(1)}, u32[]{:S(2)}, u32[]{:S(2)}) collective-permute-start(bf16[2,64,1536]{2,1,0:T(8,128)(2,1)S(1)} %gate_up.13.refs_3_), channel_id=1, source_target_pairs={{0,4},{2,6},{4,0},{6,2},{8,12},{10,14},{12,8},{14,10},{1,5},{3,7},... | collective-permute-start | bytes 1179656 | tf_op jit(solution)/shard_map/ppermute | solution.py:21
  17.7 18.7 %collective-permute-start.3 = (bf16[2,64,1536]{2,1,0:T(8,128)(2,1)S(1)}, bf16[2,64,1536]{2,1,0:T(8,128)(2,1)S(1)}, u32[]{:S(2)}, u32[]{:S(2)}) collective-permute-start(bf16[2,64,1536]{2,1,0:T(8,128)(2,1)S(1)} %gate_up.14.refs_3_), channel_id=1, source_target_pairs={{0,2},{2,0},{4,6},{6,4},{8,10},{10,8},{12,14},{14,12},{1,3},{3,1},... | collective-permute-start | bytes 1179656 | tf_op jit(solution)/shard_map/ppermute | solution.py:21
  21.5 14.9 %collective-permute-start.4 = (bf16[2,64,1536]{2,1,0:T(8,128)(2,1)S(1)}, bf16[2,64,1536]{2,1,0:T(8,128)(2,1)S(1)}, u32[]{:S(2)}, u32[]{:S(2)}) collective-permute-start(bf16[2,64,1536]{2,1,0:T(8,128)(2,1)S(1)} %gate_up.15.refs_3_), channel_id=1, source_target_pairs={{0,4},{2,6},{4,0},{6,2},{8,12},{10,14},{12,8},{14,10},{1,5},{3,7},... | collective-permute-start | bytes 1179656 | tf_op jit(solution)/shard_map/ppermute | solution.py:21
  27.5 10.5 %collective-permute-start.7 = (bf16[2,64,1024]{2,1,0:T(8,128)(2,1)S(1)}, bf16[2,64,1024]{2,1,0:T(8,128)(2,1)S(1)}, u32[]{:S(2)}, u32[]{:S(2)}) collective-permute-start(bf16[2,64,1024]{2,1,0:T(8,128)(2,1)S(1)} %get-tuple-element.71), channel_id=1, source_target_pairs={{0,4},{2,6},{4,0},{6,2},{8,12},{10,14},{12,8},{14,10},{1,5},{3,7},... | collective-permute-start | bytes 786440 | tf_op jit(solution)/shard_map/ppermute | solution.py:21
  29.6 7.7 %collective-permute-start.8 = (bf16[2,64,768]{2,1,0:T(8,128)(2,1)S(1)}, bf16[2,64,768]{2,1,0:T(8,128)(2,1)S(1)}, u32[]{:S(2)}, u32[]{:S(2)}) collective-permute-start(bf16[2,64,768]{2,1,0:T(8,128)(2,1)S(1)} %get-tuple-element.72), channel_id=1, source_target_pairs={{0,2},{2,0},{4,6},{6,4},{8,10},{10,8},{12,14},{14,12},{1,3},{3,1},... | collective-permute-start | bytes 589832 | tf_op jit(solution)/shard_map/ppermute | solution.py:21
  36.6 9.1 %collective-permute-start.6 = (bf16[2,64,768]{2,1,0:T(8,128)(2,1)S(1)}, bf16[2,64,768]{2,1,0:T(8,128)(2,1)S(1)}, u32[]{:S(2)}, u32[]{:S(2)}) collective-permute-start(bf16[2,64,768]{2,1,0:T(8,128)(2,1)S(1)} %get-tuple-element.70), channel_id=1, source_target_pairs={{0,2},{2,0},{4,6},{6,4},{8,10},{10,8},{12,14},{14,12},{1,3},{3,1},... | collective-permute-start | bytes 589832 | tf_op jit(solution)/shard_map/ppermute | solution.py:21
  37.1 8.6 %collective-permute-start.5 = (bf16[2,64,768]{2,1,0:T(8,128)(2,1)S(1)}, bf16[2,64,768]{2,1,0:T(8,128)(2,1)S(1)}, u32[]{:S(2)}, u32[]{:S(2)}) collective-permute-start(bf16[2,64,768]{2,1,0:T(8,128)(2,1)S(1)} %get-tuple-element.69), channel_id=1, source_target_pairs={{0,4},{2,6},{4,0},{6,2},{8,12},{10,14},{12,8},{14,10},{1,5},{3,7},... | collective-permute-start | bytes 589832 | tf_op jit(solution)/shard_map/ppermute | solution.py:21
  38.0 17.1 %collective-permute-start.10 = (bf16[2,64,896]{2,1,0:T(8,128)(2,1)S(1)}, bf16[2,64,896]{2,1,0:T(8,128)(2,1)S(1)}, u32[]{:S(2)}, u32[]{:S(2)}) collective-permute-start(bf16[2,64,896]{2,1,0:T(8,128)(2,1)S(1)} %get-tuple-element.77), channel_id=1, source_target_pairs={{0,8},{2,10},{4,12},{6,14},{8,0},{10,2},{12,4},{14,6},{1,9},{3,11}... | collective-permute-start | bytes 688136 | tf_op jit(solution)/shard_map/ppermute | solution.py:21
  45.8 15.0 %collective-permute-start.9 = (bf16[2,64,768]{2,1,0:T(8,128)(2,1)S(1)}, bf16[2,64,768]{2,1,0:T(8,128)(2,1)S(1)}, u32[]{:S(2)}, u32[]{:S(2)}) collective-permute-start(bf16[2,64,768]{2,1,0:T(8,128)(2,1)S(1)} %get-tuple-element.76), channel_id=1, source_target_pairs={{0,8},{2,10},{4,12},{6,14},{8,0},{10,2},{12,4},{14,6},{1,9},{3,11}... | collective-permute-start | bytes 589832 | tf_op jit(solution)/shard_map/ppermute | solution.py:21
  55.2 8.6 %collective-permute-start.12 = (bf16[64,896]{1,0:T(8,128)(2,1)S(1)}, bf16[64,896]{1,0:T(8,128)(2,1)S(1)}, u32[]{:S(2)}, u32[]{:S(2)}) collective-permute-start(bf16[64,896]{1,0:T(8,128)(2,1)S(1)} %gated.4.refs_3_.refs_0_), channel_id=1, source_target_pairs={{0,8},{2,10},{4,12},{6,14},{8,0},{10,2},{12,4},{14,6},{1,9},{3,11}... | collective-permute-start | bytes 344072 | tf_op jit(solution)/shard_map/ppermute | solution.py:21
  60.9 7.8 %collective-permute-start.11 = (bf16[64,768]{1,0:T(8,128)(2,1)S(1)}, bf16[64,768]{1,0:T(8,128)(2,1)S(1)}, u32[]{:S(2)}, u32[]{:S(2)}) collective-permute-start(bf16[64,768]{1,0:T(8,128)(2,1)S(1)} %gated.5.refs_2_.refs_0_), channel_id=1, source_target_pairs={{0,8},{2,10},{4,12},{6,14},{8,0},{10,2},{12,4},{14,6},{1,9},{3,11}... | collective-permute-start | bytes 294920 | tf_op jit(solution)/shard_map/ppermute | solution.py:21
  63.9 10.6 %collective-permute-start.15 = (bf16[64,1024]{1,0:T(8,128)(2,1)S(1)}, bf16[64,1024]{1,0:T(8,128)(2,1)S(1)}, u32[]{:S(2)}, u32[]{:S(2)}) collective-permute-start(bf16[64,1024]{1,0:T(8,128)(2,1)S(1)} %get-tuple-element.80.refs_2_.refs_0_), channel_id=1, source_target_pairs={{0,4},{2,6},{4,0},{6,2},{8,12},{10,14},{12,8},{14,10},{1,5},{3,7},... | collective-permute-start | bytes 393224 | tf_op jit(solution)/shard_map/ppermute | solution.py:21
  68.7 7.9 %collective-permute-start.14 = (bf16[64,768]{1,0:T(8,128)(2,1)S(1)}, bf16[64,768]{1,0:T(8,128)(2,1)S(1)}, u32[]{:S(2)}, u32[]{:S(2)}) collective-permute-start(bf16[64,768]{1,0:T(8,128)(2,1)S(1)} %get-tuple-element.82.refs_0_), channel_id=1, source_target_pairs={{0,2},{2,0},{4,6},{6,4},{8,10},{10,8},{12,14},{14,12},{1,3},{3,1},... | collective-permute-start | bytes 294920 | tf_op jit(solution)/shard_map/ppermute | solution.py:21
  68.7 9.0 %collective-permute-start.13 = (bf16[64,768]{1,0:T(8,128)(2,1)S(1)}, bf16[64,768]{1,0:T(8,128)(2,1)S(1)}, u32[]{:S(2)}, u32[]{:S(2)}) collective-permute-start(bf16[64,768]{1,0:T(8,128)(2,1)S(1)} %get-tuple-element.81.refs_2_.refs_0_), channel_id=1, source_target_pairs={{0,4},{2,6},{4,0},{6,2},{8,12},{10,14},{12,8},{14,10},{1,5},{3,7},... | collective-permute-start | bytes 294920 | tf_op jit(solution)/shard_map/ppermute | solution.py:21
  74.5 4.6 %collective-permute-start.17 = (bf16[64,768]{1,0:T(8,128)(2,1)S(1)}, bf16[64,768]{1,0:T(8,128)(2,1)S(1)}, u32[]{:S(2)}, u32[]{:S(2)}) collective-permute-start(bf16[64,768]{1,0:T(8,128)(2,1)S(1)} %get-tuple-element.83.refs_0_), channel_id=1, source_target_pairs={{0,2},{2,0},{4,6},{6,4},{8,10},{10,8},{12,14},{14,12},{1,3},{3,1},... | collective-permute-start | bytes 294920 | tf_op jit(solution)/shard_map/ppermute | solution.py:21
  74.5 10.7 %collective-permute-start.19 = (bf16[64,2048]{1,0:T(8,128)(2,1)S(1)}, bf16[64,2048]{1,0:T(8,128)(2,1)S(1)}, u32[]{:S(2)}, u32[]{:S(2)}) collective-permute-start(bf16[64,2048]{1,0:T(8,128)(2,1)S(1)} %join.8.refs_2_.refs_0_), channel_id=1, source_target_pairs={{0,2},{2,0},{4,6},{6,4},{8,10},{10,8},{12,14},{14,12},{1,3},{3,1},... | collective-permute-start | bytes 786440 | tf_op jit(solution)/shard_map/ppermute | solution.py:21
  76.6 8.6 %collective-permute-start.20 = (bf16[64,1536]{1,0:T(8,128)(2,1)S(1)}, bf16[64,1536]{1,0:T(8,128)(2,1)S(1)}, u32[]{:S(2)}, u32[]{:S(2)}) collective-permute-start(bf16[64,1536]{1,0:T(8,128)(2,1)S(1)} %join.9.refs_2_.refs_1_), channel_id=1, source_target_pairs={{0,4},{2,6},{4,0},{6,2},{8,12},{10,14},{12,8},{14,10},{1,5},{3,7},... | collective-permute-start | bytes 589832 | tf_op jit(solution)/shard_map/ppermute | solution.py:21
  79.1 8.2 %collective-permute-start.18 = (bf16[64,1536]{1,0:T(8,128)(2,1)S(1)}, bf16[64,1536]{1,0:T(8,128)(2,1)S(1)}, u32[]{:S(2)}, u32[]{:S(2)}) collective-permute-start(bf16[64,1536]{1,0:T(8,128)(2,1)S(1)} %join.11.refs_3_.refs_5_), channel_id=1, source_target_pairs={{0,4},{2,6},{4,0},{6,2},{8,12},{10,14},{12,8},{14,10},{1,5},{3,7},... | collective-permute-start | bytes 589832 | tf_op jit(solution)/shard_map/ppermute | solution.py:21
  79.6 7.8 %collective-permute-start.16 = (bf16[64,1536]{1,0:T(8,128)(2,1)S(1)}, bf16[64,1536]{1,0:T(8,128)(2,1)S(1)}, u32[]{:S(2)}, u32[]{:S(2)}) collective-permute-start(bf16[64,1536]{1,0:T(8,128)(2,1)S(1)} %join.10.refs_2_), channel_id=1, source_target_pairs={{0,2},{2,0},{4,6},{6,4},{8,10},{10,8},{12,14},{14,12},{1,3},{3,1},... | collective-permute-start | bytes 589832 | tf_op jit(solution)/shard_map/ppermute | solution.py:21
  87.4 1.9 %copy-start = (bf16[32,1024]{1,0:T(8,128)(2,1)S(1)}, bf16[32,1024]{1,0:T(8,128)(2,1)}, u32[]{:S(2)}) copy-start(bf16[32,1024]{1,0:T(8,128)(2,1)} %get-tuple-element.120) | copy-start | bytes 196612
  89.2 1.7 %collective-permute-start.21 = (f32[64,1024]{1,0:T(8,128)S(1)}, f32[64,1024]{1,0:T(8,128)S(1)}, u32[]{:S(2)}, u32[]{:S(2)}) collective-permute-start(f32[64,1024]{1,0:T(8,128)S(1)} %down.8), channel_id=1, source_target_pairs={{0,1},{1,0},{2,3},{3,2},{4,5},{5,4},{6,7},{7,6},{8,9},{9,8},{10,11... | collective-permute-start | bytes 786440 | tf_op jit(solution)/shard_map/ppermute | solution.py:379
  89.3 1.6 collective-permute-start.22
  92.9 14.8 %collective-permute-start.24 = (bf16[2,64,2048]{2,1,0:T(8,128)(2,1)S(1)}, bf16[2,64,2048]{2,1,0:T(8,128)(2,1)S(1)}, u32[]{:S(2)}, u32[]{:S(2)}) collective-permute-start(bf16[2,64,2048]{2,1,0:T(8,128)(2,1)S(1)} %gate_up.18.refs_2_), channel_id=1, source_target_pairs={{0,2},{2,0},{4,6},{6,4},{8,10},{10,8},{12,14},{14,12},{1,3},{3,1},... | collective-permute-start | bytes 1572872 | tf_op jit(solution)/shard_map/ppermute | solution.py:21
  96.1 13.3 %collective-permute-start.23 = (bf16[2,64,1536]{2,1,0:T(8,128)(2,1)S(1)}, bf16[2,64,1536]{2,1,0:T(8,128)(2,1)S(1)}, u32[]{:S(2)}, u32[]{:S(2)}) collective-permute-start(bf16[2,64,1536]{2,1,0:T(8,128)(2,1)S(1)} %gate_up.19.refs_2_), channel_id=1, source_target_pairs={{0,4},{2,6},{4,0},{6,2},{8,12},{10,14},{12,8},{14,10},{1,5},{3,7},... | collective-permute-start | bytes 1179656 | tf_op jit(solution)/shard_map/ppermute | solution.py:21
  99.3 17.3 %collective-permute-start.25 = (bf16[2,64,1536]{2,1,0:T(8,128)(2,1)S(1)}, bf16[2,64,1536]{2,1,0:T(8,128)(2,1)S(1)}, u32[]{:S(2)}, u32[]{:S(2)}) collective-permute-start(bf16[2,64,1536]{2,1,0:T(8,128)(2,1)S(1)} %gate_up.20.refs_2_), channel_id=1, source_target_pairs={{0,2},{2,0},{4,6},{6,4},{8,10},{10,8},{12,14},{14,12},{1,3},{3,1},... | collective-permute-start | bytes 1179656 | tf_op jit(solution)/shard_map/ppermute | solution.py:21
  101.0 15.7 %collective-permute-start.26 = (bf16[2,64,1536]{2,1,0:T(8,128)(2,1)S(1)}, bf16[2,64,1536]{2,1,0:T(8,128)(2,1)S(1)}, u32[]{:S(2)}, u32[]{:S(2)}) collective-permute-start(bf16[2,64,1536]{2,1,0:T(8,128)(2,1)S(1)} %gate_up.21.refs_3_), channel_id=1, source_target_pairs={{0,4},{2,6},{4,0},{6,2},{8,12},{10,14},{12,8},{14,10},{1,5},{3,7},... | collective-permute-start | bytes 1179656 | tf_op jit(solution)/shard_map/ppermute | solution.py:21
  107.8 14.4 %collective-permute-start.29 = (bf16[2,64,1024]{2,1,0:T(8,128)(2,1)S(1)}, bf16[2,64,1024]{2,1,0:T(8,128)(2,1)S(1)}, u32[]{:S(2)}, u32[]{:S(2)}) collective-permute-start(bf16[2,64,1024]{2,1,0:T(8,128)(2,1)S(1)} %get-tuple-element.99), channel_id=1, source_target_pairs={{0,4},{2,6},{4,0},{6,2},{8,12},{10,14},{12,8},{14,10},{1,5},{3,7},... | collective-permute-start | bytes 786440 | tf_op jit(solution)/shard_map/ppermute | solution.py:21
  109.5 10.9 %collective-permute-start.30 = (bf16[2,64,768]{2,1,0:T(8,128)(2,1)S(1)}, bf16[2,64,768]{2,1,0:T(8,128)(2,1)S(1)}, u32[]{:S(2)}, u32[]{:S(2)}) collective-permute-start(bf16[2,64,768]{2,1,0:T(8,128)(2,1)S(1)} %get-tuple-element.100), channel_id=1, source_target_pairs={{0,2},{2,0},{4,6},{6,4},{8,10},{10,8},{12,14},{14,12},{1,3},{3,1},... | collective-permute-start | bytes 589832 | tf_op jit(solution)/shard_map/ppermute | solution.py:21
  116.7 11.4 %collective-permute-start.28 = (bf16[2,64,768]{2,1,0:T(8,128)(2,1)S(1)}, bf16[2,64,768]{2,1,0:T(8,128)(2,1)S(1)}, u32[]{:S(2)}, u32[]{:S(2)}) collective-permute-start(bf16[2,64,768]{2,1,0:T(8,128)(2,1)S(1)} %get-tuple-element.98), channel_id=1, source_target_pairs={{0,2},{2,0},{4,6},{6,4},{8,10},{10,8},{12,14},{14,12},{1,3},{3,1},... | collective-permute-start | bytes 589832 | tf_op jit(solution)/shard_map/ppermute | solution.py:21
  118.1 10.0 %collective-permute-start.27 = (bf16[2,64,768]{2,1,0:T(8,128)(2,1)S(1)}, bf16[2,64,768]{2,1,0:T(8,128)(2,1)S(1)}, u32[]{:S(2)}, u32[]{:S(2)}) collective-permute-start(bf16[2,64,768]{2,1,0:T(8,128)(2,1)S(1)} %get-tuple-element.97), channel_id=1, source_target_pairs={{0,4},{2,6},{4,0},{6,2},{8,12},{10,14},{12,8},{14,10},{1,5},{3,7},... | collective-permute-start | bytes 589832 | tf_op jit(solution)/shard_map/ppermute | solution.py:21
  122.3 18.7 %collective-permute-start.32 = (bf16[2,64,896]{2,1,0:T(8,128)(2,1)S(1)}, bf16[2,64,896]{2,1,0:T(8,128)(2,1)S(1)}, u32[]{:S(2)}, u32[]{:S(2)}) collective-permute-start(bf16[2,64,896]{2,1,0:T(8,128)(2,1)S(1)} %get-tuple-element.105), channel_id=1, source_target_pairs={{0,8},{2,10},{4,12},{6,14},{8,0},{10,2},{12,4},{14,6},{1,9},{3,11}... | collective-permute-start | bytes 688136 | tf_op jit(solution)/shard_map/ppermute | solution.py:21
  128.2 16.3 %collective-permute-start.31 = (bf16[2,64,768]{2,1,0:T(8,128)(2,1)S(1)}, bf16[2,64,768]{2,1,0:T(8,128)(2,1)S(1)}, u32[]{:S(2)}, u32[]{:S(2)}) collective-permute-start(bf16[2,64,768]{2,1,0:T(8,128)(2,1)S(1)} %get-tuple-element.104), channel_id=1, source_target_pairs={{0,8},{2,10},{4,12},{6,14},{8,0},{10,2},{12,4},{14,6},{1,9},{3,11}... | collective-permute-start | bytes 589832 | tf_op jit(solution)/shard_map/ppermute | solution.py:21
  141.1 8.1 %collective-permute-start.34 = (bf16[64,896]{1,0:T(8,128)(2,1)S(1)}, bf16[64,896]{1,0:T(8,128)(2,1)S(1)}, u32[]{:S(2)}, u32[]{:S(2)}) collective-permute-start(bf16[64,896]{1,0:T(8,128)(2,1)S(1)} %gated.6.refs_2_.refs_0_), channel_id=1, source_target_pairs={{0,8},{2,10},{4,12},{6,14},{8,0},{10,2},{12,4},{14,6},{1,9},{3,11}... | collective-permute-start | bytes 344072 | tf_op jit(solution)/shard_map/ppermute | solution.py:21
  144.6 5.7 %collective-permute-start.33 = (bf16[64,768]{1,0:T(8,128)(2,1)S(1)}, bf16[64,768]{1,0:T(8,128)(2,1)S(1)}, u32[]{:S(2)}, u32[]{:S(2)}) collective-permute-start(bf16[64,768]{1,0:T(8,128)(2,1)S(1)} %gated.7.refs_2_.refs_0_), channel_id=1, source_target_pairs={{0,8},{2,10},{4,12},{6,14},{8,0},{10,2},{12,4},{14,6},{1,9},{3,11}... | collective-permute-start | bytes 294920 | tf_op jit(solution)/shard_map/ppermute | solution.py:21
  149.2 5.3 %collective-permute-start.37 = (bf16[64,1024]{1,0:T(8,128)(2,1)S(1)}, bf16[64,1024]{1,0:T(8,128)(2,1)S(1)}, u32[]{:S(2)}, u32[]{:S(2)}) collective-permute-start(bf16[64,1024]{1,0:T(8,128)(2,1)S(1)} %get-tuple-element.107.refs_2_.refs_0_), channel_id=1, source_target_pairs={{0,4},{2,6},{4,0},{6,2},{8,12},{10,14},{12,8},{14,10},{1,5},{3,7},... | collective-permute-start | bytes 393224 | tf_op jit(solution)/shard_map/ppermute | solution.py:21
  149.6 5.3 %collective-permute-start.36 = (bf16[64,768]{1,0:T(8,128)(2,1)S(1)}, bf16[64,768]{1,0:T(8,128)(2,1)S(1)}, u32[]{:S(2)}, u32[]{:S(2)}) collective-permute-start(bf16[64,768]{1,0:T(8,128)(2,1)S(1)} %get-tuple-element.109.refs_0_), channel_id=1, source_target_pairs={{0,2},{2,0},{4,6},{6,4},{8,10},{10,8},{12,14},{14,12},{1,3},{3,1},... | collective-permute-start | bytes 294920 | tf_op jit(solution)/shard_map/ppermute | solution.py:21
  150.4 6.7 %collective-permute-start.35 = (bf16[64,768]{1,0:T(8,128)(2,1)S(1)}, bf16[64,768]{1,0:T(8,128)(2,1)S(1)}, u32[]{:S(2)}, u32[]{:S(2)}) collective-permute-start(bf16[64,768]{1,0:T(8,128)(2,1)S(1)} %get-tuple-element.108.refs_2_.refs_0_), channel_id=1, source_target_pairs={{0,4},{2,6},{4,0},{6,2},{8,12},{10,14},{12,8},{14,10},{1,5},{3,7},... | collective-permute-start | bytes 294920 | tf_op jit(solution)/shard_map/ppermute | solution.py:21
  152.2 5.7 %collective-permute-start.39 = (bf16[64,768]{1,0:T(8,128)(2,1)S(1)}, bf16[64,768]{1,0:T(8,128)(2,1)S(1)}, u32[]{:S(2)}, u32[]{:S(2)}) collective-permute-start(bf16[64,768]{1,0:T(8,128)(2,1)S(1)} %get-tuple-element.110.refs_0_), channel_id=1, source_target_pairs={{0,2},{2,0},{4,6},{6,4},{8,10},{10,8},{12,14},{14,12},{1,3},{3,1},... | collective-permute-start | bytes 294920 | tf_op jit(solution)/shard_map/ppermute | solution.py:21
  154.5 9.1 %collective-permute-start.41 = (bf16[64,2048]{1,0:T(8,128)(2,1)S(1)}, bf16[64,2048]{1,0:T(8,128)(2,1)S(1)}, u32[]{:S(2)}, u32[]{:S(2)}) collective-permute-start(bf16[64,2048]{1,0:T(8,128)(2,1)S(1)} %join.12.refs_2_.refs_0_), channel_id=1, source_target_pairs={{0,2},{2,0},{4,6},{6,4},{8,10},{10,8},{12,14},{14,12},{1,3},{3,1},... | collective-permute-start | bytes 786440 | tf_op jit(solution)/shard_map/ppermute | solution.py:21
  154.9 8.7 %collective-permute-start.42 = (bf16[64,1536]{1,0:T(8,128)(2,1)S(1)}, bf16[64,1536]{1,0:T(8,128)(2,1)S(1)}, u32[]{:S(2)}, u32[]{:S(2)}) collective-permute-start(bf16[64,1536]{1,0:T(8,128)(2,1)S(1)} %join.13.refs_2_.refs_1_), channel_id=1, source_target_pairs={{0,4},{2,6},{4,0},{6,2},{8,12},{10,14},{12,8},{14,10},{1,5},{3,7},... | collective-permute-start | bytes 589832 | tf_op jit(solution)/shard_map/ppermute | solution.py:21
  157.9 7.8 %collective-permute-start.40 = (bf16[64,1536]{1,0:T(8,128)(2,1)S(1)}, bf16[64,1536]{1,0:T(8,128)(2,1)S(1)}, u32[]{:S(2)}, u32[]{:S(2)}) collective-permute-start(bf16[64,1536]{1,0:T(8,128)(2,1)S(1)} %join.15.refs_3_.refs_9_), channel_id=1, source_target_pairs={{0,4},{2,6},{4,0},{6,2},{8,12},{10,14},{12,8},{14,10},{1,5},{3,7},... | collective-permute-start | bytes 589832 | tf_op jit(solution)/shard_map/ppermute | solution.py:21
  159.2 6.5 %collective-permute-start.38 = (bf16[64,1536]{1,0:T(8,128)(2,1)S(1)}, bf16[64,1536]{1,0:T(8,128)(2,1)S(1)}, u32[]{:S(2)}, u32[]{:S(2)}) collective-permute-start(bf16[64,1536]{1,0:T(8,128)(2,1)S(1)} %join.14.refs_2_), channel_id=1, source_target_pairs={{0,2},{2,0},{4,6},{6,4},{8,10},{10,8},{12,14},{14,12},{1,3},{3,1},... | collective-permute-start | bytes 589832 | tf_op jit(solution)/shard_map/ppermute | solution.py:21
  167.6 1.4 collective-permute-start.43
